TPU v7x, 32 devices: a whole 2x2x4 slice. The times are simulated.
32 devices in a mesh: dp: 4 (over x, core), expert: 8 (over z, y).
Axes of the slice: x: 2, y: 2, z: 4, core: 2. Of those that a mesh axis runs over, the one named last changes fastest.
Arguments:
- block_input: bfloat16 [16384, 768], P(('dp', 'expert')), may hold values from -6 to 6
- cotangent: bfloat16 [16384, 768], P(('dp', 'expert')), may hold values from -6 to 6
- attn_in: bfloat16 [768, 2304], P(None, ('dp', 'expert')), may hold values from -0.21875 to 0.21875
- attn_out: bfloat16 [768, 768], P(None, ('dp', 'expert')), may hold values from -0.875 to 0.875
- router: bfloat16 [768, 16], P(('dp', 'expert')), may hold values from -0.21875 to 0.21875
- ln1_gain: bfloat16 [768], P(('dp', 'expert')), may hold values from 0.099609375 to 1.8984375
- ln1_bias: bfloat16 [768], P(('dp', 'expert')), may hold values from -3 to 3
- ln2_gain: bfloat16 [768], P(('dp', 'expert')), may hold values from 0.099609375 to 1.8984375
- ln2_bias: bfloat16 [768], P(('dp', 'expert')), may hold values from -3 to 3
- new_w1: bfloat16 [8, 768, 3072], P('expert', 'dp'), may hold values from -0.21875 to 0.21875
- new_w2: bfloat16 [8, 3072, 768], P('expert', 'dp'), may hold values from -1.75 to 1.75
- old_w1: bfloat16 [8, 768, 3072], P('expert', 'dp'), may hold values from -0.21875 to 0.21875
- old_w2: bfloat16 [8, 3072, 768], P('expert', 'dp'), may hold values from -1.75 to 1.75
- expert_ids: int32 [16384, 2], P(('dp', 'expert')), may hold values from 0 to 15, as said below
- slots: int32 [16384, 2], P(('dp', 'expert')), may hold values from 0 to 111, as said below
- drops: int32 [16384, 2], P(('dp', 'expert')), may hold values from 0 to 1, as said below
Outputs:
- mixed: bfloat16 [16384, 768], P(('dp', 'expert'))
- input_grad: float32 [16384, 768], P(('dp', 'expert'))
- attn_in_grad: float32 [768, 2304], P(None, ('dp', 'expert'))
- attn_out_grad: float32 [768, 768], P(None, ('dp', 'expert'))
- router_grad: float32 [768, 16], P(('dp', 'expert'))
- ln1_gain_grad: float32 [768], P(('dp', 'expert'))
- ln1_bias_grad: float32 [768], P(('dp', 'expert'))
- ln2_gain_grad: float32 [768], P(('dp', 'expert'))
- ln2_bias_grad: float32 [768], P(('dp', 'expert'))
- new_w1_grad: float32 [8, 768, 3072], P('expert', 'dp')
- new_w2_grad: float32 [8, 3072, 768], P('expert', 'dp')
Inputs may be any that keep to these rules, and one draw needn't show every extreme that they name: `expert_ids`: each row names two different experts. Within the 512 rows of one device, the choices of one expert are counted in order of rows, first choice before second; a choice's slot is its count, and it is dropped when its count reaches 112, in which case its slot is 0. Every device fills all 112 slots of some expert, and one expert is full from every device. 1 exactly for the choices whose count reaches 112, as stated for slots; every device drops some.
All inputs are finite; a program needn't handle non-finite values.
Results may differ from a plain program's by a relative error of at most 0.015.
Values may be sent and summed in bfloat16 or wider, within the bound.
No kernel may reach another device: no remote copies, remote signals or barrier semaphores. Data moves between devices by JAX's collectives and lax.ppermute only.
A program may use at most 192 MiB of HBM per device.

v0:
```python
import jax
import jax.numpy as jnp
from jax import lax
from jax.sharding import PartitionSpec as P

HEADS = 12
HEAD_DIM = 64


def layer_norm(values, scale_gain, shift_bias):
    centre = values - jnp.mean(values, axis=-1, keepdims=True)
    spread = jnp.mean(centre * centre, axis=-1, keepdims=True)
    return centre * lax.rsqrt(spread + 1e-05) * scale_gain + shift_bias


def masked_softmax(scores):
    length = scores.shape[-1]
    rowpos = lax.broadcasted_iota(jnp.int32, (length, length), 0)
    colpos = lax.broadcasted_iota(jnp.int32, (length, length), 1)
    return jax.nn.softmax(jnp.where((rowpos >= colpos)[None], scores, -1e30), axis=-1)


def router_softmax(logit_rows):
    return jax.nn.softmax(logit_rows, axis=-1)


def expert_backward(block_rows, grad_rows, upward, downward):
    preact = jnp.dot(block_rows, upward, preferred_element_type=jnp.float32)
    hidden_f, gelu_back = jax.vjp(jax.nn.gelu, preact)
    grad_hidden = jnp.einsum("rd,fd->rf", grad_rows, downward, preferred_element_type=jnp.float32)
    grad_pre = gelu_back(grad_hidden)[0].astype(jnp.bfloat16)
    grad_input_rows = jnp.einsum(
        "rf,df->rd", grad_pre, upward, preferred_element_type=jnp.float32
    ).astype(jnp.bfloat16)
    return (hidden_f.astype(jnp.bfloat16), grad_pre, grad_input_rows)


def shards(
    block_input,
    cotangent,
    attn_in,
    attn_out,
    router,
    ln1_gain,
    ln1_bias,
    ln2_gain,
    ln2_bias,
    new_w1,
    new_w2,
    old_w1,
    old_w2,
    expert_ids,
    slots,
    drops,
):
    length, model_width = block_input.shape
    expert_peers = lax.axis_size("expert")
    experts = 2 * expert_peers
    capacity = max(length * 7 // (2 * experts), 2)
    score_scale = HEAD_DIM ** (-0.5)
    dense_params = (
        lax.all_gather(attn_in, ("dp", "expert"), axis=1, tiled=True),
        lax.all_gather(attn_out, ("dp", "expert"), axis=1, tiled=True),
        lax.all_gather(router, ("dp", "expert"), axis=0, tiled=True),
        lax.all_gather(ln1_gain, ("dp", "expert"), axis=0, tiled=True),
        lax.all_gather(ln1_bias, ("dp", "expert"), axis=0, tiled=True),
        lax.all_gather(ln2_gain, ("dp", "expert"), axis=0, tiled=True),
        lax.all_gather(ln2_bias, ("dp", "expert"), axis=0, tiled=True),
    )
    in_full, out_full, router_full, gain_one, bias_one, gain_two, bias_two = dense_params
    owned = (
        lax.all_gather(old_w1, "dp", axis=1, tiled=True),
        lax.all_gather(old_w2, "dp", axis=1, tiled=True),
        lax.all_gather(new_w1, "dp", axis=1, tiled=True),
        lax.all_gather(new_w2, "dp", axis=1, tiled=True),
    )
    old_up, old_down, new_up, new_down = (owned[0][0], owned[1][0], owned[2][0], owned[3][0])
    inputs = block_input.astype(jnp.float32)
    normed_one = layer_norm(
        inputs, gain_one.astype(jnp.float32), bias_one.astype(jnp.float32)
    ).astype(jnp.bfloat16)
    projected = jnp.dot(normed_one, in_full, preferred_element_type=jnp.float32).astype(
        jnp.bfloat16
    )
    pieces = projected.reshape(length, 3, HEADS, HEAD_DIM)
    queries, keys_all, values = (pieces[:, 0], pieces[:, 1], pieces[:, 2])
    scores = (
        jnp.einsum("qhd,khd->hqk", queries, keys_all, preferred_element_type=jnp.float32)
        * score_scale
    )
    weights_f = masked_softmax(scores)
    weights_b = weights_f.astype(jnp.bfloat16)
    context = (
        jnp.einsum("hqk,khd->qhd", weights_b, values, preferred_element_type=jnp.float32)
        .reshape(length, model_width)
        .astype(jnp.bfloat16)
    )
    middle = inputs + jnp.dot(context, out_full, preferred_element_type=jnp.float32)
    normed_two = layer_norm(
        middle, gain_two.astype(jnp.float32), bias_two.astype(jnp.float32)
    ).astype(jnp.bfloat16)
    logits = jnp.dot(normed_two, router_full, preferred_element_type=jnp.float32)
    route_probs, route_back = jax.vjp(router_softmax, logits)
    kept_mask = (1 - drops).astype(jnp.float32)
    choose = (expert_ids[:, :, None] == lax.broadcasted_iota(jnp.int32, (1, 1, experts), 2)).astype(
        jnp.float32
    )
    gate_values = jnp.sum(choose * route_probs[:, None, :], axis=-1) * kept_mask
    target = expert_ids * capacity + slots
    columns = lax.broadcasted_iota(jnp.int32, (1, experts * capacity), 1)
    pick_one = ((columns == target[:, 0:1]) & (drops[:, 0:1] == 0)).astype(jnp.bfloat16)
    pick_two = ((columns == target[:, 1:2]) & (drops[:, 1:2] == 0)).astype(jnp.bfloat16)
    placing = pick_one + pick_two
    outgoing = jnp.einsum(
        "tc,td->cd", placing, normed_two, preferred_element_type=jnp.float32
    ).astype(jnp.bfloat16)
    outgoing = outgoing.reshape(expert_peers, 2, capacity, model_width)
    again = (
        lax.all_gather(attn_in, ("dp", "expert"), axis=1, tiled=True),
        lax.all_gather(attn_out, ("dp", "expert"), axis=1, tiled=True),
        lax.all_gather(router, ("dp", "expert"), axis=0, tiled=True),
        lax.all_gather(ln1_gain, ("dp", "expert"), axis=0, tiled=True),
        lax.all_gather(ln1_bias, ("dp", "expert"), axis=0, tiled=True),
        lax.all_gather(ln2_gain, ("dp", "expert"), axis=0, tiled=True),
        lax.all_gather(ln2_bias, ("dp", "expert"), axis=0, tiled=True),
    )
    in_back, out_back, router_back_w, gain_one_b, bias_one_b, gain_two_b, bias_two_b = again
    fresh = (
        lax.all_gather(new_w1, "dp", axis=1, tiled=True),
        lax.all_gather(new_w2, "dp", axis=1, tiled=True),
    )
    new_up_b, new_down_b = (fresh[0][0], fresh[1][0])
    upstream = cotangent.astype(jnp.float32)
    scaled_one = (gate_values[:, 0:1] * upstream).astype(jnp.bfloat16)
    scaled_two = (gate_values[:, 1:2] * upstream).astype(jnp.bfloat16)
    grad_slots = jnp.einsum("tc,td->cd", pick_one, scaled_one, preferred_element_type=jnp.float32)
    grad_slots = grad_slots + jnp.einsum(
        "tc,td->cd", pick_two, scaled_two, preferred_element_type=jnp.float32
    )
    grad_slots = grad_slots.astype(jnp.bfloat16).reshape(expert_peers, 2, capacity, model_width)
    arrived = lax.all_to_all(outgoing, "expert", split_axis=0, concat_axis=0, tiled=True)
    slot_count = arrived.shape[2]
    results = []
    for member, weights_pair in enumerate(((old_up, old_down), (new_up, new_down))):
        block_rows = arrived[:, member].reshape(-1, model_width)
        preact = jnp.dot(block_rows, weights_pair[0], preferred_element_type=jnp.float32)
        hidden = jax.nn.gelu(preact).astype(jnp.bfloat16)
        produced_rows = jnp.dot(hidden, weights_pair[1], preferred_element_type=jnp.float32).astype(
            jnp.bfloat16
        )
        results.append(produced_rows.reshape(expert_peers, slot_count, model_width))
    produced = jnp.stack(results, axis=1)
    returned_rows = lax.all_to_all(produced, "expert", split_axis=0, concat_axis=0, tiled=True)
    returned, arrived = (returned_rows, arrived)
    grad_arrived = lax.all_to_all(grad_slots, "expert", split_axis=0, concat_axis=0, tiled=True)
    old_rows = arrived[:, 0].reshape(-1, model_width)
    old_grads = grad_arrived[:, 0].reshape(-1, model_width)
    unused_hidden, unused_pre, old_grad_in = expert_backward(old_rows, old_grads, old_up, old_down)
    new_rows = arrived[:, 1].reshape(-1, model_width)
    new_grads = grad_arrived[:, 1].reshape(-1, model_width)
    new_hidden, new_pre, new_grad_in = expert_backward(new_rows, new_grads, new_up_b, new_down_b)
    grad_stack = jnp.stack(
        [
            old_grad_in.reshape(expert_peers, capacity, model_width),
            new_grad_in.reshape(expert_peers, capacity, model_width),
        ],
        axis=1,
    )
    grad_sent = lax.all_to_all(
        grad_stack, "expert", split_axis=0, concat_axis=0, tiled=True
    ).reshape(experts * capacity, model_width)
    landed = returned.reshape(experts * capacity, model_width)
    slot_one = jnp.dot(pick_one, landed, preferred_element_type=jnp.float32)
    slot_two = jnp.dot(pick_two, landed, preferred_element_type=jnp.float32)
    mixed = (middle + gate_values[:, 0:1] * slot_one + gate_values[:, 1:2] * slot_two).astype(
        jnp.bfloat16
    )
    grad_gate = jnp.stack(
        [jnp.sum(upstream * slot_one, axis=-1), jnp.sum(upstream * slot_two, axis=-1)], axis=1
    )
    grad_down = jnp.einsum("rf,rd->fd", new_hidden, new_grads, preferred_element_type=jnp.float32)
    grad_up = jnp.einsum("rd,rf->df", new_rows, new_pre, preferred_element_type=jnp.float32)
    expert_sums = (
        lax.psum_scatter(
            grad_up[None].astype(jnp.bfloat16), "dp", scatter_dimension=1, tiled=True
        ).astype(jnp.float32),
        lax.psum_scatter(
            grad_down[None].astype(jnp.bfloat16), "dp", scatter_dimension=1, tiled=True
        ).astype(jnp.float32),
    )
    grad_probs = jnp.sum(choose * (grad_gate * kept_mask)[:, :, None], axis=1)
    grad_logits = route_back(grad_probs)[0].astype(jnp.bfloat16)
    router_grad_full = jnp.einsum(
        "td,te->de", normed_two, grad_logits, preferred_element_type=jnp.float32
    )
    grad_normed_two = jnp.dot(placing, grad_sent, preferred_element_type=jnp.float32)
    grad_normed_two = grad_normed_two + jnp.einsum(
        "te,de->td", grad_logits, router_back_w, preferred_element_type=jnp.float32
    )
    unused_two, norm_two_back = jax.vjp(
        layer_norm, middle, gain_two_b.astype(jnp.float32), bias_two_b.astype(jnp.float32)
    )
    grad_middle, grad_gain_two, grad_bias_two = norm_two_back(grad_normed_two)
    grad_middle = grad_middle + upstream
    grad_branch = grad_middle.astype(jnp.bfloat16)
    out_grad_full = jnp.einsum(
        "tc,td->cd", context, grad_branch, preferred_element_type=jnp.float32
    )
    grad_context = jnp.einsum(
        "td,cd->tc", grad_branch, out_back, preferred_element_type=jnp.float32
    ).astype(jnp.bfloat16)
    grad_context = grad_context.reshape(length, HEADS, HEAD_DIM)
    unused_soft, soft_back = jax.vjp(masked_softmax, scores)
    grad_weights = jnp.einsum(
        "qhd,khd->hqk", grad_context, values, preferred_element_type=jnp.float32
    )
    grad_scores = soft_back(grad_weights)[0].astype(jnp.bfloat16)
    grad_queries = (
        jnp.einsum("hqk,khd->qhd", grad_scores, keys_all, preferred_element_type=jnp.float32)
        * score_scale
    ).astype(jnp.bfloat16)
    grad_keys = (
        jnp.einsum("hqk,qhd->khd", grad_scores, queries, preferred_element_type=jnp.float32)
        * score_scale
    ).astype(jnp.bfloat16)
    grad_values = jnp.einsum(
        "hqk,qhd->khd", weights_b, grad_context, preferred_element_type=jnp.float32
    ).astype(jnp.bfloat16)
    grad_projected = jnp.stack([grad_queries, grad_keys, grad_values], axis=1).reshape(
        length, 3 * model_width
    )
    in_grad_full = jnp.einsum(
        "td,tc->dc", normed_one, grad_projected, preferred_element_type=jnp.float32
    )
    grad_normed_one = jnp.einsum(
        "tc,dc->td", grad_projected, in_back, preferred_element_type=jnp.float32
    )
    unused_one, norm_one_back = jax.vjp(
        layer_norm, inputs, gain_one_b.astype(jnp.float32), bias_one_b.astype(jnp.float32)
    )
    grad_first, grad_gain_one, grad_bias_one = norm_one_back(grad_normed_one)
    input_grad = grad_middle + grad_first
    dense_sums = (
        lax.psum_scatter(in_grad_full, ("dp", "expert"), scatter_dimension=1, tiled=True),
        lax.psum_scatter(out_grad_full, ("dp", "expert"), scatter_dimension=1, tiled=True),
        lax.psum_scatter(router_grad_full, ("dp", "expert"), scatter_dimension=0, tiled=True),
        lax.psum_scatter(grad_gain_one, ("dp", "expert"), scatter_dimension=0, tiled=True),
        lax.psum_scatter(grad_bias_one, ("dp", "expert"), scatter_dimension=0, tiled=True),
        lax.psum_scatter(grad_gain_two, ("dp", "expert"), scatter_dimension=0, tiled=True),
        lax.psum_scatter(grad_bias_two, ("dp", "expert"), scatter_dimension=0, tiled=True),
    )
    return (
        mixed,
        input_grad,
        dense_sums[0],
        dense_sums[1],
        dense_sums[2],
        dense_sums[3],
        dense_sums[4],
        dense_sums[5],
        dense_sums[6],
        expert_sums[0],
        expert_sums[1],
    )


def solution(mesh):
    in_specs = (
        P(("dp", "expert"), None),
        P(("dp", "expert"), None),
        P(None, ("dp", "expert")),
        P(None, ("dp", "expert")),
        P(("dp", "expert"), None),
        P(("dp", "expert")),
        P(("dp", "expert")),
        P(("dp", "expert")),
        P(("dp", "expert")),
        P("expert", "dp", None),
        P("expert", "dp", None),
        P("expert", "dp", None),
        P("expert", "dp", None),
        P(("dp", "expert"), None),
        P(("dp", "expert"), None),
        P(("dp", "expert"), None),
    )
    out_specs = (
        P(("dp", "expert"), None),
        P(("dp", "expert"), None),
        P(None, ("dp", "expert")),
        P(None, ("dp", "expert")),
        P(("dp", "expert"), None),
        P(("dp", "expert")),
        P(("dp", "expert")),
        P(("dp", "expert")),
        P(("dp", "expert")),
        P("expert", "dp", None),
        P("expert", "dp", None),
    )
    return jax.shard_map(shards, mesh=mesh, in_specs=in_specs, out_specs=out_specs, check_vma=False)
```

profile of v0, /device:TPU:0, one launch (start us, length us, event | category | flops | bytes accessed | tf_op | source)
XLA Modules:
  0.0 887.4 jit_solution(14921182852545530879)
XLA Ops:
  12.8 42.2 %all-reduce.10 = (bf16[768]{0:T(1024)(128)(2,1)S(1)}, bf16[768]{0:T(1024)(128)(2,1)S(1)}, bf16[768]{0:T(1024)(128)(2,1)S(1)}, bf16[768]{0:T(1024)(128)(2,1)S(1)}) all-reduce(bf16[768]{0:T(1024)(128)(2,1)S(1)} %dynamic-update-slice.1, bf16[768]{0:T(1024)(128)(2,1)S(1)} %dynamic-update-slice, ...), channel_id=1, replica_groups=mesh['dp'=4,'expert'=8] {'dp','expert'}, use_global_device_ids=true, to_apply=%add.1 | all-reduce | flops 3072 | bytes 12288
  55.7 18.3 %all-gather.8.cloned.1.call-done = bf16[768,2304]{0,1:T(8,128)(2,1)} async-done(((bf16[768,72]{0,1:T(8,128)(2,1)}), bf16[768,2304]{0,1:T(8,128)(2,1)}) %all-gather.8.cloned.1.call-update) | async-done | bytes 3538960 | tf_op jit(solution)/shard_map/all_gather | solution.py:62
  82.4 7.6 fusion.134
  102.2 27.7 %all-gather.10.cloned.1.call-done = bf16[768,768]{0,1:T(8,128)(2,1)} async-done(((bf16[768,24]{0,1:T(8,128)(2,1)}), bf16[768,768]{0,1:T(8,128)(2,1)}) %all-gather.10.cloned.1.call-update) | async-done | bytes 1179664 | tf_op jit(solution)/shard_map/all_gather | solution.py:63
  143.2 62.1 %all-to-all-done = bf16[8,2,112,768]{3,2,1,0:T(8,128)(2,1)S(1)} async-done(((bf16[8,2,112,768]{3,2,1,0:T(8,128)(2,1)}), bf16[8,2,112,768]{3,2,1,0:T(8,128)(2,1)S(1)}, u32[]{:S(2)}, u32[]{:S(2)}) %all-to-all-start) | async-done | bytes 2752544 | tf_op jit(solution)/shard_map/all_to_all | solution.py:141
  207.1 12.2 %fusion.34 = f32[896,3072]{1,0:T(8,128)} fusion(bf16[896,768]{1,0:T(8,128)(2,1)} %bitcast.173, bf16[1,768,3072]{2,1,0:T(8,128)(2,1)} %all-gather.12.cloned.1.call-done), kind=kOutput, calls=%fused_computation.47 | convolution fusion | flops 4227858432 | bytes 17104896 | tf_op jit(solution)/shard_map/dot_general | solution.py:146
  219.3 9.3 %fusion.28 = f32[896,3072]{1,0:T(8,128)} fusion(bf16[896,768]{1,0:T(8,128)(2,1)S(1)} %bitcast.167, bf16[1,768,3072]{2,1,0:T(8,128)(2,1)} %all-gather.16.cloned.1.call-done), kind=kOutput, calls=%fused_computation.41 | convolution fusion | flops 4227858432 | bytes 17104896 | tf_op jit(solution)/shard_map/dot_general | solution.py:146
  228.6 17.0 %all-gather.14.cloned.1.call-done = bf16[1,3072,768]{2,1,0:T(8,128)(2,1)} async-done(((bf16[1,768,768]{2,1,0:T(8,128)(2,1)}), bf16[1,3072,768]{2,1,0:T(8,128)(2,1)}) %all-gather.14.cloned.1.call-update) | async-done | bytes 4718608 | tf_op jit(solution)/shard_map/all_gather | solution.py:73
  245.6 10.6 %fusion.80 = bf16[896,768]{1,0:T(8,128)(2,1)S(1)} fusion(bf16[1,3072,768]{2,1,0:T(8,128)(2,1)} %all-gather.14.cloned.1.call-done, f32[896,3072]{1,0:T(8,128)} %fusion.34), kind=kOutput, calls=%fused_computation.94 | convolution fusion | flops 4253319168 | bytes 17104896 | tf_op jit(solution)/shard_map/dot_general | solution.py:148
  256.2 28.4 %all-gather.18.cloned.1.call-done = bf16[1,3072,768]{2,1,0:T(8,128)(2,1)} async-done(((bf16[1,768,768]{2,1,0:T(8,128)(2,1)}), bf16[1,3072,768]{2,1,0:T(8,128)(2,1)}) %all-gather.18.cloned.1.call-update) | async-done | bytes 4718608 | tf_op jit(solution)/shard_map/all_gather | solution.py:75
  284.5 10.5 %fusion.72 = bf16[896,768]{1,0:T(8,128)(2,1)S(1)} fusion(bf16[1,3072,768]{2,1,0:T(8,128)(2,1)} %all-gather.18.cloned.1.call-done, f32[896,3072]{1,0:T(8,128)} %fusion.28), kind=kOutput, calls=%fused_computation.92 | convolution fusion | flops 4253319168 | bytes 17104896 | tf_op jit(solution)/shard_map/dot_general | solution.py:148
  302.6 118.5 %all-gather = bf16[32,24,16]{1,2,0:T(8,128)(2,1)S(1)} all-gather(bf16[1,24,16]{1,2,0:T(8,128)(2,1)S(1)} %bitcast.181), channel_id=1, replica_groups=mesh['dp'=4,'expert'=8] {'dp','expert'}, dimensions={0}, use_global_device_ids=true | all-gather | bytes 25344 | tf_op jit(solution)/shard_map/all_gather | solution.py:64
  438.7 63.1 %all_to_all.20 = bf16[8,2,112,768]{3,2,1,0:T(8,128)(2,1)S(1)} all-to-all(bf16[8,2,112,768]{3,2,1,0:T(8,128)(2,1)S(1)} %bitcast.164), channel_id=1, replica_groups=mesh['dp'=4,'expert'=8] {'expert'}, dimensions={0} | all-to-all | bytes 5505024 | tf_op jit(solution)/shard_map/all_to_all | solution.py:155
  502.1 8.7 fusion.37
  511.3 13.8 %fusion.14 = bf16[896,3072]{1,0:T(8,128)(2,1)S(1)} fusion(f32[896,3072]{1,0:T(8,128)} %fusion.28, bf16[896,768]{1,0:T(8,128)(2,1)} %bitcast.171, bf16[1,3072,768]{2,1,0:T(8,128)(2,1)} %all-gather.18.cloned.1.call-done), kind=kOutput, calls=%fused_computation.23 | convolution fusion | flops 4282908672 | bytes 22609920 | tf_op jit(solution)/shard_map/rd,fd->rf/dot_general | solution.py:30
  527.5 6.8 fusion.36
  534.3 18.6 %fusion.75 = bf16[896,768]{1,0:T(8,128)(2,1)S(1)} fusion(bf16[1,768,3072]{2,1,0:T(8,128)(2,1)} %all-gather.12.cloned.1.call-done, f32[896,3072]{1,0:T(8,128)} %fusion.34, bf16[896,768]{1,0:T(8,128)(2,1)S(1)} %bitcast.169, bf16[1,3072,768]{2,1,0:T(8,128)(2,1)} %all-gather.14.cloned.1.call-done), kind=kOutput, calls=%fused_computation.93 | convolution fusion | flops 8511455232 | bytes 23199744 | tf_op jit(solution)/shard_map/rf,df->rd/dot_general | solution.py:32
  552.9 8.6 fusion.69
  570.1 57.7 %all-to-all-done.3 = bf16[8,2,112,768]{3,2,1,0:T(8,128)(2,1)S(1)} async-done(((bf16[8,2,112,768]{3,2,1,0:T(8,128)(2,1)}), bf16[8,2,112,768]{3,2,1,0:T(8,128)(2,1)S(1)}, u32[]{:S(2)}, u32[]{:S(2)}) %all-to-all-start.3) | async-done | bytes 2752544 | tf_op jit(solution)/shard_map/all_to_all | solution.py:169
  640.1 8.5 multiply_reduce_fusion
  656.7 10.1 %select_convert_fusion = bf16[12,512,512]{1,2,0:T(8,128)(2,1)S(1)} fusion(f32[12,512,512]{1,2,0:T(8,128)} %get-tuple-element.45, f32[12,512,512]{1,2,0:T(8,128)} %get-tuple-element.53, f32[12,512]{1,0:T(8,128)S(1)} %neg.20, f32[12,512]{1,0:T(8,128)S(1)} %copy-done.31, pred[512,512]{0,1:T(8,128)(4,1)S(1)} %copy-done.28), kind=kLoop, calls=%fused_computation.5 | loop fusion | flops 15728640 | bytes 31768576 | tf_op jit(solution)/shard_map/convert_element_type | solution.py:217
  685.3 39.4 %all-reduce.9 = (f32[768,16]{0,1:T(8,128)S(1)}, f32[768]{0:T(1024)S(1)}, f32[768]{0:T(1024)S(1)}, f32[768]{0:T(1024)S(1)}, f32[768]{0:T(1024)S(1)}) all-reduce(f32[768,16]{0,1:T(8,128)S(1)} %fusion.138, f32[768]{0:T(1024)S(1)} %get-tuple-element.13, ...), channel_id=4, replica_groups=mesh['dp'=4,'expert'=8] {'dp','expert'}, use_global_device_ids=true, to_apply=%region_20.21.clone | all-reduce | flops 15360 | bytes 122880
  736.8 18.5 %reduce-scatter.8.cloned.1.call-done = f32[768,24]{0,1:T(8,128)} async-done(((f32[768,768]{0,1:T(8,128)}), f32[768,24]{0,1:T(8,128)}) %reduce-scatter.8.cloned.1.call-update) | async-done | bytes 73744 | tf_op jit(solution)/shard_map/reduce_scatter | solution.py:245
  755.3 125.1 %reduce-scatter.6.cloned.1.call-done = f32[768,72]{0,1:T(8,128)} async-done(((f32[768,2304]{0,1:T(8,128)}), f32[768,72]{0,1:T(8,128)}) %reduce-scatter.6.cloned.1.call-update) | async-done | bytes 221200 | tf_op jit(solution)/shard_map/reduce_scatter | solution.py:244
  (267 shorter events, 128.6 us)
Async XLA Ops:
  7.2 66.7 %all-gather.8.cloned.1.call-start = ((), (), s32[]{:S(2)}) async-start(), calls=%async_computation.8 | async-start | bytes 3649536 | tf_op jit(solution)/shard_map/all_gather | solution.py:62
  8.0 47.1 %copy-start.53 = (s32[512,2]{0,1:T(2,128)S(1)}, s32[512,2]{0,1:T(2,128)}, u32[]{:S(2)}) copy-start(s32[512,2]{0,1:T(2,128)} %param.29) | copy-start | bytes 12292
  8.0 121.9 %all-gather.10.cloned.1.call-start = ((), (), s32[]{:S(2)}) async-start(), calls=%async_computation.9 | async-start | bytes 1216512 | tf_op jit(solution)/shard_map/all_gather | solution.py:63
  8.7 198.4 %all-gather.12.cloned.1.call-start = ((), (), s32[]{:S(2)}) async-start(), calls=%async_computation.10 | async-start | bytes 5898240 | tf_op jit(solution)/shard_map/all_gather | solution.py:72
  9.5 209.8 %all-gather.16.cloned.1.call-start = ((), (), s32[]{:S(2)}) async-start(), calls=%async_computation.12 | async-start | bytes 5898240 | tf_op jit(solution)/shard_map/all_gather | solution.py:74
  10.1 235.6 %all-gather.14.cloned.1.call-start = ((), (), s32[]{:S(2)}) async-start(), calls=%async_computation.11 | async-start | bytes 5898240 | tf_op jit(solution)/shard_map/all_gather | solution.py:73
  10.7 71.7 %copy-start.27 = (pred[512,512]{0,1:T(8,128)(4,1)}, pred[512,512]{0,1:T(8,128)(4,1)S(1)}, u32[]{:S(2)}) copy-start(pred[512,512]{0,1:T(8,128)(4,1)S(1)} %iota_compare_fusion.2) | copy-start | bytes 786436
  10.9 68.6 %copy-start.42 = (f32[512]{0:T(512)}, f32[512]{0:T(512)S(1)}, u32[]{:S(2)}) copy-start(f32[512]{0:T(512)S(1)} %broadcast_multiply_fusion.1) | copy-start | bytes 6148
  11.3 68.2 %copy-start.49 = (f32[512]{0:T(512)}, f32[512]{0:T(512)S(1)}, u32[]{:S(2)}) copy-start(f32[512]{0:T(512)S(1)} %fusion.86) | copy-start | bytes 6148
  55.0 78.6 %copy-start.34 = (f32[768]{0:T(1024)}, f32[768]{0:T(1024)S(1)}, u32[]{:S(2)}) copy-start(f32[768]{0:T(1024)S(1)} %convert_element_type.148) | copy-start | bytes 9220
  134.0 289.6 %copy-start.9 = (bf16[512,768]{1,0:T(8,128)(2,1)}, bf16[512,768]{1,0:T(8,128)(2,1)S(1)}, u32[]{:S(2)}) copy-start(bf16[512,768]{1,0:T(8,128)(2,1)S(1)} %add_convert_fusion.2) | copy-start | bytes 2359300
  138.3 67.1 %all-to-all-start = ((bf16[8,2,112,768]{3,2,1,0:T(8,128)(2,1)}), bf16[8,2,112,768]{3,2,1,0:T(8,128)(2,1)S(1)}, u32[]{:S(2)}, u32[]{:S(2)}) async-start(bf16[8,2,112,768]{3,2,1,0:T(8,128)(2,1)} %bitcast.163), calls=%async_computation | async-start | bytes 5505024 | tf_op jit(solution)/shard_map/all_to_all | solution.py:141
  142.7 141.9 %all-gather.18.cloned.1.call-start = ((), (), s32[]{:S(2)}) async-start(), calls=%async_computation.13 | async-start | bytes 5898240 | tf_op jit(solution)/shard_map/all_gather | solution.py:75
  296.9 128.3 %all-to-all-start.1 = ((bf16[8,2,112,768]{3,2,1,0:T(8,128)(2,1)}), bf16[8,2,112,768]{3,2,1,0:T(8,128)(2,1)S(1)}, u32[]{:S(2)}, u32[]{:S(2)}) async-start(bf16[8,2,112,768]{3,2,1,0:T(8,128)(2,1)} %pad_maximum_fusion), calls=%async_computation.1 | async-start | bytes 5505024 | tf_op jit(solution)/shard_map/all_to_all | solution.py:153
  302.6 428.4 %reduce-scatter.12.cloned.1.call-start = ((), (), s32[]{:S(2)}) async-start(), calls=%async_computation.17 | async-start | bytes 5898240 | tf_op jit(solution)/shard_map/reduce_scatter | solution.py:187
  424.6 143.8 %copy-start.36 = (f32[512]{0:T(512)}, f32[512]{0:T(512)S(1)}, u32[]{:S(2)}) copy-start(f32[512]{0:T(512)S(1)} %get-tuple-element.49) | copy-start | bytes 6148
  425.3 141.8 %copy-start.44 = (f32[512]{0:T(512)}, f32[512]{0:T(512)S(1)}, u32[]{:S(2)}) copy-start(f32[512]{0:T(512)S(1)} %fusion.109) | copy-start | bytes 6148
  436.6 65.4 %slice-start = ((s8[11010048]{0:T(1024)(128)(4,1)}), s8[2621440]{0:T(1024)(128)(4,1)S(1)}, s32[]{:S(2)}) async-start(s8[11010048]{0:T(1024)(128)(4,1)} %bitcast.192), calls=%async_computation.18 | async-start | bytes 5242880
  436.6 65.4 %slice-start.1 = ((s8[11010048]{0:T(1024)(128)(4,1)}), s8[4194304]{0:T(1024)(128)(4,1)S(1)}, s32[]{:S(2)}) async-start(s8[11010048]{0:T(1024)(128)(4,1)} %bitcast.192), calls=%async_computation.19 | async-start | bytes 8388608
  438.7 63.4 %slice-start.2 = ((s8[11010048]{0:T(1024)(128)(4,1)}), s8[4194304]{0:T(1024)(128)(4,1)S(1)}, s32[]{:S(2)}) async-start(s8[11010048]{0:T(1024)(128)(4,1)} %bitcast.192), calls=%async_computation.20 | async-start | bytes 8388608
  510.8 223.0 %reduce-scatter.10.cloned.1.call-start = ((), (), s32[]{:S(2)}) async-start(), calls=%async_computation.16 | async-start | bytes 5898240 | tf_op jit(solution)/shard_map/reduce_scatter | solution.py:184
  563.3 64.5 %all-to-all-start.3 = ((bf16[8,2,112,768]{3,2,1,0:T(8,128)(2,1)}), bf16[8,2,112,768]{3,2,1,0:T(8,128)(2,1)S(1)}, u32[]{:S(2)}, u32[]{:S(2)}) async-start(bf16[8,2,112,768]{3,2,1,0:T(8,128)(2,1)} %pad_maximum_fusion.1), calls=%async_computation.3 | async-start | bytes 5505024 | tf_op jit(solution)/shard_map/all_to_all | solution.py:169
  567.0 188.3 %reduce-scatter.8.cloned.1.call-start = ((), (), s32[]{:S(2)}) async-start(), calls=%async_computation.15 | async-start | bytes 2433024 | tf_op jit(solution)/shard_map/reduce_scatter | solution.py:245
  656.6 223.8 %reduce-scatter.6.cloned.1.call-start = ((), (), s32[]{:S(2)}) async-start(), calls=%async_computation.14 | async-start | bytes 7299072 | tf_op jit(solution)/shard_map/reduce_scatter | solution.py:244
  (68 other events, 419.8 us)
Sparse Core Ops, SparseCore 0:
  11.0 62.9 all-gather.7
  76.9 52.9 all-gather.9
  131.5 36.3 all-gather.11
  169.2 37.4 all-gather.15
  208.1 37.4 all-gather.13
  247.0 37.4 all-gather.17
  510.9 46.4 reduce-scatter.11
  560.1 47.8 reduce-scatter.9
  656.7 98.5 reduce-scatter.7
  762.3 118.0 reduce-scatter.5
where the time goes:
time: 898 us; the launch traced here: 887 us
  waiting for transfers between devices  358 us (40%)
  blocking collectives  263 us (29%)
  matrix products  170 us (19%)
  other arithmetic  37.7 us (4%)
  local copies, waits for them, and re-layouts  27.9 us (3%)
  between operations  15.4 us (2%)
  starting transfers between devices  15 us (2%)
    reduce_scatter x1, waiting for transfers between devices, shards(): lax.psum_scatter(in_grad_full, ('dp', 'expert'), scatter_dimension=1, til...  125 us
    all_gather x1, blocking collectives, shards(): lax.all_gather(router, ('dp', 'expert'), axis=0, tiled=True)  119 us
    unnamed x2, blocking collectives  81.7 us
    all_to_all x1, blocking collectives, shards(): lax.all_to_all(grad_slots, 'expert', split_axis=0, concat_axis=0, tiled=T...  63.1 us
    all_to_all x1, waiting for transfers between devices, shards(): lax.all_to_all(outgoing, 'expert', split_axis=0, concat_axis=0, tiled=True)  62.1 us
    all_to_all x1, waiting for transfers between devices, shards(): lax.all_to_all(grad_stack, 'expert', split_axis=0, concat_axis=0, tiled=T...  57.7 us
    all_gather x1, waiting for transfers between devices, shards(): lax.all_gather(new_w2, 'dp', axis=1, tiled=True)  28.4 us
    all_gather x1, waiting for transfers between devices, shards(): lax.all_gather(attn_out, ('dp', 'expert'), axis=1, tiled=True)  27.7 us
  transfers between devices with their start and end apart: 13, of which 8 were waited for; matrix products, arithmetic and copies ran while one was open for 21% of the time, Pallas kernels for 0%

commit v1 on v0

v1 whole, which is shorter than its diff:
```python
import functools

import jax
import jax.numpy as jnp
from jax import lax
from jax.experimental import pallas as pl
from jax.experimental.pallas import tpu as pltpu
from jax.sharding import PartitionSpec as P

HEADS = 12
HEAD_DIM = 64
BF = jnp.bfloat16
F32 = jnp.float32


def mm(a, b, dims, out=F32):
    return lax.dot_general(a, b, (dims, ((), ())), preferred_element_type=F32).astype(out)


def powers(count):
    found = []
    bit = 1
    while bit < count:
        found.append(bit)
        bit *= 2
    return found


def swap(values, axis, bit):
    count = lax.axis_size(axis)
    return lax.ppermute(values, axis, [(i, i ^ bit) for i in range(count)])


def my_bit(axis, bit):
    return (lax.axis_index(axis) // bit) % 2


def canonical():
    return [("dp", b) for b in reversed(powers(lax.axis_size("dp")))] + [
        ("expert", b) for b in reversed(powers(lax.axis_size("expert")))
    ]


def orders():
    dp_bits = powers(lax.axis_size("dp"))
    expert_bits = powers(lax.axis_size("expert"))
    core = [("dp", dp_bits[0])]
    xs = [("dp", b) for b in reversed(dp_bits[1:])]
    ys = [("expert", expert_bits[0])]
    zs = [("expert", b) for b in reversed(expert_bits[1:])]
    return (zs + ys + xs + core, xs + zs + ys + core, ys + xs + zs + core)


def gather_blocks(block, order):
    lead = []
    current = block
    for axis, bit in order:
        other = swap(current, axis, bit)
        low = my_bit(axis, bit) == 0
        current = jnp.stack([jnp.where(low, current, other), jnp.where(low, other, current)])
        lead.insert(0, (axis, bit))
    want = canonical()
    tail = list(range(len(lead), len(lead) + block.ndim))
    current = current.transpose([lead.index(w) for w in want] + tail)
    return current.reshape((-1,) + block.shape[1:])


def scatter_blocks(values, order):
    lead = canonical()
    current = values.reshape([2] * len(lead) + [-1] + list(values.shape[1:]))
    for axis, bit in reversed(order):
        at = lead.index((axis, bit))
        mine = my_bit(axis, bit)
        keep = lax.dynamic_index_in_dim(current, mine, at, keepdims=False)
        send = lax.dynamic_index_in_dim(current, 1 - mine, at, keepdims=False)
        got = swap(send.astype(BF), axis, bit)
        current = keep.astype(F32) + got.astype(F32)
        lead.pop(at)
    return current


def gather_dp(shard):
    dp_bits = powers(lax.axis_size("dp"))
    current = shard
    order = [("dp", b) for b in reversed(dp_bits)]
    lead = []
    for axis, bit in order:
        other = swap(current, axis, bit)
        low = my_bit(axis, bit) == 0
        current = jnp.stack([jnp.where(low, current, other), jnp.where(low, other, current)])
        lead.insert(0, (axis, bit))
    tail = list(range(len(lead), len(lead) + shard.ndim))
    current = current.transpose([lead.index(w) for w in order] + tail)
    return current.reshape((-1,) + shard.shape[1:])


def scatter_dp(values):
    dp_bits = powers(lax.axis_size("dp"))
    lead = [("dp", b) for b in reversed(dp_bits)]
    current = values.reshape([2] * len(lead) + [-1] + list(values.shape[1:]))
    for axis, bit in [("dp", b) for b in dp_bits]:
        at = lead.index((axis, bit))
        mine = my_bit(axis, bit)
        keep = lax.dynamic_index_in_dim(current, mine, at, keepdims=False)
        send = lax.dynamic_index_in_dim(current, 1 - mine, at, keepdims=False)
        got = swap(send.astype(BF), axis, bit)
        current = keep.astype(F32) + got.astype(F32)
        lead.pop(at)
    return current


LIMIT = 56 * 1024 * 1024
QUERY_BLOCK = 128
SCALE = HEAD_DIM ** (-0.5)


def dot(a, b, over_a, over_b):
    return lax.dot_general(
        a, b, (((over_a,), (over_b,)), ((), ())), preferred_element_type=F32
    )


def whole(array):
    return jax.ShapeDtypeStruct(array[0], array[1])


def plain_call(body, outs, scratch, name, *args):
    space = pl.BlockSpec(memory_space=pltpu.VMEM)
    return pl.pallas_call(
        body,
        out_shape=[whole(o) for o in outs],
        in_specs=[space] * len(args),
        out_specs=[space] * len(outs),
        scratch_shapes=scratch,
        compiler_params=pltpu.CompilerParams(vmem_limit_bytes=LIMIT),
        name=name,
    )(*args)


def norm_parts(values):
    centre = values - jnp.mean(values, axis=-1, keepdims=True)
    spread = jnp.mean(centre * centre, axis=-1, keepdims=True)
    scale = lax.rsqrt(spread + 1e-05)
    return centre * scale, scale


def norm_back(values, gain, grad):
    normal, scale = norm_parts(values)
    scaled = grad * gain
    back = scale * (
        scaled
        - jnp.mean(scaled, axis=-1, keepdims=True)
        - normal * jnp.mean(scaled * normal, axis=-1, keepdims=True)
    )
    return back, jnp.sum(grad * normal, axis=0, keepdims=True), jnp.sum(grad, axis=0, keepdims=True)


def place_rows(target_ref, values, first, count):
    tokens = values.shape[0]
    at = lax.broadcasted_iota(jnp.int32, (count, tokens), 0) + first
    hit = (at == target_ref[0:1, :]) | (at == target_ref[1:2, :])
    return dot(hit.astype(F32).astype(BF), values, 1, 0).astype(BF)


def place_kernel(target_ref, values_ref, old_ref, new_ref):
    values = values_ref[...]
    count = old_ref.shape[0]
    half = count // 2
    for at, ref in ((0, old_ref), (count, new_ref)):
        for part in range(2):
            ref[part * half : (part + 1) * half, :] = place_rows(
                target_ref, values, at + part * half, half
            )


def take_rows(target_ref, slots_refs, tokens):
    total = None
    first = 0
    for ref in slots_refs:
        count = ref.shape[0]
        at = lax.broadcasted_iota(jnp.int32, (tokens, count), 1) + first
        hit = (at == target_ref[:, 0:1]) | (at == target_ref[:, 1:2])
        part = dot(hit.astype(F32).astype(BF), ref[...], 1, 0)
        total = part if total is None else total + part
        first += count
    return total


def causal(size):
    rowpos = lax.broadcasted_iota(jnp.int32, (size, size), 0)
    colpos = lax.broadcasted_iota(jnp.int32, (size, size), 1)
    return rowpos >= colpos


def head_lanes(block, which):
    lane = lax.broadcasted_iota(jnp.int32, block.shape, 1)
    keep = (lane < HEAD_DIM) if which == 0 else (lane >= HEAD_DIM)
    return jnp.where(keep, block, jnp.zeros_like(block))


def block_softmax(query, keys, seen):
    size = query.shape[0]
    before = keys.shape[0] - size
    own = dot(query, keys[before:], 1, 1)
    own = jnp.where(seen, own, -1e30)
    top = jnp.max(own, axis=-1, keepdims=True)
    if before:
        past = dot(query, keys[:before], 1, 1)
        top = jnp.maximum(top, jnp.max(past, axis=-1, keepdims=True))
        past = jnp.exp(past - top)
    own = jnp.exp(own - top)
    total = jnp.sum(own, axis=-1, keepdims=True)
    if before:
        total = total + jnp.sum(past, axis=-1, keepdims=True)
    inverse = 1.0 / total
    own = own * inverse
    return (past * inverse, own) if before else (own,)


def pair_columns(pair, part, width):
    return pl.ds(pl.multiple_of(part * width + pair * 2 * HEAD_DIM, 2 * HEAD_DIM), 2 * HEAD_DIM)


def forward_kernel(
    x_ref,
    in_ref,
    out_ref,
    vec_ref,
    target_ref,
    normed_ref,
    proj_ref,
    context_ref,
    middle_ref,
    old_ref,
    new_ref,
):
    length, width = x_ref.shape
    x = x_ref[...].astype(F32)
    normal, _ = norm_parts(x)
    normed = (normal * vec_ref[0:1, :] + vec_ref[1:2, :]).astype(BF)
    normed_ref[...] = normed
    for part in range(3):
        cols = slice(part * width, (part + 1) * width)
        proj_ref[:, cols] = dot(normed, in_ref[cols, :], 1, 1).astype(BF)
    size = min(QUERY_BLOCK, length)
    seen = causal(size)

    def one_pair(pair, carry):
        q_at, k_at, v_at = (pair_columns(pair, part, width) for part in range(3))
        for block in range(length // size):
            rows = slice(block * size, (block + 1) * size)
            upto = (block + 1) * size
            query = proj_ref[rows, q_at] * BF(SCALE)
            keys = proj_ref[0:upto, k_at]
            values = proj_ref[0:upto, v_at]
            outs = []
            for which in range(2):
                probs = block_softmax(head_lanes(query, which), keys, seen)
                probs = [p.astype(BF) for p in probs]
                out = dot(probs[-1], values[upto - size :], 1, 0)
                if len(probs) > 1:
                    out = out + dot(probs[0], values[: upto - size], 1, 0)
                outs.append(out)
            lane = lax.broadcasted_iota(jnp.int32, outs[0].shape, 1)
            context_ref[rows, pair_columns(pair, 0, width)] = jnp.where(
                lane < HEAD_DIM, outs[0], outs[1]
            ).astype(BF)
        return carry

    lax.fori_loop(0, HEADS // 2, one_pair, 0)
    middle = x + dot(context_ref[...], out_ref[...], 1, 1)
    middle_ref[...] = middle
    normal, _ = norm_parts(middle)
    normed_two = (normal * vec_ref[2:3, :] + vec_ref[3:4, :]).astype(BF)
    count = old_ref.shape[0]
    half = count // 2
    for at, ref in ((0, old_ref), (count, new_ref)):
        for part in range(2):
            ref[part * half : (part + 1) * half, :] = place_rows(
                target_ref, normed_two, at + part * half, half
            )


def branch_kernel(
    old_ref,
    new_ref,
    target_ref,
    cot_ref,
    middle_ref,
    context_ref,
    out_ref,
    vec_ref,
    gmid_ref,
    gctx_ref,
    og0_ref,
    og1_ref,
    og2_ref,
    sums_ref,
):
    length, width = cot_ref.shape
    grad = take_rows(target_ref, (old_ref, new_ref), length)
    back, gain_sum, bias_sum = norm_back(middle_ref[...], vec_ref[2:3, :], grad)
    gmid = back + cot_ref[...].astype(F32)
    gmid_ref[...] = gmid
    sums_ref[...] = jnp.concatenate([gain_sum, bias_sum, jnp.zeros((6, width), F32)], axis=0)
    branch = gmid.astype(BF)
    gctx_ref[...] = dot(branch, out_ref[...], 1, 0).astype(BF)
    third = width // 3
    for part, ref in enumerate((og0_ref, og1_ref, og2_ref)):
        ref[...] = dot(branch, context_ref[:, part * third : (part + 1) * third], 0, 0).astype(BF)


def attention_back_kernel(
    proj_ref, gctx_ref, normed_ref, gproj_ref, ig0_ref, ig1_ref, ig2_ref, gk_acc, gv_acc
):
    length, width = gctx_ref.shape
    size = min(QUERY_BLOCK, length)
    seen = causal(size)

    def one_pair(pair, carry):
        q_at, k_at, v_at = (pair_columns(pair, part, width) for part in range(3))
        gk_acc[...] = jnp.zeros_like(gk_acc)
        gv_acc[...] = jnp.zeros_like(gv_acc)
        for block in range(length // size):
            rows = slice(block * size, (block + 1) * size)
            upto = (block + 1) * size
            query = proj_ref[rows, q_at] * BF(SCALE)
            keys = proj_ref[0:upto, k_at]
            values = proj_ref[0:upto, v_at]
            gout = gctx_ref[rows, pair_columns(pair, 0, width)]
            grads = []
            for which in range(2):
                mine = head_lanes(query, which)
                gmine = head_lanes(gout, which)
                probs = block_softmax(mine, keys, seen)
                spans = [slice(upto - size, upto)]
                if len(probs) > 1:
                    spans = [slice(0, upto - size)] + spans
                gprobs = [dot(gmine, values[s], 1, 1) for s in spans]
                row = sum(jnp.sum(p * g, axis=-1, keepdims=True) for p, g in zip(probs, gprobs))
                gquery = None
                for p, g, s in zip(probs, gprobs, spans):
                    gscore = (p * (g - row)).astype(BF)
                    part = dot(gscore, keys[s], 1, 0)
                    gquery = part if gquery is None else gquery + part
                    gk_acc[s, :] += dot(gscore, mine, 0, 0)
                    gv_acc[s, :] += dot(p.astype(BF), gmine, 0, 0)
                grads.append(gquery * SCALE)
            lane = lax.broadcasted_iota(jnp.int32, grads[0].shape, 1)
            gproj_ref[rows, q_at] = jnp.where(lane < HEAD_DIM, grads[0], grads[1]).astype(BF)
        gproj_ref[:, k_at] = gk_acc[...].astype(BF)
        gproj_ref[:, v_at] = gv_acc[...].astype(BF)
        return carry

    lax.fori_loop(0, HEADS // 2, one_pair, 0)
    third = width // 3
    for part, ref in enumerate((ig0_ref, ig1_ref, ig2_ref)):
        ref[...] = dot(
            gproj_ref[...], normed_ref[:, part * third : (part + 1) * third], 0, 0
        ).astype(BF)


def input_kernel(gproj_ref, in_ref, x_ref, vec_ref, gmid_ref, grad_ref, sums_ref):
    grad = dot(gproj_ref[...], in_ref[...], 1, 0)
    back, gain_sum, bias_sum = norm_back(x_ref[...].astype(F32), vec_ref[0:1, :], grad)
    grad_ref[...] = gmid_ref[...] + back
    width = x_ref.shape[1]
    sums_ref[...] = jnp.concatenate([gain_sum, bias_sum, jnp.zeros((6, width), F32)], axis=0)


def mixed_kernel(old_ref, new_ref, target_ref, middle_ref, mixed_ref):
    total = take_rows(target_ref, (old_ref, new_ref), middle_ref.shape[0])
    mixed_ref[...] = (middle_ref[...] + total).astype(BF)


def gelu_pair(x):
    c = 0.7978845608028654
    sq = x * x
    t = jnp.tanh(c * x * (1.0 + 0.044715 * sq))
    half = 0.5 * (1.0 + t)
    slope = half + 0.5 * x * (1.0 - t * t) * (c * (1.0 + 3 * 0.044715 * sq))
    return x * half, slope

def expert_kernel(train, steps, mine_ref, rows_ref, grads_ref, router_ref, up_ref, down_ref, *rest):
    if train:
        gated_ref, gin_ref, rgrad_ref, dup_ref, ddown_ref, out_acc, gin_acc, scaled, gate_s, probs_s = rest
    else:
        gated_ref, gin_ref, rgrad_ref, out_acc, gin_acc, scaled, gate_s, probs_s = rest
    j = pl.program_id(0)
    mine = mine_ref[0:1, :]

    @pl.when(j == 0)
    def _():
        logits = dot(rows_ref[...], router_ref[...], 1, 0)
        live = lax.broadcasted_iota(jnp.int32, logits.shape, 1) < mine_ref[1, 0].astype(jnp.int32)
        logits = jnp.where(live, logits, -1e30)
        e = jnp.exp(logits - jnp.max(logits, axis=1, keepdims=True))
        probs = e / jnp.sum(e, axis=1, keepdims=True)
        probs_s[...] = probs
        gate = jnp.sum(probs * mine, axis=1, keepdims=True)
        gate_s[...] = jnp.broadcast_to(gate, gate_s.shape)
        scaled[...] = (grads_ref[...].astype(F32) * gate).astype(BF)

    rows = rows_ref[...]
    up = up_ref[...]
    down = down_ref[...]
    pre = dot(rows, up, 1, 0)
    hid, slope = gelu_pair(pre)
    hid = hid.astype(BF)
    gh = dot(scaled[...], down, 1, 1)
    gpre = (gh * slope).astype(BF)
    o = dot(hid, down, 1, 0)
    gi = dot(gpre, up, 1, 1)

    @pl.when(j == 0)
    def _():
        out_acc[...] = o
        gin_acc[...] = gi

    @pl.when(j > 0)
    def _():
        out_acc[...] += o
        gin_acc[...] += gi

    if train:
        dup_ref[...] = dot(rows, gpre, 0, 0).astype(BF)
        ddown_ref[...] = dot(hid, scaled[...], 0, 0).astype(BF)

    @pl.when(j == steps - 1)
    def _():
        produced = out_acc[...].astype(BF).astype(F32)
        gate = gate_s[:, 0:1]
        gated_ref[...] = (produced * gate).astype(BF)
        grad_gate = jnp.sum(produced * grads_ref[...].astype(F32), axis=1, keepdims=True)
        gl = (grad_gate * gate * (mine - probs_s[...])).astype(BF)
        gin_ref[...] = (gin_acc[...] + dot(gl, router_ref[...], 1, 1)).astype(BF)
        rgrad_ref[...] = dot(gl, rows_ref[...], 0, 0)

def expert_call(mine, rows, grads, router_pad, up, down, train, ft=768, limit=LIMIT):
    n, d = rows.shape
    f = up.shape[1]
    steps = f // ft
    one = pl.Buffered(buffer_count=1)
    whole = lambda s: pl.BlockSpec(s, lambda j: (0, 0), pipeline_mode=one)
    outs = [jax.ShapeDtypeStruct((n, d), BF), jax.ShapeDtypeStruct((n, d), BF), jax.ShapeDtypeStruct((128, d), F32)]
    out_specs = [whole((n, d)), whole((n, d)), whole((128, d))]
    if train:
        outs += [jax.ShapeDtypeStruct((d, f), BF), jax.ShapeDtypeStruct((f, d), BF)]
        out_specs += [pl.BlockSpec((d, ft), lambda j: (0, j)), pl.BlockSpec((ft, d), lambda j: (j, 0))]
    return pl.pallas_call(
        functools.partial(expert_kernel, train, steps),
        grid=(steps,),
        in_specs=[whole((8, 128)), whole((n, d)), whole((n, d)), whole((d, 128)),
                  pl.BlockSpec((d, ft), lambda j: (0, j)), pl.BlockSpec((ft, d), lambda j: (j, 0))],
        out_specs=out_specs, out_shape=outs,
        scratch_shapes=[pltpu.VMEM((n, d), F32), pltpu.VMEM((n, d), F32), pltpu.VMEM((n, d), BF), pltpu.VMEM((n, 128), F32), pltpu.VMEM((n, 128), F32)],
        compiler_params=pltpu.CompilerParams(vmem_limit_bytes=limit),
        name="expert_new" if train else "expert_old",
    )(mine, rows, grads, router_pad, up, down)


def shards(
    block_input,
    cotangent,
    attn_in,
    attn_out,
    router,
    ln1_gain,
    ln1_bias,
    ln2_gain,
    ln2_bias,
    new_w1,
    new_w2,
    old_w1,
    old_w2,
    expert_ids,
    slots,
    drops,
):
    length, width = block_input.shape
    peers = lax.axis_size("expert")
    devices = lax.axis_size("dp") * peers
    experts = 2 * peers
    capacity = max(length * 7 // (2 * experts), 2)
    me = lax.axis_index("expert")
    ways = orders()
    third = width // 3
    in_share = attn_in.shape[1]
    share = width // devices
    router_size = router.size

    small = jnp.concatenate(
        [router.reshape(-1), ln1_gain, ln1_bias, ln2_gain, ln2_bias]
    )
    used = small.size
    lines = -(-used // width)
    small = jnp.pad(small, (0, lines * width - used)).reshape(lines, width)
    packed = jnp.concatenate([attn_in.T, attn_out.T, small], axis=0)
    packed = jnp.pad(packed, ((0, -packed.shape[0] % 8), (0, 0)))
    parts = [
        gather_blocks(packed[:, p * third : (p + 1) * third], ways[p]).reshape(
            devices, packed.shape[0], third
        )
        for p in range(3)
    ]
    full = jnp.concatenate(parts, axis=2)
    in_full = full[:, :in_share].reshape(3 * width, width)
    out_full = full[:, in_share : in_share + share].reshape(width, width)
    small_full = full[:, in_share + share : in_share + share + lines].reshape(devices, -1)
    router_full = small_full[:, :router_size].reshape(width, experts)
    router_pad = jnp.pad(router_full, ((0, 0), (0, 128 - experts)))
    vectors = small_full[:, router_size:used].reshape(devices, 4, share).transpose(1, 0, 2)
    vectors = jnp.pad(vectors.reshape(4, width).astype(F32), ((0, 4), (0, 0)))

    (old_w1, old_w2, new_w1, new_w2), parts = lax.optimization_barrier(
        ((old_w1, old_w2, new_w1, new_w2), parts)
    )
    old_up = gather_dp(old_w1[0])
    old_down = gather_dp(old_w2[0])
    new_up = gather_dp(new_w1[0])
    new_down = gather_dp(new_w2[0])

    target = ((expert_ids % 2) * peers + expert_ids // 2) * capacity + slots
    target = jnp.where(drops == 0, target, -1)
    target_rows = jnp.pad(target.T, ((0, 6), (0, 0)), constant_values=-1)
    count = peers * capacity

    def send(block):
        block = block.reshape(peers, capacity, width)
        moved = lax.all_to_all(block, "expert", split_axis=0, concat_axis=0, tiled=True)
        return moved.reshape(count, width)

    slot_outs = [((count, width), BF)] * 2
    gold, gnew = plain_call(place_kernel, slot_outs, [], "place_grads", target_rows, cotangent)
    gold = send(gold)
    gnew = send(gnew)

    normed, proj, context, middle, rold, rnew = plain_call(
        forward_kernel,
        [
            ((length, width), BF),
            ((length, 3 * width), BF),
            ((length, width), BF),
            ((length, width), F32),
        ]
        + slot_outs,
        [],
        "attention_forward",
        block_input,
        in_full,
        out_full,
        vectors,
        target_rows,
    )
    rold = send(rold)
    rnew = send(rnew)

    lane = lax.broadcasted_iota(jnp.int32, (8, 128), 1)
    line = lax.broadcasted_iota(jnp.int32, (8, 128), 0)

    def chosen(expert):
        return jnp.where(line == 0, (lane == expert).astype(F32), F32(experts))

    old_gated, old_in, old_router = expert_call(
        chosen(2 * me), rold, gold, router_pad, old_up, old_down, False
    )
    old_in = send(old_in)
    new_gated, new_in, new_router, grad_up, grad_down = expert_call(
        chosen(2 * me + 1), rnew, gnew, router_pad, new_up, new_down, True
    )
    new_in = send(new_in)
    old_gated = send(old_gated)
    new_gated = send(new_gated)
    new_w1_grad = scatter_dp(grad_up)[None]
    new_w2_grad = scatter_dp(grad_down)[None]
    router_part = (old_router + new_router)[:experts].T

    gmid, gctx, og0, og1, og2, sums_two = plain_call(
        branch_kernel,
        [((length, width), F32), ((length, width), BF)]
        + [((width, third), BF)] * 3
        + [((8, width), F32)],
        [],
        "branch_backward",
        old_in,
        new_in,
        target,
        cotangent,
        middle,
        context,
        out_full,
        vectors,
    )
    attn_out_grad = jnp.concatenate(
        [scatter_blocks(og, way) for og, way in zip((og0, og1, og2), ways)], axis=1
    ).T
    gproj, ig0, ig1, ig2 = plain_call(
        attention_back_kernel,
        [((length, 3 * width), BF)] + [((3 * width, third), BF)] * 3,
        [pltpu.VMEM((length, 2 * HEAD_DIM), F32)] * 2,
        "attention_backward",
        proj,
        gctx,
        normed,
    )
    attn_in_grad = jnp.concatenate(
        [scatter_blocks(ig, way) for ig, way in zip((ig0, ig1, ig2), ways)], axis=1
    ).T
    input_grad, sums_one = plain_call(
        input_kernel,
        [((length, width), F32), ((8, width), F32)],
        [],
        "input_backward",
        gproj,
        in_full,
        block_input,
        vectors,
        gmid,
    )
    (mixed,) = plain_call(
        mixed_kernel,
        [((length, width), BF)],
        [],
        "mixed_output",
        old_gated,
        new_gated,
        target,
        middle,
    )
    vector_grads = jnp.concatenate([sums_one[:2], sums_two[:2]], axis=0)
    vector_grads = vector_grads.reshape(4, devices, share).transpose(1, 0, 2)
    small_grads = jnp.concatenate(
        [router_part.reshape(devices, -1), vector_grads.reshape(devices, -1)], axis=1
    )
    small_grads = scatter_blocks(small_grads, ways[1]).reshape(-1)
    router_grad = small_grads[:router_size].reshape(share, experts)
    vector_grads = small_grads[router_size:].reshape(4, share)
    return (
        mixed,
        input_grad,
        attn_in_grad,
        attn_out_grad,
        router_grad,
        vector_grads[0],
        vector_grads[1],
        vector_grads[2],
        vector_grads[3],
        new_w1_grad,
        new_w2_grad,
    )


def solution(mesh):
    both = ("dp", "expert")
    rows = P(both, None)
    columns = P(None, both)
    vector = P(both)
    weight = P("expert", "dp", None)
    in_specs = (
        [rows, rows, columns, columns, rows] + [vector] * 4 + [weight] * 4 + [rows] * 3
    )
    out_specs = [rows, rows, columns, columns, rows] + [vector] * 4 + [weight] * 2
    return jax.shard_map(
        shards, mesh=mesh, in_specs=tuple(in_specs), out_specs=tuple(out_specs), check_vma=False
    )
```

time: 898 us -> 564 us (0.63)
  blocking collectives: 263 us -> 0 us
  matrix products: 170 us -> 0 us
  waiting for transfers between devices: 358 us -> 206 us
  Pallas kernels: 0 us -> 149 us
  starting transfers between devices: 15 us -> 96.7 us
  local copies, waits for them, and re-layouts: 27.9 us -> 47.3 us
  other arithmetic: 37.7 us -> 57 us
  between operations: 15.4 us -> 2.37 us
    ppermute x0 -> x62, waiting for transfers between devices: none -> 181 us  [swap(): return lax.ppermute(values, axis, [(i, i ^ bit) for i in range(count)])]
    dot_general x29 -> x0, matrix products: 162 us -> none  [the longest x2 27.2 us: expert_backward(): jnp.einsum('rf,df->rd', grad_pre, upward, preferred_element_type=jnp.floa...]
    pallas_call x0 -> x8, Pallas kernels: none -> 149 us  [the longest x6 83.9 us: plain_call(): pl.pallas_call(body, out_shape=[whole(o) for o in outs], in_specs=[space]...]
    reduce_scatter x4 -> x0, waiting for transfers between devices: 144 us -> none  [the longest x1 125 us: shards(): lax.psum_scatter(in_grad_full, ('dp', 'expert'), scatter_dimension=1, til...]
    all_gather x1 -> x0, blocking collectives: 119 us -> none  [shards(): lax.all_gather(router, ('dp', 'expert'), axis=0, tiled=True)]
    all_to_all x3 -> x8, waiting for transfers between devices: 120 us -> 25.3 us  [send(): lax.all_to_all(block, 'expert', split_axis=0, concat_axis=0, tiled=True)]
    all_gather x6 -> x0, waiting for transfers between devices: 91.4 us -> none  [the longest x1 28.4 us: shards(): lax.all_gather(new_w2, 'dp', axis=1, tiled=True)]
    unnamed x2 -> x0, blocking collectives: 81.7 us -> none
  transfers between devices with their start and end apart: 13 -> 70, of which waited for: 8 -> 32; matrix products, arithmetic and copies ran while one was open for 21% -> 16% of each run, Pallas kernels for 0% -> 27%
where the time goes in v1:
time: 564 us; the launch traced here: 558 us
  waiting for transfers between devices  206 us (37%)
  Pallas kernels  149 us (26%)
  starting transfers between devices  96.7 us (17%)
  other arithmetic  57 us (10%)
  local copies, waits for them, and re-layouts  47.3 us (8%)
    ppermute x62, waiting for transfers between devices, swap(): return lax.ppermute(values, axis, [(i, i ^ bit) for i in range(count)])  181 us
    pallas_call x6, Pallas kernels, plain_call(): pl.pallas_call(body, out_shape=[whole(o) for o in outs], in_specs=[space]...  83.9 us
    pallas_call x2, Pallas kernels, expert_call(): pl.pallas_call(functools.partial(expert_kernel, train, steps), grid=(step...  65 us
    ppermute x62, starting transfers between devices, swap(): return lax.ppermute(values, axis, [(i, i ^ bit) for i in range(count)])  54.2 us
    all_to_all x8, starting transfers between devices, send(): lax.all_to_all(block, 'expert', split_axis=0, concat_axis=0, tiled=True)  42.6 us
    all_to_all x8, waiting for transfers between devices, send(): lax.all_to_all(block, 'expert', split_axis=0, concat_axis=0, tiled=True)  25.3 us
    another operation x12, other arithmetic, gather_dp(): jnp.stack([jnp.where(low, current, other), jnp.where(low, other, current)])  19.9 us
  transfers between devices with their start and end apart: 70, of which 32 were waited for; matrix products, arithmetic and copies ran while one was open for 16% of the time, Pallas kernels for 27%

profile of v1, /device:TPU:0, one launch (start us, length us, event | category | flops | bytes accessed | tf_op | source)
XLA Modules:
  0.0 558.3 jit_solution(2311778967189987686)
XLA Ops:
  28.3 20.0 %collective-permute-done.1 = bf16[2,104,256]{2,1,0:T(8,128)(2,1)S(1)} collective-permute-done((bf16[2,104,256]{2,1,0:T(8,128)(2,1)S(1)}, bf16[2,104,256]{2,1,0:T(8,128)(2,1)S(1)}, u32[]{:S(2)}, u32[]{:S(2)}) %collective-permute-start.1) | collective-permute-done | bytes 106528 | tf_op jit(solution)/shard_map/ppermute | solution.py:31
  48.3 11.6 %collective-permute-done.6 = bf16[2,104,256]{2,1,0:T(8,128)(2,1)S(1)} collective-permute-done((bf16[2,104,256]{2,1,0:T(8,128)(2,1)S(1)}, bf16[2,104,256]{2,1,0:T(8,128)(2,1)S(1)}, u32[]{:S(2)}, u32[]{:S(2)}) %collective-permute-start.6) | collective-permute-done | bytes 106528 | tf_op jit(solution)/shard_map/ppermute | solution.py:31
  63.7 8.0 %collective-permute-done.7 = bf16[2,2,104,256]{3,2,1,0:T(8,128)(2,1)S(1)} collective-permute-done((bf16[2,2,104,256]{3,2,1,0:T(8,128)(2,1)S(1)}, bf16[2,2,104,256]{3,2,1,0:T(8,128)(2,1)S(1)}, u32[]{:S(2)}, u32[]{:S(2)}) %collective-permute-start.7) | collective-permute-done | bytes 213024 | tf_op jit(solution)/shard_map/ppermute | solution.py:31
  73.6 8.8 %collective-permute-done.8 = bf16[2,2,2,104,256]{4,3,2,1,0:T(8,128)(2,1)S(1)} collective-permute-done((bf16[2,2,2,104,256]{4,3,2,1,0:T(8,128)(2,1)S(1)}, bf16[2,2,2,104,256]{4,3,2,1,0:T(8,128)(2,1)S(1)}, u32[]{:S(2)}, u32[]{:S(2)}) %collective-permute-start.8) | collective-permute-done | bytes 426016 | tf_op jit(solution)/shard_map/ppermute | solution.py:31
  85.4 10.5 %collective-permute-done.3 = bf16[2,2,2,104,256]{4,3,2,1,0:T(8,128)(2,1)} collective-permute-done((bf16[2,2,2,104,256]{4,3,2,1,0:T(8,128)(2,1)S(1)}, bf16[2,2,2,104,256]{4,3,2,1,0:T(8,128)(2,1)}, u32[]{:S(2)}, u32[]{:S(2)}) %collective-permute-start.3) | collective-permute-done | bytes 426016 | tf_op jit(solution)/shard_map/ppermute | solution.py:31
  118.7 26.8 %attention_forward.1 = (bf16[512,768]{1,0:T(8,128)(2,1)}, bf16[512,2304]{1,0:T(8,128)(2,1)}, bf16[512,768]{1,0:T(8,128)(2,1)}, f32[512,768]{1,0:T(8,128)}, bf16[...) custom-call(bf16[512,768]{1,0:T(8,128)(2,1)} %x_ref.3, bf16[2304,768]{1,0:T(8,128)(2,1)} %bitcast.378, ...), custom_call_target="tpu_custom_call" | custom-call | tf_op jit(solution)/shard_map/attention_forward/pallas_call | solution.py:129
  145.6 6.1 %all-to-all-start.3 = ((bf16[8,112,768]{2,1,0:T(8,128)(2,1)}), bf16[8,112,768]{2,1,0:T(8,128)(2,1)}, u32[]{:S(2)}, u32[]{:S(2)}) async-start(bf16[8,112,768]{2,1,0:T(8,128)(2,1)} %bitcast.414), calls=%async_computation.3 | async-start | bytes 2752512 | tf_op jit(solution)/shard_map/all_to_all | solution.py:530
  167.4 21.6 %collective-permute-done.17 = bf16[768,768]{1,0:T(8,128)(2,1)S(1)} collective-permute-done((bf16[768,768]{1,0:T(8,128)(2,1)S(1)}, bf16[768,768]{1,0:T(8,128)(2,1)S(1)}, u32[]{:S(2)}, u32[]{:S(2)}) %collective-permute-start.17) | collective-permute-done | bytes 1179680 | tf_op jit(solution)/shard_map/ppermute | solution.py:31
  191.0 6.2 %all-to-all-start = ((bf16[8,112,768]{2,1,0:T(8,128)(2,1)}), bf16[8,112,768]{2,1,0:T(8,128)(2,1)}, u32[]{:S(2)}, u32[]{:S(2)}) async-start(bf16[8,112,768]{2,1,0:T(8,128)(2,1)} %bitcast.412), calls=%async_computation | async-start | bytes 2752512 | tf_op jit(solution)/shard_map/all_to_all | solution.py:530
  197.3 16.8 %collective-permute-done.15 = bf16[192,3072]{1,0:T(8,128)(2,1)} collective-permute-done((bf16[192,3072]{1,0:T(8,128)(2,1)}, bf16[192,3072]{1,0:T(8,128)(2,1)}, u32[]{:S(2)}, u32[]{:S(2)}) %collective-permute-start.15) | collective-permute-done | bytes 1179680 | tf_op jit(solution)/shard_map/ppermute | solution.py:31
  228.6 38.1 %expert_new.1 = (bf16[896,768]{1,0:T(8,128)(2,1)}, bf16[896,768]{1,0:T(8,128)(2,1)}, f32[128,768]{1,0:T(8,128)}, bf16[768,3072]{1,0:T(8,128)(2,1)}, bf16[3072,768]{1,0:T(8,128)(2,1)}) custom-call(f32[8,128]{1,0:T(8,128)} %get-tuple-element.168.mine_ref, bf16[896,768]{1,0:T(8,128)(2,1)} %bitcast.67.rows_ref, bf16[896,768]{1,0:T(8,128)(2,1)} %bitcast.402, ...), custom_call_target="tpu_custom_call" | custom-call | tf_op jit(solution)/shard_map/expert_new/pallas_call | solution.py:450
  266.8 6.4 %all-to-all-start.7 = ((bf16[8,112,768]{2,1,0:T(8,128)(2,1)}), bf16[8,112,768]{2,1,0:T(8,128)(2,1)}, u32[]{:S(2)}, u32[]{:S(2)}) async-start(bf16[8,112,768]{2,1,0:T(8,128)(2,1)} %bitcast.415), calls=%async_computation.7 | async-start | bytes 2752512 | tf_op jit(solution)/shard_map/all_to_all | solution.py:530
  283.0 26.8 %expert_old.1 = (bf16[896,768]{1,0:T(8,128)(2,1)}, bf16[896,768]{1,0:T(8,128)(2,1)}, f32[128,768]{1,0:T(8,128)}) custom-call(f32[8,128]{1,0:T(8,128)} %get-tuple-element.169.mine_ref, bf16[896,768]{1,0:T(8,128)(2,1)} %bitcast.46.rows_ref, bf16[896,768]{1,0:T(8,128)(2,1)} %bitcast.48.grads_ref, bf16[768,128]{1,0:T(8,128)(2,1)} %pad.27.router_ref, ...), custom_call_target="tpu_custom_call" | custom-call | tf_op jit(solution)/shard_map/expert_old/pallas_call | solution.py:450
  309.9 6.0 %all-to-all-start.6 = ((bf16[8,112,768]{2,1,0:T(8,128)(2,1)}), bf16[8,112,768]{2,1,0:T(8,128)(2,1)S(1)}, u32[]{:S(2)}, u32[]{:S(2)}) async-start(bf16[8,112,768]{2,1,0:T(8,128)(2,1)} %bitcast.413), calls=%async_computation.6 | async-start | bytes 2752512 | tf_op jit(solution)/shard_map/all_to_all | solution.py:530
  322.9 25.2 %all-to-all-done.6 = bf16[8,112,768]{2,1,0:T(8,128)(2,1)S(1)} async-done(((bf16[8,112,768]{2,1,0:T(8,128)(2,1)}), bf16[8,112,768]{2,1,0:T(8,128)(2,1)S(1)}, u32[]{:S(2)}, u32[]{:S(2)}) %all-to-all-start.6) | async-done | bytes 1376288 | tf_op jit(solution)/shard_map/all_to_all | solution.py:530
  365.1 8.5 %branch_backward.1 = (f32[512,768]{1,0:T(8,128)}, bf16[512,768]{1,0:T(8,128)(2,1)}, bf16[768,256]{1,0:T(8,128)(2,1)}, bf16[768,256]{1,0:T(8,128)(2,1)}, bf16[768,256]{1,0:T(8,128)(2,1)}, /*index=5*/f32[8,768]{1,0:T(8,128)}) custom-call(bf16[896,768]{1,0:T(8,128)(2,1)} %bitcast.400, bf16[896,768]{1,0:T(8,128)(2,1)} %bitcast.89.new_ref, s32[512,2]{1,0:T(8,128)} %copy-done.17, ...), custom_call_target="tpu_custom_call" | custom-call | tf_op jit(solution)/shard_map/branch_backward/pallas_call | solution.py:129
  373.6 32.5 %attention_backward.1 = (bf16[512,2304]{1,0:T(8,128)(2,1)}, bf16[2304,256]{1,0:T(8,128)(2,1)}, bf16[2304,256]{1,0:T(8,128)(2,1)}, bf16[2304,256]{1,0:T(8,128)(2,1)}) custom-call(bf16[512,2304]{1,0:T(8,128)(2,1)} %get-tuple-element.54.proj_ref, bf16[512,768]{1,0:T(8,128)(2,1)} %get-tuple-element.58.gctx_ref, bf16[512,768]{1,0:T(8,128)(2,1)} %get-tuple-element.59.normed_ref), custom_call_target="tpu_custom_call" | custom-call | tf_op jit(solution)/shard_map/attention_backward/pallas_call | solution.py:129
  406.1 7.1 %input_backward.1 = (f32[512,768]{1,0:T(8,128)}, f32[8,768]{1,0:T(8,128)}) custom-call(bf16[512,2304]{1,0:T(8,128)(2,1)} %get-tuple-element.60.gproj_ref, bf16[2304,768]{1,0:T(8,128)(2,1)} %bitcast.379, bf16[512,768]{1,0:T(8,128)(2,1)} %x_ref.3, f32[8,768]{1,0:T(8,128)} %pad_convert_fusion.vec_ref, f32[512,768]{1,0:T(8,128)} %get-tuple-element.61.gmid_ref), custom_call_target="tpu_custom_call" | custom-call | tf_op jit(solution)/shard_map/input_backward/pallas_call | solution.py:129
  415.6 6.0 %all-to-all-start.2 = ((bf16[8,112,768]{2,1,0:T(8,128)(2,1)}), bf16[8,112,768]{2,1,0:T(8,128)(2,1)S(1)}, u32[]{:S(2)}, u32[]{:S(2)}) async-start(bf16[8,112,768]{2,1,0:T(8,128)(2,1)} %bitcast.410), calls=%async_computation.2 | async-start | bytes 2752512 | tf_op jit(solution)/shard_map/all_to_all | solution.py:530
  428.4 5.2 collective-permute-done.54
  435.6 10.5 %collective-permute-done.55 = bf16[2,2,1,480]{3,1,0,2:T(2,128)(2,1)S(1)} collective-permute-done((bf16[2,2,1,480]{3,1,0,2:T(2,128)(2,1)S(1)}, bf16[2,2,1,480]{3,1,0,2:T(2,128)(2,1)S(1)}, u32[]{:S(2)}, u32[]{:S(2)}) %collective-permute-start.55) | collective-permute-done | bytes 3872 | tf_op jit(solution)/shard_map/ppermute | solution.py:31
  449.5 5.7 %collective-permute-done.56 = bf16[2,1,480]{2,0,1:T(2,128)(2,1)S(1)} collective-permute-done((bf16[2,1,480]{2,0,1:T(2,128)(2,1)S(1)}, bf16[2,1,480]{2,0,1:T(2,128)(2,1)S(1)}, u32[]{:S(2)}, u32[]{:S(2)}) %collective-permute-start.56) | collective-permute-done | bytes 1952 | tf_op jit(solution)/shard_map/ppermute | solution.py:31
  461.0 5.1 mixed_output.1
  526.7 6.0 %collective-permute-done.24 = bf16[2,2,2,72,256]{4,3,0,1,2:T(8,128)(2,1)S(1)} collective-permute-done((bf16[2,2,2,72,256]{4,3,0,1,2:T(8,128)(2,1)S(1)}, bf16[2,2,2,72,256]{4,3,0,1,2:T(8,128)(2,1)S(1)}, u32[]{:S(2)}, u32[]{:S(2)}) %collective-permute-start.24) | collective-permute-done | bytes 294944 | tf_op jit(solution)/shard_map/ppermute | solution.py:31
  (398 shorter events, 230.2 us)
Async XLA Ops:
  19.6 78.3 %all-to-all-start.4 = ((bf16[8,112,768]{2,1,0:T(8,128)(2,1)}), bf16[8,112,768]{2,1,0:T(8,128)(2,1)S(1)}, u32[]{:S(2)}, u32[]{:S(2)}) async-start(bf16[8,112,768]{2,1,0:T(8,128)(2,1)} %bitcast.409), calls=%async_computation.4 | async-start | bytes 2752512 | tf_op jit(solution)/shard_map/all_to_all | solution.py:530
  25.3 34.7 %collective-permute-start.6 = (bf16[2,104,256]{2,1,0:T(8,128)(2,1)S(1)}, bf16[2,104,256]{2,1,0:T(8,128)(2,1)S(1)}, u32[]{:S(2)}, u32[]{:S(2)}) collective-permute-start(bf16[2,104,256]{2,1,0:T(8,128)(2,1)S(1)} %pad_maximum_fusion.17), channel_id=1, source_target_pairs={{0,4},{1,5},{2,6},{3,7},{4,0},{5,1},{6,2},{7,3},{8,12},{9,13},{10,... | collective-permute-start | bytes 319496 | tf_op jit(solution)/shard_map/ppermute | solution.py:31
  97.9 47.7 %all-to-all-start.1 = ((bf16[8,112,768]{2,1,0:T(8,128)(2,1)}), bf16[8,112,768]{2,1,0:T(8,128)(2,1)}, u32[]{:S(2)}, u32[]{:S(2)}) async-start(bf16[8,112,768]{2,1,0:T(8,128)(2,1)} %bitcast.408), calls=%async_computation.1 | async-start | bytes 2752512 | tf_op jit(solution)/shard_map/all_to_all | solution.py:530
  109.5 45.8 %collective-permute-start.21 = (bf16[768,768]{1,0:T(8,128)(2,1)}, bf16[768,768]{1,0:T(8,128)(2,1)}, u32[]{:S(2)}, u32[]{:S(2)}) collective-permute-start(bf16[768,768]{1,0:T(8,128)(2,1)} %bitcast.77), channel_id=1, source_target_pairs={{0,16},{8,24},{16,0},{24,8},{1,17},{9,25},{17,1},{25,9},{2,18},{10... | collective-permute-start | bytes 3538952 | tf_op jit(solution)/shard_map/ppermute | solution.py:31
  110.0 53.8 %collective-permute-start.19 = (bf16[192,3072]{1,0:T(8,128)(2,1)}, bf16[192,3072]{1,0:T(8,128)(2,1)}, u32[]{:S(2)}, u32[]{:S(2)}) collective-permute-start(bf16[192,3072]{1,0:T(8,128)(2,1)} %bitcast.416), channel_id=1, source_target_pairs={{0,16},{8,24},{16,0},{24,8},{1,17},{9,25},{17,1},{25,9},{2,18},{10... | collective-permute-start | bytes 3538952 | tf_op jit(solution)/shard_map/ppermute | solution.py:31
  145.6 45.4 %all-to-all-start.3 = ((bf16[8,112,768]{2,1,0:T(8,128)(2,1)}), bf16[8,112,768]{2,1,0:T(8,128)(2,1)}, u32[]{:S(2)}, u32[]{:S(2)}) async-start(bf16[8,112,768]{2,1,0:T(8,128)(2,1)} %bitcast.414), calls=%async_computation.3 | async-start | bytes 2752512 | tf_op jit(solution)/shard_map/all_to_all | solution.py:530
  153.3 35.7 %collective-permute-start.17 = (bf16[768,768]{1,0:T(8,128)(2,1)S(1)}, bf16[768,768]{1,0:T(8,128)(2,1)S(1)}, u32[]{:S(2)}, u32[]{:S(2)}) collective-permute-start(bf16[768,768]{1,0:T(8,128)(2,1)S(1)} %bitcast.417), channel_id=1, source_target_pairs={{0,16},{8,24},{16,0},{24,8},{1,17},{9,25},{17,1},{25,9},{2,18},{10... | collective-permute-start | bytes 3538952 | tf_op jit(solution)/shard_map/ppermute | solution.py:31
  153.8 60.2 %collective-permute-start.15 = (bf16[192,3072]{1,0:T(8,128)(2,1)}, bf16[192,3072]{1,0:T(8,128)(2,1)}, u32[]{:S(2)}, u32[]{:S(2)}) collective-permute-start(bf16[192,3072]{1,0:T(8,128)(2,1)} %bitcast.50), channel_id=1, source_target_pairs={{0,16},{8,24},{16,0},{24,8},{1,17},{9,25},{17,1},{25,9},{2,18},{10... | collective-permute-start | bytes 3538952 | tf_op jit(solution)/shard_map/ppermute | solution.py:31
  159.3 58.4 %collective-permute-start.22 = (bf16[2,768,768]{2,1,0:T(8,128)(2,1)}, bf16[2,768,768]{2,1,0:T(8,128)(2,1)}, u32[]{:S(2)}, u32[]{:S(2)}) collective-permute-start(bf16[2,768,768]{2,1,0:T(8,128)(2,1)} %pad_maximum_fusion.4), channel_id=1, source_target_pairs={{0,8},{8,0},{16,24},{24,16},{1,9},{9,1},{17,25},{25,17},{2,10},{10... | collective-permute-start | bytes 7077896 | tf_op jit(solution)/shard_map/ppermute | solution.py:31
  167.4 56.2 %collective-permute-start.20 = (bf16[2,192,3072]{2,1,0:T(8,128)(2,1)}, bf16[2,192,3072]{2,1,0:T(8,128)(2,1)}, u32[]{:S(2)}, u32[]{:S(2)}) collective-permute-start(bf16[2,192,3072]{2,1,0:T(8,128)(2,1)} %pad_maximum_fusion.3), channel_id=1, source_target_pairs={{0,8},{8,0},{16,24},{24,16},{1,9},{9,1},{17,25},{25,17},{2,10},{10... | collective-permute-start | bytes 7077896 | tf_op jit(solution)/shard_map/ppermute | solution.py:31
  191.0 82.2 %collective-permute-start.18 = (bf16[2,768,768]{2,1,0:T(8,128)(2,1)}, bf16[2,768,768]{2,1,0:T(8,128)(2,1)}, u32[]{:S(2)}, u32[]{:S(2)}) collective-permute-start(bf16[2,768,768]{2,1,0:T(8,128)(2,1)} %pad_maximum_fusion.2), channel_id=1, source_target_pairs={{0,8},{8,0},{16,24},{24,16},{1,9},{9,1},{17,25},{25,17},{2,10},{10... | collective-permute-start | bytes 7077896 | tf_op jit(solution)/shard_map/ppermute | solution.py:31
  191.0 75.7 %all-to-all-start = ((bf16[8,112,768]{2,1,0:T(8,128)(2,1)}), bf16[8,112,768]{2,1,0:T(8,128)(2,1)}, u32[]{:S(2)}, u32[]{:S(2)}) async-start(bf16[8,112,768]{2,1,0:T(8,128)(2,1)} %bitcast.412), calls=%async_computation | async-start | bytes 2752512 | tf_op jit(solution)/shard_map/all_to_all | solution.py:530
  217.7 60.4 %collective-permute-start.16 = (bf16[2,192,3072]{2,1,0:T(8,128)(2,1)}, bf16[2,192,3072]{2,1,0:T(8,128)(2,1)}, u32[]{:S(2)}, u32[]{:S(2)}) collective-permute-start(bf16[2,192,3072]{2,1,0:T(8,128)(2,1)} %pad_maximum_fusion.1), channel_id=1, source_target_pairs={{0,8},{8,0},{16,24},{24,16},{1,9},{9,1},{17,25},{25,17},{2,10},{10... | collective-permute-start | bytes 7077896 | tf_op jit(solution)/shard_map/ppermute | solution.py:31
  266.8 43.1 %all-to-all-start.7 = ((bf16[8,112,768]{2,1,0:T(8,128)(2,1)}), bf16[8,112,768]{2,1,0:T(8,128)(2,1)}, u32[]{:S(2)}, u32[]{:S(2)}) async-start(bf16[8,112,768]{2,1,0:T(8,128)(2,1)} %bitcast.415), calls=%async_computation.7 | async-start | bytes 2752512 | tf_op jit(solution)/shard_map/all_to_all | solution.py:530
  309.9 38.2 %all-to-all-start.6 = ((bf16[8,112,768]{2,1,0:T(8,128)(2,1)}), bf16[8,112,768]{2,1,0:T(8,128)(2,1)S(1)}, u32[]{:S(2)}, u32[]{:S(2)}) async-start(bf16[8,112,768]{2,1,0:T(8,128)(2,1)} %bitcast.413), calls=%async_computation.6 | async-start | bytes 2752512 | tf_op jit(solution)/shard_map/all_to_all | solution.py:530
  322.4 35.5 %collective-permute-start.58 = (bf16[2,192,3072]{2,1,0:T(8,128)(2,1)}, bf16[2,192,3072]{2,1,0:T(8,128)(2,1)}, u32[]{:S(2)}, u32[]{:S(2)}) collective-permute-start(bf16[2,192,3072]{2,1,0:T(8,128)(2,1)} %dynamic-slice_bitcast_fusion.1), channel_id=1, source_target_pairs={{0,8},{8,0},{16,24},{24,16},{1,9},{9,1},{17,25},{25,17},{2,10},{10... | collective-permute-start | bytes 7077896 | tf_op jit(solution)/shard_map/ppermute | solution.py:31
  348.1 67.5 %all-to-all-start.5 = ((bf16[8,112,768]{2,1,0:T(8,128)(2,1)}), bf16[8,112,768]{2,1,0:T(8,128)(2,1)S(1)}, u32[]{:S(2)}, u32[]{:S(2)}) async-start(bf16[8,112,768]{2,1,0:T(8,128)(2,1)} %bitcast.411), calls=%async_computation.5 | async-start | bytes 2752512 | tf_op jit(solution)/shard_map/all_to_all | solution.py:530
  357.3 197.0 %collective-permute-start.61 = (bf16[768,768]{1,0:T(8,128)(2,1)}, bf16[768,768]{1,0:T(8,128)(2,1)}, u32[]{:S(2)}, u32[]{:S(2)}) collective-permute-start(bf16[768,768]{1,0:T(8,128)(2,1)} %fusion.3), channel_id=1, source_target_pairs={{0,16},{8,24},{16,0},{24,8},{1,17},{9,25},{17,1},{25,9},{2,18},{10... | collective-permute-start | bytes 3538952 | tf_op jit(solution)/shard_map/ppermute | solution.py:31
  363.7 187.5 %collective-permute-start.59 = (bf16[192,3072]{1,0:T(8,128)(2,1)}, bf16[192,3072]{1,0:T(8,128)(2,1)}, u32[]{:S(2)}, u32[]{:S(2)}) collective-permute-start(bf16[192,3072]{1,0:T(8,128)(2,1)} %fusion.2), channel_id=1, source_target_pairs={{0,16},{8,24},{16,0},{24,8},{1,17},{9,25},{17,1},{25,9},{2,18},{10... | collective-permute-start | bytes 3538952 | tf_op jit(solution)/shard_map/ppermute | solution.py:31
  415.6 44.3 %all-to-all-start.2 = ((bf16[8,112,768]{2,1,0:T(8,128)(2,1)}), bf16[8,112,768]{2,1,0:T(8,128)(2,1)S(1)}, u32[]{:S(2)}, u32[]{:S(2)}) async-start(bf16[8,112,768]{2,1,0:T(8,128)(2,1)} %bitcast.410), calls=%async_computation.2 | async-start | bytes 2752512 | tf_op jit(solution)/shard_map/all_to_all | solution.py:530
  423.6 43.9 %collective-permute-start.38 = (bf16[2,2,2,2,24,256]{5,4,1,2,3,0:T(8,128)(2,1)}, bf16[2,2,2,2,24,256]{5,4,1,2,3,0:T(8,128)(2,1)}, u32[]{:S(2)}, u32[]{:S(2)}) collective-permute-start(bf16[2,2,2,2,24,256]{5,4,1,2,3,0:T(8,128)(2,1)} %bitcast.373), channel_id=1, source_target_pairs={{0,8},{8,0},{16,24},{24,16},{1,9},{9,1},{17,25},{25,17},{2,10},{10... | collective-permute-start | bytes 589832 | tf_op jit(solution)/shard_map/ppermute | solution.py:31
  424.5 44.5 %collective-permute-start.43 = (bf16[2,2,2,2,24,256]{5,4,0,1,2,3:T(8,128)(2,1)}, bf16[2,2,2,2,24,256]{5,4,0,1,2,3:T(8,128)(2,1)}, u32[]{:S(2)}, u32[]{:S(2)}) collective-permute-start(bf16[2,2,2,2,24,256]{5,4,0,1,2,3:T(8,128)(2,1)} %bitcast.372), channel_id=1, source_target_pairs={{0,8},{8,0},{16,24},{24,16},{1,9},{9,1},{17,25},{25,17},{2,10},{10... | collective-permute-start | bytes 589832 | tf_op jit(solution)/shard_map/ppermute | solution.py:31
  467.5 55.5 %collective-permute-start.23 = (bf16[2,2,2,2,72,256]{5,4,1,2,3,0:T(8,128)(2,1)}, bf16[2,2,2,2,72,256]{5,4,1,2,3,0:T(8,128)(2,1)S(1)}, u32[]{:S(2)}, u32[]{:S(2)}) collective-permute-start(bf16[2,2,2,2,72,256]{5,4,1,2,3,0:T(8,128)(2,1)} %bitcast.423), channel_id=1, source_target_pairs={{0,8},{8,0},{16,24},{24,16},{1,9},{9,1},{17,25},{25,17},{2,10},{10... | collective-permute-start | bytes 1769480 | tf_op jit(solution)/shard_map/ppermute | solution.py:31
  469.0 55.6 %collective-permute-start.28 = (bf16[2,2,2,2,72,256]{5,4,0,1,2,3:T(8,128)(2,1)}, bf16[2,2,2,2,72,256]{5,4,0,1,2,3:T(8,128)(2,1)S(1)}, u32[]{:S(2)}, u32[]{:S(2)}) collective-permute-start(bf16[2,2,2,2,72,256]{5,4,0,1,2,3:T(8,128)(2,1)} %bitcast.422), channel_id=1, source_target_pairs={{0,8},{8,0},{16,24},{24,16},{1,9},{9,1},{17,25},{25,17},{2,10},{10... | collective-permute-start | bytes 1769480 | tf_op jit(solution)/shard_map/ppermute | solution.py:31
  (86 other events, 780.0 us)

commit v2 on v1

v2 whole, which is shorter than its diff:
```python
import functools

import jax
import jax.numpy as jnp
from jax import lax
from jax.experimental import pallas as pl
from jax.experimental.pallas import tpu as pltpu
from jax.sharding import PartitionSpec as P

HEADS = 12
HEAD_DIM = 64
BF = jnp.bfloat16
F32 = jnp.float32


def mm(a, b, dims, out=F32):
    return lax.dot_general(a, b, (dims, ((), ())), preferred_element_type=F32).astype(out)


def powers(count):
    found = []
    bit = 1
    while bit < count:
        found.append(bit)
        bit *= 2
    return found


def swap(values, axis, bit):
    count = lax.axis_size(axis)
    return lax.ppermute(values, axis, [(i, i ^ bit) for i in range(count)])


def my_bit(axis, bit):
    return (lax.axis_index(axis) // bit) % 2


def canonical():
    return [("dp", b) for b in reversed(powers(lax.axis_size("dp")))] + [
        ("expert", b) for b in reversed(powers(lax.axis_size("expert")))
    ]


def orders():
    dp_bits = powers(lax.axis_size("dp"))
    expert_bits = powers(lax.axis_size("expert"))
    core = [("dp", dp_bits[0])]
    xs = [("dp", b) for b in reversed(dp_bits[1:])]
    ys = [("expert", expert_bits[0])]
    zs = [("expert", b) for b in reversed(expert_bits[1:])]
    gathering = (zs + ys + xs + core, xs + zs + ys + core, ys + xs + zs + core)
    near = zs[::-1]
    summing = (xs + ys + near, ys + near + xs, near + xs + ys, near + ys + xs)
    return gathering, summing


def gather_steps(state, order):
    current, lead = state
    lead = list(lead)
    for axis, bit in order:
        other = swap(current, axis, bit)
        low = my_bit(axis, bit) == 0
        current = jnp.stack([jnp.where(low, current, other), jnp.where(low, other, current)])
        lead.insert(0, (axis, bit))
    return current, lead


def gather_finish(state):
    current, lead = state
    tail = current.shape[len(lead) :]
    perm = [lead.index(w) for w in canonical()]
    current = current.transpose(perm + list(range(len(lead), current.ndim)))
    return current.reshape((-1,) + tail)


def after(values, *earlier):
    if not earlier:
        return values
    return lax.optimization_barrier((values, earlier))[0]


def scatter_steps(state, order):
    current, lead = state
    lead = list(lead)
    for axis, bit in order:
        at = lead.index((axis, bit))
        mine = my_bit(axis, bit)
        keep = lax.dynamic_index_in_dim(current, mine, at, keepdims=False)
        send = lax.dynamic_index_in_dim(current, 1 - mine, at, keepdims=False)
        got = swap(send.astype(BF), axis, bit)
        current = keep.astype(F32) + got.astype(F32)
        lead.pop(at)
    return current, lead


def dp_pieces(shard, first, second):
    bits = powers(lax.axis_size("dp"))
    found = {0: shard, bits[0]: swap(after(shard, *first), "dp", bits[0])}
    far = {}
    for bit in bits[1:]:
        for away, piece in [(0, after(shard, *first)), *far.items()]:
            far[away ^ bit] = swap(piece, "dp", bit)
    for away, piece in far.items():
        found[away] = piece
        found[away ^ bits[0]] = swap(after(piece, *second), "dp", bits[0])
    return [found[away] for away in range(len(found))], far


def scatter_dp(keep, send):
    bits = powers(lax.axis_size("dp"))
    total = keep.astype(F32) + swap(send, "dp", bits[0]).astype(F32)
    order = [("dp", b) for b in bits[1:]]
    total = total.reshape([2] * len(order) + list(total.shape[1:]))
    return scatter_steps((total, order[::-1]), order)[0]


LIMIT = 56 * 1024 * 1024
QUERY_BLOCK = 128
SCALE = HEAD_DIM ** (-0.5)


def dot(a, b, over_a, over_b):
    return lax.dot_general(
        a, b, (((over_a,), (over_b,)), ((), ())), preferred_element_type=F32
    )


def dot_parts(values, parts):
    width = parts[0].shape[1]
    total = None
    for at, part in enumerate(parts):
        term = dot(values[:, at * width : (at + 1) * width], part, 1, 1)
        total = term if total is None else total + term
    return total


def whole(array):
    return jax.ShapeDtypeStruct(array[0], array[1])


def cost(micros):
    return pl.CostEstimate(flops=int(micros * 0.25e9), bytes_accessed=0, transcendentals=0)


def plain_call(body, outs, scratch, name, micros, *args):
    space = pl.BlockSpec(memory_space=pltpu.VMEM)
    return pl.pallas_call(
        body,
        out_shape=[whole(o) for o in outs],
        in_specs=[space] * len(args),
        out_specs=[space] * len(outs),
        scratch_shapes=scratch,
        compiler_params=pltpu.CompilerParams(vmem_limit_bytes=LIMIT),
        cost_estimate=cost(micros),
        name=name,
    )(*args)


def norm_parts(values):
    centre = values - jnp.mean(values, axis=-1, keepdims=True)
    spread = jnp.mean(centre * centre, axis=-1, keepdims=True)
    scale = lax.rsqrt(spread + 1e-05)
    return centre * scale, scale


def norm_back(values, gain, grad):
    normal, scale = norm_parts(values)
    scaled = grad * gain
    back = scale * (
        scaled
        - jnp.mean(scaled, axis=-1, keepdims=True)
        - normal * jnp.mean(scaled * normal, axis=-1, keepdims=True)
    )
    return back, jnp.sum(grad * normal, axis=0, keepdims=True), jnp.sum(grad, axis=0, keepdims=True)


def place_rows(target_ref, values, first, count):
    tokens = values.shape[0]
    at = lax.broadcasted_iota(jnp.int32, (count, tokens), 0) + first
    hit = (at == target_ref[0:1, :]) | (at == target_ref[1:2, :])
    return dot(hit.astype(F32).astype(BF), values, 1, 0).astype(BF)


def place_kernel(target_ref, values_ref, slots_ref):
    values = values_ref[...]
    part = slots_ref.shape[0] // 4
    for at in range(4):
        slots_ref[at * part : (at + 1) * part, :] = place_rows(
            target_ref, values, at * part, part
        )


def take_rows(target_ref, slots_refs, tokens):
    total = None
    first = 0
    for ref in slots_refs:
        count = ref.shape[0]
        at = lax.broadcasted_iota(jnp.int32, (tokens, count), 1) + first
        hit = (at == target_ref[:, 0:1]) | (at == target_ref[:, 1:2])
        part = dot(hit.astype(F32).astype(BF), ref[...], 1, 0)
        total = part if total is None else total + part
        first += count
    return total


def causal(size):
    rowpos = lax.broadcasted_iota(jnp.int32, (size, size), 0)
    colpos = lax.broadcasted_iota(jnp.int32, (size, size), 1)
    return rowpos >= colpos


def head_lanes(block, which):
    lane = lax.broadcasted_iota(jnp.int32, block.shape, 1)
    keep = (lane < HEAD_DIM) if which == 0 else (lane >= HEAD_DIM)
    return jnp.where(keep, block, jnp.zeros_like(block))


def block_softmax(query, keys, seen):
    size = query.shape[0]
    before = keys.shape[0] - size
    own = dot(query, keys[before:], 1, 1)
    own = jnp.where(seen, own, -1e30)
    top = jnp.max(own, axis=-1, keepdims=True)
    if before:
        past = dot(query, keys[:before], 1, 1)
        top = jnp.maximum(top, jnp.max(past, axis=-1, keepdims=True))
        past = jnp.exp(past - top)
    own = jnp.exp(own - top)
    total = jnp.sum(own, axis=-1, keepdims=True)
    if before:
        total = total + jnp.sum(past, axis=-1, keepdims=True)
    inverse = 1.0 / total
    own = own * inverse
    return (past * inverse, own) if before else (own,)


def pair_columns(pair, part, width):
    return pl.ds(pl.multiple_of(part * width + pair * 2 * HEAD_DIM, 2 * HEAD_DIM), 2 * HEAD_DIM)


def forward_kernel(
    x_ref,
    in0_ref,
    in1_ref,
    in2_ref,
    out0_ref,
    out1_ref,
    out2_ref,
    vec_ref,
    target_ref,
    normed_ref,
    proj_ref,
    context_ref,
    middle_ref,
    old_ref,
    new_ref,
):
    length, width = x_ref.shape
    x = x_ref[...].astype(F32)
    normal, _ = norm_parts(x)
    normed = (normal * vec_ref[0:1, :] + vec_ref[1:2, :]).astype(BF)
    normed_ref[...] = normed
    for part in range(3):
        cols = slice(part * width, (part + 1) * width)
        proj_ref[:, cols] = dot_parts(
            normed, [ref[cols, :] for ref in (in0_ref, in1_ref, in2_ref)]
        ).astype(BF)
    size = min(QUERY_BLOCK, length)
    seen = causal(size)

    def one_pair(pair, carry):
        q_at, k_at, v_at = (pair_columns(pair, part, width) for part in range(3))
        for block in range(length // size):
            rows = slice(block * size, (block + 1) * size)
            upto = (block + 1) * size
            query = proj_ref[rows, q_at] * BF(SCALE)
            keys = proj_ref[0:upto, k_at]
            values = proj_ref[0:upto, v_at]
            outs = []
            for which in range(2):
                probs = block_softmax(head_lanes(query, which), keys, seen)
                probs = [p.astype(BF) for p in probs]
                out = dot(probs[-1], values[upto - size :], 1, 0)
                if len(probs) > 1:
                    out = out + dot(probs[0], values[: upto - size], 1, 0)
                outs.append(out)
            lane = lax.broadcasted_iota(jnp.int32, outs[0].shape, 1)
            context_ref[rows, pair_columns(pair, 0, width)] = jnp.where(
                lane < HEAD_DIM, outs[0], outs[1]
            ).astype(BF)
        return carry

    lax.fori_loop(0, HEADS // 2, one_pair, 0)
    middle = x + dot_parts(context_ref[...], [ref[...] for ref in (out0_ref, out1_ref, out2_ref)])
    middle_ref[...] = middle
    normal, _ = norm_parts(middle)
    normed_two = (normal * vec_ref[2:3, :] + vec_ref[3:4, :]).astype(BF)
    count = old_ref.shape[0]
    half = count // 2
    for at, ref in ((0, old_ref), (count, new_ref)):
        for part in range(2):
            ref[part * half : (part + 1) * half, :] = place_rows(
                target_ref, normed_two, at + part * half, half
            )


def branch_kernel(
    old_ref,
    new_ref,
    target_ref,
    cot_ref,
    middle_ref,
    context_ref,
    out0_ref,
    out1_ref,
    out2_ref,
    vec_ref,
    gmid_ref,
    gctx_ref,
    outgrad_ref,
    sums_ref,
):
    length, width = cot_ref.shape
    grad = take_rows(target_ref, (old_ref, new_ref), length)
    back, gain_sum, bias_sum = norm_back(middle_ref[...], vec_ref[2:3, :], grad)
    gmid = back + cot_ref[...].astype(F32)
    gmid_ref[...] = gmid
    sums_ref[...] = jnp.concatenate([gain_sum, bias_sum, jnp.zeros((6, width), F32)], axis=0)
    branch = gmid.astype(BF)
    third = width // 3
    for part, ref in enumerate((out0_ref, out1_ref, out2_ref)):
        gctx_ref[:, part * third : (part + 1) * third] = dot(branch, ref[...], 1, 0).astype(BF)
    outgrad_ref[...] = dot(branch, context_ref[...], 0, 0).astype(BF)


def attention_back_kernel(
    place_ref,
    proj_ref,
    gctx_ref,
    normed_ref,
    gproj_ref,
    keep0_ref,
    keep1_ref,
    keep2_ref,
    send0_ref,
    send1_ref,
    send2_ref,
    gk_acc,
    gv_acc,
):
    length, width = gctx_ref.shape
    size = min(QUERY_BLOCK, length)
    seen = causal(size)

    def one_pair(pair, carry):
        q_at, k_at, v_at = (pair_columns(pair, part, width) for part in range(3))
        gk_acc[...] = jnp.zeros_like(gk_acc)
        gv_acc[...] = jnp.zeros_like(gv_acc)
        for block in range(length // size):
            rows = slice(block * size, (block + 1) * size)
            upto = (block + 1) * size
            query = proj_ref[rows, q_at] * BF(SCALE)
            keys = proj_ref[0:upto, k_at]
            values = proj_ref[0:upto, v_at]
            gout = gctx_ref[rows, pair_columns(pair, 0, width)]
            grads = []
            for which in range(2):
                mine = head_lanes(query, which)
                gmine = head_lanes(gout, which)
                probs = block_softmax(mine, keys, seen)
                spans = [slice(upto - size, upto)]
                if len(probs) > 1:
                    spans = [slice(0, upto - size)] + spans
                gprobs = [dot(gmine, values[s], 1, 1) for s in spans]
                row = sum(jnp.sum(p * g, axis=-1, keepdims=True) for p, g in zip(probs, gprobs))
                gquery = None
                for p, g, s in zip(probs, gprobs, spans):
                    gscore = (p * (g - row)).astype(BF)
                    part = dot(gscore, keys[s], 1, 0)
                    gquery = part if gquery is None else gquery + part
                    gk_acc[s, :] += dot(gscore, mine, 0, 0)
                    gv_acc[s, :] += dot(p.astype(BF), gmine, 0, 0)
                grads.append(gquery * SCALE)
            lane = lax.broadcasted_iota(jnp.int32, grads[0].shape, 1)
            gproj_ref[rows, q_at] = jnp.where(lane < HEAD_DIM, grads[0], grads[1]).astype(BF)
        gproj_ref[:, k_at] = gk_acc[...].astype(BF)
        gproj_ref[:, v_at] = gv_acc[...].astype(BF)
        return carry

    lax.fori_loop(0, HEADS // 2, one_pair, 0)
    third = width // 3
    core = place_ref[0] % 2
    halves, rows, _ = keep0_ref.shape
    refs = ((keep0_ref, send0_ref), (keep1_ref, send1_ref), (keep2_ref, send2_ref))
    for part, (keep_ref, send_ref) in enumerate(refs):
        grad = dot(gproj_ref[...], normed_ref[:, part * third : (part + 1) * third], 0, 0)
        grad = grad.astype(BF)
        for at in range(halves):
            first = grad[2 * at * rows : (2 * at + 1) * rows]
            second = grad[(2 * at + 1) * rows : (2 * at + 2) * rows]
            keep_ref[at] = jnp.where(core == 0, first, second)
            send_ref[at] = jnp.where(core == 0, second, first)


def input_kernel(
    gproj_ref, in0_ref, in1_ref, in2_ref, x_ref, vec_ref, gmid_ref, grad_ref, sums_ref
):
    grad = jnp.concatenate(
        [dot(gproj_ref[...], ref[...], 1, 0) for ref in (in0_ref, in1_ref, in2_ref)], axis=1
    )
    back, gain_sum, bias_sum = norm_back(x_ref[...].astype(F32), vec_ref[0:1, :], grad)
    grad_ref[...] = gmid_ref[...] + back
    width = x_ref.shape[1]
    sums_ref[...] = jnp.concatenate([gain_sum, bias_sum, jnp.zeros((6, width), F32)], axis=0)


def mixed_kernel(old_ref, new_ref, target_ref, middle_ref, mixed_ref):
    total = take_rows(target_ref, (old_ref, new_ref), middle_ref.shape[0])
    mixed_ref[...] = (middle_ref[...] + total).astype(BF)


def gelu_pair(x):
    c = 0.7978845608028654
    sq = x * x
    t = jnp.tanh(c * x * (1.0 + 0.044715 * sq))
    half = 0.5 * (1.0 + t)
    slope = half + 0.5 * x * (1.0 - t * t) * (c * (1.0 + 3 * 0.044715 * sq))
    return x * half, slope

def expert_kernel(train, steps, pieces, place_ref, mine_ref, rows_ref, grads4_ref, router_ref, *rest):
    ups, downs, rest = rest[:pieces], rest[pieces : 2 * pieces], rest[2 * pieces :]
    if train:
        gated_ref, gin_ref, rgrad_ref, upkeep_ref, upsend_ref, downkeep_ref, downsend_ref = rest[:7]
        rest = rest[7:]
    else:
        gated_ref, gin_ref, rgrad_ref = rest[:3]
        rest = rest[3:]
    up_s, down_s, out_acc, gin_acc, scaled, gate_s, probs_s, sems = rest
    j = pl.program_id(0)
    mine = mine_ref[0:1, :]
    up_rows = up_s.shape[0] // pieces
    down_rows = down_s.shape[0] // pieces
    tile = up_s.shape[1] // steps

    def grads():
        return grads4_ref[...].reshape(rows_ref.shape).astype(F32)

    def fetches():
        found = []
        for at in range(pieces):
            owner = place_ref[at]
            to = pl.ds(pl.multiple_of(owner * up_rows, up_rows), up_rows)
            found.append(pltpu.make_async_copy(ups[at], up_s.at[to], sems.at[0, at]))
            to = pl.ds(pl.multiple_of(owner * down_rows, down_rows), down_rows)
            found.append(pltpu.make_async_copy(downs[at], down_s.at[to], sems.at[1, at]))
        return found

    @pl.when(j == 0)
    def _():
        for fetch in fetches():
            fetch.start()
        logits = dot(rows_ref[...], router_ref[...], 1, 1)
        live = lax.broadcasted_iota(jnp.int32, logits.shape, 1) < mine_ref[1, 0].astype(jnp.int32)
        logits = jnp.where(live, logits, -1e30)
        e = jnp.exp(logits - jnp.max(logits, axis=1, keepdims=True))
        probs = e / jnp.sum(e, axis=1, keepdims=True)
        probs_s[...] = probs
        gate = jnp.sum(probs * mine, axis=1, keepdims=True)
        gate_s[...] = jnp.broadcast_to(gate, gate_s.shape)
        scaled[...] = (grads() * gate).astype(BF)
        out_acc[...] = jnp.zeros_like(out_acc)
        gin_acc[...] = jnp.zeros_like(gin_acc)
        for fetch in fetches():
            fetch.wait()

    rows = rows_ref[...]
    here = pl.ds(pl.multiple_of(j * tile, tile), tile)
    up = up_s[:, here]
    down = down_s[here, :]
    hid, slope = gelu_pair(dot(rows, up, 1, 0))
    hid = hid.astype(BF)
    gpre = (dot(scaled[...], down, 1, 1) * slope).astype(BF)
    out_acc[...] += dot(hid, down, 1, 0)
    gin_acc[...] += dot(gpre, up, 1, 1)

    if train:
        core = place_ref[0] % 2
        grad_up = dot(rows, gpre, 0, 0).astype(BF)
        for pair in range(pieces // 2):
            first = grad_up[2 * pair * up_rows : (2 * pair + 1) * up_rows]
            second = grad_up[(2 * pair + 1) * up_rows : (2 * pair + 2) * up_rows]
            upkeep_ref[pair] = jnp.where(core == 0, first, second)
            upsend_ref[pair] = jnp.where(core == 0, second, first)
        grad_down = dot(hid, scaled[...], 0, 0).astype(BF)
        inside = tile // down_rows
        for at in range(inside):
            block = grad_down[at * down_rows : (at + 1) * down_rows]
            owner = j * inside + at

            @pl.when(owner % 2 == core)
            def _():
                downkeep_ref[owner // 2] = block

            @pl.when(owner % 2 != core)
            def _():
                downsend_ref[owner // 2] = block

    @pl.when(j == steps - 1)
    def _():
        produced = out_acc[...].astype(BF).astype(F32)
        gate = gate_s[:, 0:1]
        gated_ref[...] = (produced * gate).astype(BF)
        grad_gate = jnp.sum(produced * grads(), axis=1, keepdims=True)
        gl = (grad_gate * gate * (mine - probs_s[...])).astype(BF)
        gin_ref[...] = (gin_acc[...] + dot(gl, router_ref[...], 1, 0)).astype(BF)
        rgrad_ref[...] = dot(gl, rows_ref[...], 0, 0)


def expert_call(owners, mine, rows, grads, router_pad, ups, downs, train):
    n, d = rows.shape
    pieces = len(ups)
    f = ups[0].shape[1]
    tile = max(d, f // pieces)
    steps = f // tile
    peers, _, capacity, _ = grads.shape
    member = 1 if train else 0
    one = pl.Buffered(buffer_count=1)

    def all_of(shape):
        return pl.BlockSpec(shape, lambda j: (0,) * len(shape), pipeline_mode=one)

    slot_spec = pl.BlockSpec(
        (peers, 1, capacity, d), lambda j: (0, member, 0, 0), pipeline_mode=one
    )
    anywhere = pl.BlockSpec(memory_space=pl.ANY)
    outs = [((n, d), BF), ((n, d), BF), ((128, d), F32)]
    out_specs = [all_of((n, d)), all_of((n, d)), all_of((128, d))]
    if train:
        half = pieces // 2
        up_shape = (half, d // pieces, f)
        down_shape = (half, f // pieces, d)
        outs += [(up_shape, BF)] * 2 + [(down_shape, BF)] * 2
        out_specs += [pl.BlockSpec((half, d // pieces, tile), lambda j: (0, 0, j))] * 2
        out_specs += [all_of(down_shape)] * 2
    args = [owners, mine, rows, grads, router_pad, *ups, *downs]
    return pl.pallas_call(
        functools.partial(expert_kernel, train, steps, pieces),
        grid=(steps,),
        in_specs=[
            pl.BlockSpec(memory_space=pltpu.SMEM),
            all_of((8, 128)),
            all_of((n, d)),
            slot_spec,
            all_of((128, d)),
        ]
        + [anywhere] * (2 * pieces),
        out_specs=out_specs,
        out_shape=[whole(o) for o in outs],
        scratch_shapes=[
            pltpu.VMEM((d, f), BF),
            pltpu.VMEM((f, d), BF),
            pltpu.VMEM((n, d), F32),
            pltpu.VMEM((n, d), F32),
            pltpu.VMEM((n, d), BF),
            pltpu.VMEM((n, 128), F32),
            pltpu.VMEM((n, 128), F32),
            pltpu.SemaphoreType.DMA((2, pieces)),
        ],
        compiler_params=pltpu.CompilerParams(vmem_limit_bytes=LIMIT),
        cost_estimate=cost(40 if train else 27),
        name="expert_new" if train else "expert_old",
    )(*args)


def shards(
    block_input,
    cotangent,
    attn_in,
    attn_out,
    router,
    ln1_gain,
    ln1_bias,
    ln2_gain,
    ln2_bias,
    new_w1,
    new_w2,
    old_w1,
    old_w2,
    expert_ids,
    slots,
    drops,
):
    length, width = block_input.shape
    peers = lax.axis_size("expert")
    devices = lax.axis_size("dp") * peers
    experts = 2 * peers
    capacity = max(length * 7 // (2 * experts), 2)
    me = lax.axis_index("expert")
    ways, scatter_ways = orders()
    third = width // 3
    in_share = attn_in.shape[1]
    share = width // devices

    small = jnp.concatenate(
        [v[None] for v in (ln1_gain, ln1_bias, ln2_gain, ln2_bias)] + [router.T], axis=0
    )
    lines = small.shape[0]
    small = jnp.pad(small, ((0, -lines % 8), (0, third - share)))
    in_t, out_t = attn_in.T, attn_out.T
    states = []
    for p in range(3):
        cols = slice(p * third, (p + 1) * third)
        rows = [in_t[:, cols], out_t[:, cols]] + ([small] if p == 0 else [])
        states.append((jnp.concatenate(rows, axis=0), []))
    states = [gather_steps(states[p], ways[p][:2]) for p in range(3)]
    early = [state[0] for state in states]
    states = [gather_steps(states[p], ways[p][2:-1]) for p in range(3)]
    between = [state[0] for state in states]
    parts = [gather_finish(gather_steps(states[p], ways[p][-1:])) for p in range(3)]
    parts = [part.reshape(devices, -1, third) for part in parts]
    in_parts = [part[:, :in_share].reshape(3 * width, third) for part in parts]
    out_parts = [part[:, in_share : in_share + share].reshape(width, third) for part in parts]
    small_full = parts[0][:, in_share + share : in_share + share + lines, :share]
    small_full = small_full.transpose(1, 0, 2).reshape(lines, width)
    vectors = jnp.pad(small_full[:4].astype(F32), ((0, 4), (0, 0)))
    router_pad = jnp.pad(small_full[4:], ((0, 128 - experts), (0, 0)))

    target = jnp.where(drops == 0, expert_ids * capacity + slots, -1)
    by_member = ((expert_ids % 2) * peers + expert_ids // 2) * capacity + slots
    by_member = jnp.where(drops == 0, by_member, -1)
    target_rows = jnp.pad(target.T, ((0, 6), (0, 0)), constant_values=-1)
    member_rows = jnp.pad(by_member.T, ((0, 6), (0, 0)), constant_values=-1)
    count = peers * capacity
    both_shape = (peers, 2, capacity, width)

    def move(block):
        return lax.all_to_all(block, "expert", split_axis=0, concat_axis=0, tiled=True)

    def send(block, *earlier):
        block = after(block, *earlier).reshape(peers, capacity, width)
        return move(block).reshape(count, width)

    (grad_slots,) = plain_call(
        place_kernel, [((2 * count, width), BF)], [], "place_grads", 4, target_rows, after(cotangent, early)
    )
    grads = move(after(grad_slots, between).reshape(both_shape))
    slot_outs = [((count, width), BF)] * 2

    normed, proj, context, middle, rold, rnew = plain_call(
        forward_kernel,
        [
            ((length, width), BF),
            ((length, 3 * width), BF),
            ((length, width), BF),
            ((length, width), F32),
        ]
        + slot_outs,
        [],
        "attention_forward", 27,
        block_input,
        *in_parts,
        *out_parts,
        vectors,
        member_rows,
    )
    owners = lax.axis_index("dp") ^ jnp.arange(lax.axis_size("dp"), dtype=jnp.int32)
    new_ups, far_up = dp_pieces(new_w1[0], (between,), ())
    new_downs, far_down = dp_pieces(new_w2[0], (between,), ())
    old_ups, _ = dp_pieces(old_w1[0], (between, far_up), ())
    old_downs, _ = dp_pieces(old_w2[0], (between, far_up), ())
    rold = send(rold, grads, far_up, far_down)
    rnew = send(rnew, rold)

    lane = lax.broadcasted_iota(jnp.int32, (8, 128), 1)
    line = lax.broadcasted_iota(jnp.int32, (8, 128), 0)

    def chosen(expert):
        return jnp.where(line == 0, (lane == expert).astype(F32), F32(experts))

    old_gated, old_in, old_router = expert_call(
        owners, chosen(2 * me), rold, grads, router_pad, old_ups, old_downs, False
    )
    rnew, old_in = lax.optimization_barrier((rnew, old_in))
    old_in = send(old_in, rnew)
    new_gated, new_in, new_router, up_keep, up_send, down_keep, down_send = expert_call(
        owners, chosen(2 * me + 1), rnew, grads, router_pad, new_ups, new_downs, True
    )
    new_in = send(new_in, old_in)
    old_gated = send(old_gated, new_in)
    new_gated = send(new_gated, old_gated)
    up_send, down_send = after((up_send, down_send), old_in)
    new_w1_grad = scatter_dp(up_keep, up_send)[None]
    new_w2_grad = scatter_dp(down_keep, down_send)[None]
    router_part = (old_router + new_router)[:experts]

    gmid, gctx, out_grad, sums_two = plain_call(
        branch_kernel,
        [
            ((length, width), F32),
            ((length, width), BF),
            ((width, width), BF),
            ((8, width), F32),
        ],
        [],
        "branch_backward",
        0,
        old_in,
        new_in,
        by_member,
        cotangent,
        middle,
        context,
        *out_parts,
        vectors,
    )
    half = lax.axis_size("dp") // 2
    gproj, *split = plain_call(
        attention_back_kernel,
        [((length, 3 * width), BF)] + [((half, 3 * width // (2 * half), third), BF)] * 6,
        [pltpu.VMEM((length, 2 * HEAD_DIM), F32)] * 2,
        "attention_backward",
        0,
        owners,
        proj,
        gctx,
        normed,
    )
    input_grad, sums_one = plain_call(
        input_kernel,
        [((length, width), F32), ((8, width), F32)],
        [],
        "input_backward", 0,
        gproj,
        *in_parts,
        block_input,
        vectors,
        gmid,
    )
    (mixed,) = plain_call(
        mixed_kernel,
        [((length, width), BF)],
        [],
        "mixed_output", 0,
        old_gated,
        new_gated,
        by_member,
        middle,
    )
    lead = canonical()
    core = [("dp", powers(lax.axis_size("dp"))[0])]
    states = []
    for keep, away in zip(split[:3], split[3:]):
        total = keep.astype(F32) + swap(away, *core[0]).astype(F32)
        left = [step for step in lead if step != core[0]]
        states.append((total.reshape([2] * len(left) + [in_share, third]), left))
    small_grads = jnp.concatenate([sums_one[:2], sums_two[:2], router_part], axis=0)
    small_grads = small_grads.reshape(lines, devices, share).transpose(1, 0, 2)
    small_grads = small_grads.reshape(devices, 1, lines * share).astype(BF)
    small_rows = -(-lines * share // width)
    small_grads = jnp.pad(small_grads, ((0, 0), (0, 0), (0, small_rows * width - lines * share)))
    rest = jnp.concatenate(
        [out_grad.reshape(devices, share, width), small_grads.reshape(devices, small_rows, width)],
        axis=1,
    )
    rest = rest.reshape([2] * len(lead) + list(rest.shape[1:]))
    states.append(scatter_steps((rest, lead), core))
    held = after([values for values, _ in states], old_gated, new_gated)
    sums = [
        scatter_steps((held[p], states[p][1]), scatter_ways[p])[0] for p in range(len(states))
    ]
    attn_in_grad = jnp.concatenate(sums[:3], axis=1).T
    attn_out_grad = sums[3][:share].T
    small_grads = sums[3][share:].reshape(-1)[: lines * share].reshape(lines, share)
    vector_grads = small_grads[:4]
    router_grad = small_grads[4:].T
    return (
        mixed,
        input_grad,
        attn_in_grad,
        attn_out_grad,
        router_grad,
        vector_grads[0],
        vector_grads[1],
        vector_grads[2],
        vector_grads[3],
        new_w1_grad,
        new_w2_grad,
    )


def solution(mesh):
    both = ("dp", "expert")
    rows = P(both, None)
    columns = P(None, both)
    vector = P(both)
    weight = P("expert", "dp", None)
    in_specs = (
        [rows, rows, columns, columns, rows] + [vector] * 4 + [weight] * 4 + [rows] * 3
    )
    out_specs = [rows, rows, columns, columns, rows] + [vector] * 4 + [weight] * 2
    return jax.shard_map(
        shards, mesh=mesh, in_specs=tuple(in_specs), out_specs=tuple(out_specs), check_vma=False
    )
```

time: 564 us -> 464 us (0.82)
  waiting for transfers between devices: 206 us -> 155 us
  other arithmetic: 57 us -> 33.1 us
  starting transfers between devices: 96.7 us -> 79.7 us
  local copies, waits for them, and re-layouts: 47.3 us -> 35.2 us
    ppermute x62 -> x51, waiting for transfers between devices: 181 us -> 70.8 us  [swap(): return lax.ppermute(values, axis, [(i, i ^ bit) for i in range(count)])]
    all_to_all x8 -> x7, waiting for transfers between devices: 25.3 us -> 84.6 us  [move(): lax.all_to_all(block, 'expert', split_axis=0, concat_axis=0, tiled=True)]
    another operation x37 -> x28, other arithmetic: 29.7 us -> 7.5 us  [the longest x27 6.67 us: gather_steps(): jnp.stack([jnp.where(low, current, other), jnp.where(low, other, current)])]
    transpose x8 -> x4, local copies, waits for them, and re-layouts: 10.4 us -> 0.93 us  [the longest x1 0.64 us: shards(): attn_out_grad = sums[3][:share].T]
    ppermute x62 -> x51, starting transfers between devices: 54.2 us -> 45 us  [swap(): return lax.ppermute(values, axis, [(i, i ^ bit) for i in range(count)])]
    all_to_all x8 -> x7, starting transfers between devices: 42.6 us -> 34.7 us  [move(): lax.all_to_all(block, 'expert', split_axis=0, concat_axis=0, tiled=True)]
    dynamic_slice x15 -> x2, local copies, waits for them, and re-layouts: 6.93 us -> 0.21 us  [scatter_steps(): keep = lax.dynamic_index_in_dim(current, mine, at, keepdims=False)]
    slice x7 -> x17, local copies, waits for them, and re-layouts: 3.56 us -> 9.83 us  [the longest x3 3.39 us: shards(): in_parts = [part[:, :in_share].reshape(3 * width, third) for part in parts]]
  transfers between devices with their start and end apart: 70 -> 58, of which waited for: 32 -> 26; matrix products, arithmetic and copies ran while one was open for 16% -> 12% of each run, Pallas kernels for 27% -> 32%
where the time goes in v2:
time: 464 us; the launch traced here: 458 us
  waiting for transfers between devices  155 us (33%)
  Pallas kernels  153 us (33%)
  starting transfers between devices  79.7 us (17%)
  local copies, waits for them, and re-layouts  35.2 us (8%)
  other arithmetic  33.1 us (7%)
    pallas_call x6, Pallas kernels, plain_call(): pl.pallas_call(body, out_shape=[whole(o) for o in outs], in_specs=[space]...  84.8 us
    all_to_all x7, waiting for transfers between devices, move(): lax.all_to_all(block, 'expert', split_axis=0, concat_axis=0, tiled=True)  84.6 us
    ppermute x51, waiting for transfers between devices, swap(): return lax.ppermute(values, axis, [(i, i ^ bit) for i in range(count)])  70.8 us
    pallas_call x2, Pallas kernels, expert_call(): pl.pallas_call(functools.partial(expert_kernel, train, steps, pieces), gr...  68 us
    ppermute x51, starting transfers between devices, swap(): return lax.ppermute(values, axis, [(i, i ^ bit) for i in range(count)])  45 us
    all_to_all x7, starting transfers between devices, move(): lax.all_to_all(block, 'expert', split_axis=0, concat_axis=0, tiled=True)  34.7 us
    unnamed x64, local copies, waits for them, and re-layouts  13.2 us
  transfers between devices with their start and end apart: 58, of which 26 were waited for; matrix products, arithmetic and copies ran while one was open for 12% of the time, Pallas kernels for 32%

profile of v2, /device:TPU:0, one launch (start us, length us, event | category | flops | bytes accessed | tf_op | source)
XLA Modules:
  0.0 458.4 jit_solution(4800837670721248069)
XLA Ops:
  24.9 4.3 place_grads.1
  34.9 4.2 collective-permute-done.8
  45.3 4.7 %all-to-all-start = ((bf16[8,2,112,768]{3,2,1,0:T(8,128)(2,1)}), bf16[8,2,112,768]{3,2,1,0:T(8,128)(2,1)}, u32[]{:S(2)}, u32[]{:S(2)}) async-start(bf16[8,2,112,768]{3,2,1,0:T(8,128)(2,1)} %bitcast.245), calls=%async_computation | async-start | bytes 5505024 | tf_op jit(solution)/shard_map/all_to_all | solution.py:637
  64.0 26.8 %attention_forward.1 = (bf16[512,768]{1,0:T(8,128)(2,1)}, bf16[512,2304]{1,0:T(8,128)(2,1)}, bf16[512,768]{1,0:T(8,128)(2,1)}, f32[512,768]{1,0:T(8,128)}, bf16[...) custom-call(bf16[512,768]{1,0:T(8,128)(2,1)} %x_ref.3, bf16[2304,256]{1,0:T(8,128)(2,1)} %bitcast.236, ...), custom_call_target="tpu_custom_call" | custom-call | flops 6750000128 | tf_op jit(solution)/shard_map/attention_forward/pallas_call | solution.py:147
  90.8 14.5 %collective-permute-done.16.rest_6_ = bf16[768,768]{1,0:T(8,128)(2,1)} collective-permute-done((bf16[768,768]{1,0:T(8,128)(2,1)}, bf16[768,768]{1,0:T(8,128)(2,1)}, u32[]{:S(2)}, u32[]{:S(2)}) %collective-permute-start.16) | collective-permute-done | bytes 1179680 | tf_op jit(solution)/shard_map/ppermute | solution.py:31
  105.3 4.9 %all-to-all-done.grads4_ref = bf16[8,2,112,768]{3,2,1,0:T(8,128)(2,1)} async-done(((bf16[8,2,112,768]{3,2,1,0:T(8,128)(2,1)}), bf16[8,2,112,768]{3,2,1,0:T(8,128)(2,1)}, u32[]{:S(2)}, u32[]{:S(2)}) %all-to-all-start) | async-done | bytes 2752544 | tf_op jit(solution)/shard_map/all_to_all | solution.py:637
  110.2 3.6 all-to-all-start.1
  115.9 30.9 %all-to-all-done.1 = bf16[8,112,768]{2,1,0:T(8,128)(2,1)S(1)} async-done(((bf16[8,112,768]{2,1,0:T(8,128)(2,1)}), bf16[8,112,768]{2,1,0:T(8,128)(2,1)S(1)}, u32[]{:S(2)}, u32[]{:S(2)}) %all-to-all-start.1) | async-done | bytes 1376288 | tf_op jit(solution)/shard_map/all_to_all | solution.py:637
  147.9 4.2 all-to-all-start.2
  152.8 14.3 %collective-permute-done.18.rest_2_ = bf16[192,3072]{1,0:T(8,128)(2,1)} collective-permute-done((bf16[192,3072]{1,0:T(8,128)(2,1)}, bf16[192,3072]{1,0:T(8,128)(2,1)}, u32[]{:S(2)}, u32[]{:S(2)}) %collective-permute-start.18) | collective-permute-done | bytes 1179680 | tf_op jit(solution)/shard_map/ppermute | solution.py:31
  170.3 27.4 %expert_old.1 = (bf16[896,768]{1,0:T(8,128)(2,1)}, bf16[896,768]{1,0:T(8,128)(2,1)}, f32[128,768]{1,0:T(8,128)}) custom-call(s32[4]{0:T(128)} %iota_xor_fusion.place_ref, f32[8,128]{1,0:T(8,128)} %get-tuple-element.152.mine_ref, bf16[896,768]{1,0:T(8,128)(2,1)} %bitcast.256, bf16[8,2,112,768]{3,2,1,0:T(8,128)(2,1)} %all-to-all-done.grads4_ref, ...), custom_call_target="tpu_custom_call" | custom-call | flops 6750000128 | tf_op jit(solution)/shard_map/expert_old/pallas_call | solution.py:546
  198.8 5.9 %all-to-all-start.3 = ((bf16[8,112,768]{2,1,0:T(8,128)(2,1)}), bf16[8,112,768]{2,1,0:T(8,128)(2,1)S(1)}, u32[]{:S(2)}, u32[]{:S(2)}) async-start(bf16[8,112,768]{2,1,0:T(8,128)(2,1)} %bitcast.257), calls=%async_computation.3 | async-start | bytes 2752512 | tf_op jit(solution)/shard_map/all_to_all | solution.py:637
  214.0 40.6 %expert_new.1 = (bf16[896,768]{1,0:T(8,128)(2,1)}, bf16[896,768]{1,0:T(8,128)(2,1)}, f32[128,768]{1,0:T(8,128)}, bf16[2,192,3072]{2,1,0:T(8,128)(2,1)}, bf16[2,1...) custom-call(s32[4]{0:T(128)} %iota_xor_fusion.place_ref, ...), custom_call_target="tpu_custom_call" | custom-call | flops 10000000000 | tf_op jit(solution)/shard_map/expert_new/pallas_call | solution.py:546
  255.7 6.0 %all-to-all-start.4 = ((bf16[8,112,768]{2,1,0:T(8,128)(2,1)}), bf16[8,112,768]{2,1,0:T(8,128)(2,1)S(1)}, u32[]{:S(2)}, u32[]{:S(2)}) async-start(bf16[8,112,768]{2,1,0:T(8,128)(2,1)} %bitcast.255), calls=%async_computation.4 | async-start | bytes 2752512 | tf_op jit(solution)/shard_map/all_to_all | solution.py:637
  262.2 32.6 %all-to-all-done.4 = bf16[8,112,768]{2,1,0:T(8,128)(2,1)S(1)} async-done(((bf16[8,112,768]{2,1,0:T(8,128)(2,1)}), bf16[8,112,768]{2,1,0:T(8,128)(2,1)S(1)}, u32[]{:S(2)}, u32[]{:S(2)}) %all-to-all-start.4) | async-done | bytes 1376288 | tf_op jit(solution)/shard_map/all_to_all | solution.py:637
  295.9 3.9 all-to-all-start.5
  313.1 8.6 %branch_backward.1 = (f32[512,768]{1,0:T(8,128)}, bf16[512,768]{1,0:T(8,128)(2,1)}, bf16[768,768]{1,0:T(8,128)(2,1)}, f32[8,768]{1,0:T(8,128)}) custom-call(bf16[896,768]{1,0:T(8,128)(2,1)} %bitcast.228, bf16[896,768]{1,0:T(8,128)(2,1)} %bitcast.230, s32[512,2]{1,0:T(8,128)} %copy-done.7, bf16[512,768]{1,0:T(8,128)(2,1)} %cot_ref.1, ...), custom_call_target="tpu_custom_call" | custom-call | tf_op jit(solution)/shard_map/branch_backward/pallas_call | solution.py:147
  321.6 32.8 %attention_backward.1 = (bf16[512,2304]{1,0:T(8,128)(2,1)}, bf16[2,576,256]{2,1,0:T(8,128)(2,1)}, bf16[2,576,256]{2,1,0:T(8,128)(2,1)}, bf16[2,576,256]{2,1,0:T(...) custom-call(s32[4]{0:T(128)} %iota_xor_fusion.place_ref, ...), custom_call_target="tpu_custom_call" | custom-call | tf_op jit(solution)/shard_map/attention_backward/pallas_call | solution.py:147
  354.4 7.2 %input_backward.1 = (f32[512,768]{1,0:T(8,128)}, f32[8,768]{1,0:T(8,128)}) custom-call(bf16[512,2304]{1,0:T(8,128)(2,1)} %get-tuple-element.85.gproj_ref, bf16[2304,256]{1,0:T(8,128)(2,1)} %bitcast.237, bf16[2304,256]{1,0:T(8,128)(2,1)} %bitcast.235, bf16[2304,256]{1,0:T(8,128)(2,1)} %bitcast.233, bf16[512,768]{1,0:T(8,128)(2,1)} %x_ref.3, ...), custom_call_target="tpu_custom_call" | custom-call | tf_op jit(solution)/shard_map/input_backward/pallas_call | solution.py:147
  367.3 6.3 %all-to-all-start.6 = ((bf16[8,112,768]{2,1,0:T(8,128)(2,1)}), bf16[8,112,768]{2,1,0:T(8,128)(2,1)S(1)}, u32[]{:S(2)}, u32[]{:S(2)}) async-start(bf16[8,112,768]{2,1,0:T(8,128)(2,1)} %bitcast.252), calls=%async_computation.6 | async-start | bytes 2752512 | tf_op jit(solution)/shard_map/all_to_all | solution.py:637
  390.7 16.2 %all-to-all-done.6 = bf16[8,112,768]{2,1,0:T(8,128)(2,1)S(1)} async-done(((bf16[8,112,768]{2,1,0:T(8,128)(2,1)}), bf16[8,112,768]{2,1,0:T(8,128)(2,1)S(1)}, u32[]{:S(2)}, u32[]{:S(2)}) %all-to-all-start.6) | async-done | bytes 1376288 | tf_op jit(solution)/shard_map/all_to_all | solution.py:637
  408.1 5.2 %mixed_output.1 = bf16[512,768]{1,0:T(8,128)(2,1)} custom-call(bf16[896,768]{1,0:T(8,128)(2,1)} %bitcast.229, bf16[896,768]{1,0:T(8,128)(2,1)} %bitcast.231, s32[512,2]{1,0:T(8,128)} %copy-done.7, f32[512,768]{1,0:T(8,128)} %get-tuple-element.80.middle_ref), custom_call_target="tpu_custom_call" | custom-call | tf_op jit(solution)/shard_map/mixed_output/pallas_call | solution.py:147
  425.6 4.5 collective-permute-done.39
  436.8 7.3 %collective-permute-done.40 = bf16[2,2,72,256]{3,2,1,0:T(8,128)(2,1)S(1)} collective-permute-done((bf16[2,2,72,256]{3,2,1,0:T(8,128)(2,1)S(1)}, bf16[2,2,72,256]{3,2,1,0:T(8,128)(2,1)S(1)}, u32[]{:S(2)}, u32[]{:S(2)}) %collective-permute-start.40) | collective-permute-done | bytes 147488 | tf_op jit(solution)/shard_map/ppermute | solution.py:31
  (295 shorter events, 139.3 us)
Async XLA Ops:
  45.3 65.0 %all-to-all-start = ((bf16[8,2,112,768]{3,2,1,0:T(8,128)(2,1)}), bf16[8,2,112,768]{3,2,1,0:T(8,128)(2,1)}, u32[]{:S(2)}, u32[]{:S(2)}) async-start(bf16[8,2,112,768]{3,2,1,0:T(8,128)(2,1)} %bitcast.245), calls=%async_computation | async-start | bytes 5505024 | tf_op jit(solution)/shard_map/all_to_all | solution.py:637
  51.4 39.4 %collective-permute-start.15 = (bf16[192,3072]{1,0:T(8,128)(2,1)}, bf16[192,3072]{1,0:T(8,128)(2,1)}, u32[]{:S(2)}, u32[]{:S(2)}) collective-permute-start(bf16[192,3072]{1,0:T(8,128)(2,1)} %bitcast.271), channel_id=1, source_target_pairs={{0,16},{8,24},{16,0},{24,8},{1,17},{9,25},{17,1},{25,9},{2,18},{10... | collective-permute-start | bytes 3538952 | tf_op jit(solution)/shard_map/ppermute | solution.py:31
  52.9 52.4 %collective-permute-start.16 = (bf16[768,768]{1,0:T(8,128)(2,1)}, bf16[768,768]{1,0:T(8,128)(2,1)}, u32[]{:S(2)}, u32[]{:S(2)}) collective-permute-start(bf16[768,768]{1,0:T(8,128)(2,1)} %bitcast.274), channel_id=1, source_target_pairs={{0,16},{8,24},{16,0},{24,8},{1,17},{9,25},{17,1},{25,9},{2,18},{10... | collective-permute-start | bytes 3538952 | tf_op jit(solution)/shard_map/ppermute | solution.py:31
  110.2 36.6 %all-to-all-start.1 = ((bf16[8,112,768]{2,1,0:T(8,128)(2,1)}), bf16[8,112,768]{2,1,0:T(8,128)(2,1)S(1)}, u32[]{:S(2)}, u32[]{:S(2)}) async-start(bf16[8,112,768]{2,1,0:T(8,128)(2,1)} %bitcast.258), calls=%async_computation.1 | async-start | bytes 2752512 | tf_op jit(solution)/shard_map/all_to_all | solution.py:637
  113.9 38.8 %collective-permute-start.21 = (bf16[768,768]{1,0:T(8,128)(2,1)}, bf16[768,768]{1,0:T(8,128)(2,1)}, u32[]{:S(2)}, u32[]{:S(2)}) collective-permute-start(bf16[768,768]{1,0:T(8,128)(2,1)} %bitcast.62.rest_4_), channel_id=1, source_target_pairs={{0,16},{8,24},{16,0},{24,8},{1,17},{9,25},{17,1},{25,9},{2,18},{10... | collective-permute-start | bytes 3538952 | tf_op jit(solution)/shard_map/ppermute | solution.py:31
  115.1 52.0 %collective-permute-start.18 = (bf16[192,3072]{1,0:T(8,128)(2,1)}, bf16[192,3072]{1,0:T(8,128)(2,1)}, u32[]{:S(2)}, u32[]{:S(2)}) collective-permute-start(bf16[192,3072]{1,0:T(8,128)(2,1)} %bitcast.61.rest_0_), channel_id=1, source_target_pairs={{0,16},{8,24},{16,0},{24,8},{1,17},{9,25},{17,1},{25,9},{2,18},{10... | collective-permute-start | bytes 3538952 | tf_op jit(solution)/shard_map/ppermute | solution.py:31
  147.9 49.8 %all-to-all-start.2 = ((bf16[8,112,768]{2,1,0:T(8,128)(2,1)}), bf16[8,112,768]{2,1,0:T(8,128)(2,1)S(1)}, u32[]{:S(2)}, u32[]{:S(2)}) async-start(bf16[8,112,768]{2,1,0:T(8,128)(2,1)} %bitcast.63), calls=%async_computation.2 | async-start | bytes 2752512 | tf_op jit(solution)/shard_map/all_to_all | solution.py:637
  152.1 17.1 %collective-permute-start.20 = (bf16[768,768]{1,0:T(8,128)(2,1)}, bf16[768,768]{1,0:T(8,128)(2,1)S(1)}, u32[]{:S(2)}, u32[]{:S(2)}) collective-permute-start(bf16[768,768]{1,0:T(8,128)(2,1)} %bitcast.62.rest_4_), channel_id=1, source_target_pairs={{0,8},{8,0},{16,24},{24,16},{1,9},{9,1},{17,25},{25,17},{2,10},{10... | collective-permute-start | bytes 3538952 | tf_op jit(solution)/shard_map/ppermute | solution.py:31
  152.2 17.1 %collective-permute-start.17 = (bf16[192,3072]{1,0:T(8,128)(2,1)}, bf16[192,3072]{1,0:T(8,128)(2,1)}, u32[]{:S(2)}, u32[]{:S(2)}) collective-permute-start(bf16[192,3072]{1,0:T(8,128)(2,1)} %bitcast.61.rest_0_), channel_id=1, source_target_pairs={{0,8},{8,0},{16,24},{24,16},{1,9},{9,1},{17,25},{25,17},{2,10},{10... | collective-permute-start | bytes 3538952 | tf_op jit(solution)/shard_map/ppermute | solution.py:31
  152.7 16.6 %collective-permute-start.22 = (bf16[768,768]{1,0:T(8,128)(2,1)}, bf16[768,768]{1,0:T(8,128)(2,1)}, u32[]{:S(2)}, u32[]{:S(2)}) collective-permute-start(bf16[768,768]{1,0:T(8,128)(2,1)} %collective-permute-done.21.rest_6_), channel_id=1, source_target_pairs={{0,8},{8,0},{16,24},{24,16},{1,9},{9,1},{17,25},{25,17},{2,10},{10... | collective-permute-start | bytes 3538952 | tf_op jit(solution)/shard_map/ppermute | solution.py:31
  198.8 55.8 %all-to-all-start.3 = ((bf16[8,112,768]{2,1,0:T(8,128)(2,1)}), bf16[8,112,768]{2,1,0:T(8,128)(2,1)S(1)}, u32[]{:S(2)}, u32[]{:S(2)}) async-start(bf16[8,112,768]{2,1,0:T(8,128)(2,1)} %bitcast.257), calls=%async_computation.3 | async-start | bytes 2752512 | tf_op jit(solution)/shard_map/all_to_all | solution.py:637
  255.7 39.1 %all-to-all-start.4 = ((bf16[8,112,768]{2,1,0:T(8,128)(2,1)}), bf16[8,112,768]{2,1,0:T(8,128)(2,1)S(1)}, u32[]{:S(2)}, u32[]{:S(2)}) async-start(bf16[8,112,768]{2,1,0:T(8,128)(2,1)} %bitcast.255), calls=%async_computation.4 | async-start | bytes 2752512 | tf_op jit(solution)/shard_map/all_to_all | solution.py:637
  261.7 38.9 %collective-permute-start.49 = (bf16[2,768,768]{2,1,0:T(8,128)(2,1)}, bf16[2,768,768]{2,1,0:T(8,128)(2,1)}, u32[]{:S(2)}, u32[]{:S(2)}) collective-permute-start(bf16[2,768,768]{2,1,0:T(8,128)(2,1)} %get-tuple-element.108), channel_id=1, source_target_pairs={{0,8},{8,0},{16,24},{24,16},{1,9},{9,1},{17,25},{25,17},{2,10},{10... | collective-permute-start | bytes 7077896 | tf_op jit(solution)/shard_map/ppermute | solution.py:31
  261.7 44.0 %collective-permute-start.47 = (bf16[2,192,3072]{2,1,0:T(8,128)(2,1)}, bf16[2,192,3072]{2,1,0:T(8,128)(2,1)}, u32[]{:S(2)}, u32[]{:S(2)}) collective-permute-start(bf16[2,192,3072]{2,1,0:T(8,128)(2,1)} %get-tuple-element.106), channel_id=1, source_target_pairs={{0,8},{8,0},{16,24},{24,16},{1,9},{9,1},{17,25},{25,17},{2,10},{10... | collective-permute-start | bytes 7077896 | tf_op jit(solution)/shard_map/ppermute | solution.py:31
  295.9 70.3 %all-to-all-start.5 = ((bf16[8,112,768]{2,1,0:T(8,128)(2,1)}), bf16[8,112,768]{2,1,0:T(8,128)(2,1)S(1)}, u32[]{:S(2)}, u32[]{:S(2)}) async-start(bf16[8,112,768]{2,1,0:T(8,128)(2,1)} %bitcast.253), calls=%async_computation.5 | async-start | bytes 2752512 | tf_op jit(solution)/shard_map/all_to_all | solution.py:637
  304.7 80.1 %collective-permute-start.50 = (bf16[768,768]{1,0:T(8,128)(2,1)}, bf16[768,768]{1,0:T(8,128)(2,1)}, u32[]{:S(2)}, u32[]{:S(2)}) collective-permute-start(bf16[768,768]{1,0:T(8,128)(2,1)} %fusion.3), channel_id=1, source_target_pairs={{0,16},{8,24},{16,0},{24,8},{1,17},{9,25},{17,1},{25,9},{2,18},{10... | collective-permute-start | bytes 3538952 | tf_op jit(solution)/shard_map/ppermute | solution.py:31
  312.0 75.7 %collective-permute-start.48 = (bf16[192,3072]{1,0:T(8,128)(2,1)}, bf16[192,3072]{1,0:T(8,128)(2,1)}, u32[]{:S(2)}, u32[]{:S(2)}) collective-permute-start(bf16[192,3072]{1,0:T(8,128)(2,1)} %fusion.2), channel_id=1, source_target_pairs={{0,16},{8,24},{16,0},{24,8},{1,17},{9,25},{17,1},{25,9},{2,18},{10... | collective-permute-start | bytes 3538952 | tf_op jit(solution)/shard_map/ppermute | solution.py:31
  363.7 14.8 %collective-permute-start.28 = (bf16[2,576,256]{2,1,0:T(8,128)(2,1)}, bf16[2,576,256]{2,1,0:T(8,128)(2,1)}, u32[]{:S(2)}, u32[]{:S(2)}) collective-permute-start(bf16[2,576,256]{2,1,0:T(8,128)(2,1)} %get-tuple-element.91), channel_id=1, source_target_pairs={{0,8},{8,0},{16,24},{24,16},{1,9},{9,1},{17,25},{25,17},{2,10},{10... | collective-permute-start | bytes 1769480 | tf_op jit(solution)/shard_map/ppermute | solution.py:31
  364.2 16.7 %collective-permute-start.27 = (bf16[2,576,256]{2,1,0:T(8,128)(2,1)}, bf16[2,576,256]{2,1,0:T(8,128)(2,1)}, u32[]{:S(2)}, u32[]{:S(2)}) collective-permute-start(bf16[2,576,256]{2,1,0:T(8,128)(2,1)} %get-tuple-element.89), channel_id=1, source_target_pairs={{0,8},{8,0},{16,24},{24,16},{1,9},{9,1},{17,25},{25,17},{2,10},{10... | collective-permute-start | bytes 1769480 | tf_op jit(solution)/shard_map/ppermute | solution.py:31
  367.3 39.7 %all-to-all-start.6 = ((bf16[8,112,768]{2,1,0:T(8,128)(2,1)}), bf16[8,112,768]{2,1,0:T(8,128)(2,1)S(1)}, u32[]{:S(2)}, u32[]{:S(2)}) async-start(bf16[8,112,768]{2,1,0:T(8,128)(2,1)} %bitcast.252), calls=%async_computation.6 | async-start | bytes 2752512 | tf_op jit(solution)/shard_map/all_to_all | solution.py:637
  413.6 17.5 %collective-permute-start.43 = (bf16[2,2,2,25,768]{4,2,3,1,0:T(2,128)(2,1)S(1)}, bf16[2,2,2,25,768]{4,2,3,1,0:T(2,128)(2,1)S(1)}, u32[]{:S(2)}, u32[]{:S(2)}) collective-permute-start(bf16[2,2,2,25,768]{4,2,3,1,0:T(2,128)(2,1)S(1)} %fusion.4), channel_id=1, source_target_pairs={{0,2},{1,3},{2,0},{3,1},{4,6},{5,7},{6,4},{7,5},{8,10},{9,11},{10,... | collective-permute-start | bytes 921608 | tf_op jit(solution)/shard_map/ppermute | solution.py:31
  431.5 15.1 %collective-permute-start.44 = (bf16[2,2,25,768]{3,1,2,0:T(2,128)(2,1)S(1)}, bf16[2,2,25,768]{3,1,2,0:T(2,128)(2,1)S(1)}, u32[]{:S(2)}, u32[]{:S(2)}) collective-permute-start(bf16[2,2,25,768]{3,1,2,0:T(2,128)(2,1)S(1)} %fusion.15), channel_id=1, source_target_pairs={{0,4},{1,5},{2,6},{3,7},{4,0},{5,1},{6,2},{7,3},{8,12},{9,13},{10,... | collective-permute-start | bytes 460808 | tf_op jit(solution)/shard_map/ppermute | solution.py:31
  433.7 14.2 %collective-permute-start.33 = (bf16[2,72,256]{2,1,0:T(8,128)(2,1)S(1)}, bf16[2,72,256]{2,1,0:T(8,128)(2,1)S(1)}, u32[]{:S(2)}, u32[]{:S(2)}) collective-permute-start(bf16[2,72,256]{2,1,0:T(8,128)(2,1)S(1)} %fusion.20), channel_id=1, source_target_pairs={{0,2},{1,3},{2,0},{3,1},{4,6},{5,7},{6,4},{7,5},{8,10},{9,11},{10,... | collective-permute-start | bytes 221192 | tf_op jit(solution)/shard_map/ppermute | solution.py:31
  434.0 14.1 %collective-permute-start.37 = (bf16[2,72,256]{2,1,0:T(8,128)(2,1)S(1)}, bf16[2,72,256]{2,1,0:T(8,128)(2,1)S(1)}, u32[]{:S(2)}, u32[]{:S(2)}) collective-permute-start(bf16[2,72,256]{2,1,0:T(8,128)(2,1)S(1)} %fusion.21), channel_id=1, source_target_pairs={{0,4},{1,5},{2,6},{3,7},{4,0},{5,1},{6,2},{7,3},{8,12},{9,13},{10,... | collective-permute-start | bytes 221192 | tf_op jit(solution)/shard_map/ppermute | solution.py:31
  (63 other events, 430.3 us)

commit v3 on v2

--- a/solution.py
+++ b/solution.py
@@ -79,39 +79,77 @@
     return lax.optimization_barrier((values, earlier))[0]
 
 
-def scatter_steps(state, order):
-    current, lead = state
-    lead = list(lead)
-    for axis, bit in order:
-        at = lead.index((axis, bit))
-        mine = my_bit(axis, bit)
-        keep = lax.dynamic_index_in_dim(current, mine, at, keepdims=False)
-        send = lax.dynamic_index_in_dim(current, 1 - mine, at, keepdims=False)
-        got = swap(send.astype(BF), axis, bit)
-        current = keep.astype(F32) + got.astype(F32)
-        lead.pop(at)
-    return current, lead
-
-
-def dp_pieces(shard, first, second):
-    bits = powers(lax.axis_size("dp"))
-    found = {0: shard, bits[0]: swap(after(shard, *first), "dp", bits[0])}
+def total(addends):
+    found = addends[0].astype(F32)
+    for addend in addends[1:]:
+        found = found + addend.astype(F32)
+    return found
+
+
+def away_part(addends, lead, step):
+    at = lead.index(step)
+    mine = my_bit(*step)
+    send = total([lax.dynamic_index_in_dim(a, 1 - mine, at, keepdims=False) for a in addends])
+    return send.astype(BF)
+
+
+def scatter_step(addends, lead, step):
+    return swap(away_part(addends, lead, step), *step)
+
+
+def scatter_rest(addends, lead, step, got):
+    at = lead.index(step)
+    addends = [lax.dynamic_index_in_dim(a, my_bit(*step), at, keepdims=False) for a in addends]
+    return addends + [got], lead[:at] + lead[at + 1 :]
+
+
+def core_swap(piece):
+    return swap(piece, "dp", powers(lax.axis_size("dp"))[0])
+
+
+def dp_far(shard):
     far = {}
-    for bit in bits[1:]:
-        for away, piece in [(0, after(shard, *first)), *far.items()]:
+    for bit in powers(lax.axis_size("dp"))[1:]:
+        for away, piece in [(0, shard), *far.items()]:
             far[away ^ bit] = swap(piece, "dp", bit)
-    for away, piece in far.items():
-        found[away] = piece
-        found[away ^ bits[0]] = swap(after(piece, *second), "dp", bits[0])
-    return [found[away] for away in range(len(found))], far
-
-
-def scatter_dp(keep, send):
-    bits = powers(lax.axis_size("dp"))
-    total = keep.astype(F32) + swap(send, "dp", bits[0]).astype(F32)
-    order = [("dp", b) for b in bits[1:]]
-    total = total.reshape([2] * len(order) + list(total.shape[1:]))
-    return scatter_steps((total, order[::-1]), order)[0]
+    return far
+
+
+def dp_pieces(shard, own, far, near):
+    core = powers(lax.axis_size("dp"))[0]
+    found = {0: shard, core: own, **far}
+    found.update({away ^ core: piece for away, piece in near.items()})
+    return [found[away] for away in range(len(found))]
+
+
+def x_steps():
+    return [("dp", b) for b in powers(lax.axis_size("dp"))[1:]]
+
+
+def scatter_dp_first(addends):
+    order = x_steps()
+    addends = [a.reshape([2] * len(order) + list(a.shape[1:])) for a in addends]
+    return away_part(addends, order[::-1], order[0])
+
+
+def scatter_dp(addends, first):
+    order = x_steps()
+    lead = order[::-1]
+    addends = [a.reshape([2] * len(order) + list(a.shape[1:])) for a in addends]
+    arrived = [swap(first, *order[0])]
+    for at, step in enumerate(order[1:]):
+        addends, lead = scatter_rest(addends, lead, order[at], arrived[-1])
+        arrived.append(scatter_step(addends, lead, step))
+    return arrived
+
+
+def scatter_dp_total(addends, arrived):
+    order = x_steps()
+    lead = order[::-1]
+    addends = [a.reshape([2] * len(order) + list(a.shape[1:])) for a in addends]
+    for step, got in zip(order, arrived):
+        addends, lead = scatter_rest(addends, lead, step, got)
+    return total(addends)
 
 
 LIMIT = 56 * 1024 * 1024
@@ -333,27 +371,14 @@
     outgrad_ref[...] = dot(branch, context_ref[...], 0, 0).astype(BF)
 
 
-def attention_back_kernel(
-    place_ref,
-    proj_ref,
-    gctx_ref,
-    normed_ref,
-    gproj_ref,
-    keep0_ref,
-    keep1_ref,
-    keep2_ref,
-    send0_ref,
-    send1_ref,
-    send2_ref,
-    gk_acc,
-    gv_acc,
-):
+def pairs_back(proj_ref, gctx_ref, gproj_ref, gk_acc, gv_acc, first, last, shift, spread):
     length, width = gctx_ref.shape
     size = min(QUERY_BLOCK, length)
     seen = causal(size)
 
     def one_pair(pair, carry):
         q_at, k_at, v_at = (pair_columns(pair, part, width) for part in range(3))
+        q_to, k_to, v_to = (pair_columns(pair - shift, part, spread) for part in range(3))
         gk_acc[...] = jnp.zeros_like(gk_acc)
         gv_acc[...] = jnp.zeros_like(gv_acc)
         for block in range(length // size):
@@ -382,12 +407,50 @@
                     gv_acc[s, :] += dot(p.astype(BF), gmine, 0, 0)
                 grads.append(gquery * SCALE)
             lane = lax.broadcasted_iota(jnp.int32, grads[0].shape, 1)
-            gproj_ref[rows, q_at] = jnp.where(lane < HEAD_DIM, grads[0], grads[1]).astype(BF)
-        gproj_ref[:, k_at] = gk_acc[...].astype(BF)
-        gproj_ref[:, v_at] = gv_acc[...].astype(BF)
+            gproj_ref[rows, q_to] = jnp.where(lane < HEAD_DIM, grads[0], grads[1]).astype(BF)
+        gproj_ref[:, k_to] = gk_acc[...].astype(BF)
+        gproj_ref[:, v_to] = gv_acc[...].astype(BF)
         return carry
 
-    lax.fori_loop(0, HEADS // 2, one_pair, 0)
+    lax.fori_loop(first, last, one_pair, 0)
+
+def attention_first_kernel(proj_ref, gctx_ref, gproj_ref, gk_acc, gv_acc):
+    spread = gproj_ref.shape[1] // 3
+    last = spread // (2 * HEAD_DIM)
+    pairs_back(proj_ref, gctx_ref, gproj_ref, gk_acc, gv_acc, 0, last, 0, spread)
+
+
+def attention_back_kernel(
+    place_ref,
+    proj_ref,
+    gctx_ref,
+    normed_ref,
+    before_ref,
+    gproj_ref,
+    keep0_ref,
+    keep1_ref,
+    keep2_ref,
+    send0_ref,
+    send1_ref,
+    send2_ref,
+    gk_acc,
+    gv_acc,
+):
+    width = gctx_ref.shape[1]
+    done = before_ref.shape[1] // 3
+    for part in range(3):
+        gproj_ref[:, part * width : part * width + done] = before_ref[
+            :, part * done : (part + 1) * done
+        ]
+    first = done // (2 * HEAD_DIM)
+    pairs_back(proj_ref, gctx_ref, gproj_ref, gk_acc, gv_acc, first, HEADS // 2, 0, width)
+    length, width = gctx_ref.shape
+    size = min(QUERY_BLOCK, length)
+    seen = causal(size)
+
+    def one_pair(pair, carry):
+        q_at, k_at, v_at = (pair_columns(pair, part, width) for part in range(3))
+        gk
     third = width // 3
     core = place_ref[0] % 2
     halves, rows, _ = keep0_ref.shape
@@ -430,8 +493,8 @@
 def expert_kernel(train, steps, pieces, place_ref, mine_ref, rows_ref, grads4_ref, router_ref, *rest):
     ups, downs, rest = rest[:pieces], rest[pieces : 2 * pieces], rest[2 * pieces :]
     if train:
-        gated_ref, gin_ref, rgrad_ref, upkeep_ref, upsend_ref, downkeep_ref, downsend_ref = rest[:7]
-        rest = rest[7:]
+        gated_ref, gin_ref, rgrad_ref, hid_ref, gpre_ref, scaled_ref = rest[:6]
+        rest = rest[6:]
     else:
         gated_ref, gin_ref, rgrad_ref = rest[:3]
         rest = rest[3:]
@@ -484,26 +547,12 @@
     gin_acc[...] += dot(gpre, up, 1, 1)
 
     if train:
-        core = place_ref[0] % 2
-        grad_up = dot(rows, gpre, 0, 0).astype(BF)
-        for pair in range(pieces // 2):
-            first = grad_up[2 * pair * up_rows : (2 * pair + 1) * up_rows]
-            second = grad_up[(2 * pair + 1) * up_rows : (2 * pair + 2) * up_rows]
-            upkeep_ref[pair] = jnp.where(core == 0, first, second)
-            upsend_ref[pair] = jnp.where(core == 0, second, first)
-        grad_down = dot(hid, scaled[...], 0, 0).astype(BF)
-        inside = tile // down_rows
-        for at in range(inside):
-            block = grad_down[at * down_rows : (at + 1) * down_rows]
-            owner = j * inside + at
-
-            @pl.when(owner % 2 == core)
-            def _():
-                downkeep_ref[owner // 2] = block
-
-            @pl.when(owner % 2 != core)
-            def _():
-                downsend_ref[owner // 2] = block
+        hid_ref[...] = hid
+        gpre_ref[...] = gpre
+
+        @pl.when(j == 0)
+        def _():
+            scaled_ref[...] = scaled[...]
 
     @pl.when(j == steps - 1)
     def _():
@@ -536,12 +585,8 @@
     outs = [((n, d), BF), ((n, d), BF), ((128, d), F32)]
     out_specs = [all_of((n, d)), all_of((n, d)), all_of((128, d))]
     if train:
-        half = pieces // 2
-        up_shape = (half, d // pieces, f)
-        down_shape = (half, f // pieces, d)
-        outs += [(up_shape, BF)] * 2 + [(down_shape, BF)] * 2
-        out_specs += [pl.BlockSpec((half, d // pieces, tile), lambda j: (0, 0, j))] * 2
-        out_specs += [all_of(down_shape)] * 2
+        outs += [((n, f), BF)] * 2 + [((n, d), BF)]
+        out_specs += [pl.BlockSpec((n, tile), lambda j: (0, j))] * 2 + [all_of((n, d))]
     args = [owners, mine, rows, grads, router_pad, *ups, *downs]
     return pl.pallas_call(
         functools.partial(expert_kernel, train, steps, pieces),
@@ -567,9 +612,70 @@
             pltpu.SemaphoreType.DMA((2, pieces)),
         ],
         compiler_params=pltpu.CompilerParams(vmem_limit_bytes=LIMIT),
-        cost_estimate=cost(40 if train else 27),
+        cost_estimate=cost(29),
         name="expert_new" if train else "expert_old",
     )(*args)
+
+
+def weight_grads_kernel(
+    pieces,
+    place_ref,
+    rows_ref,
+    scaled_ref,
+    hid_ref,
+    gpre_ref,
+    upkeep_ref,
+    upsend_ref,
+    downkeep_ref,
+    downsend_ref,
+):
+    j = pl.program_id(0)
+    core = place_ref[0] % 2
+    half, up_rows, tile = upkeep_ref.shape
+    down_rows = downkeep_ref.shape[1]
+    grad_up = dot(rows_ref[...], gpre_ref[...], 0, 0).astype(BF)
+    for pair in range(half):
+        first = grad_up[2 * pair * up_rows : (2 * pair + 1) * up_rows]
+        second = grad_up[(2 * pair + 1) * up_rows : (2 * pair + 2) * up_rows]
+        upkeep_ref[pair] = jnp.where(core == 0, first, second)
+        upsend_ref[pair] = jnp.where(core == 0, second, first)
+    grad_down = dot(hid_ref[...], scaled_ref[...], 0, 0).astype(BF)
+    inside = tile // down_rows
+    for at in range(inside):
+        block = grad_down[at * down_rows : (at + 1) * down_rows]
+        owner = j * inside + at
+
+        @pl.when(owner % 2 == core)
+        def _():
+            downkeep_ref[owner // 2] = block
+
+        @pl.when(owner % 2 != core)
+        def _():
+            downsend_ref[owner // 2] = block
+
+
+def weight_grads_call(owners, rows, scaled, hidden, grad_pre):
+    n, d = rows.shape
+    f = hidden.shape[1]
+    pieces = owners.shape[0]
+    half = pieces // 2
+    tile = max(d, f // pieces)
+    one = pl.Buffered(buffer_count=1)
+    up_shape = (half, d // pieces, f)
+    down_shape = (half, f // pieces, d)
+    flat = pl.BlockSpec((n, d), lambda j: (0, 0), pipeline_mode=one)
+    tiled = pl.BlockSpec((n, tile), lambda j: (0, j))
+    return pl.pallas_call(
+        functools.partial(weight_grads_kernel, pieces),
+        grid=(f // tile,),
+        in_specs=[pl.BlockSpec(memory_space=pltpu.SMEM), flat, flat, tiled, tiled],
+        out_specs=[pl.BlockSpec((half, d // pieces, tile), lambda j: (0, 0, j))] * 2
+        + [pl.BlockSpec(down_shape, lambda j: (0, 0, 0), pipeline_mode=one)] * 2,
+        out_shape=[whole((up_shape, BF))] * 2 + [whole((down_shape, BF))] * 2,
+        compiler_params=pltpu.CompilerParams(vmem_limit_bytes=LIMIT),
+        cost_estimate=cost(14),
+        name="weight_grads",
+    )(owners, rows, scaled, hidden, grad_pre)
 
 
 def shards(
@@ -613,6 +719,7 @@
         rows = [in_t[:, cols], out_t[:, cols]] + ([small] if p == 0 else [])
         states.append((jnp.concatenate(rows, axis=0), []))
     states = [gather_steps(states[p], ways[p][:2]) for p in range(3)]
+    shards_dp = [old_w1[0], old_w2[0], new_w1[0], new_w2[0]]
     early = [state[0] for state in states]
     states = [gather_steps(states[p], ways[p][2:-1]) for p in range(3)]
     between = [state[0] for state in states]
@@ -664,12 +771,13 @@
         member_rows,
     )
     owners = lax.axis_index("dp") ^ jnp.arange(lax.axis_size("dp"), dtype=jnp.int32)
-    new_ups, far_up = dp_pieces(new_w1[0], (between,), ())
-    new_downs, far_down = dp_pieces(new_w2[0], (between,), ())
-    old_ups, _ = dp_pieces(old_w1[0], (between, far_up), ())
-    old_downs, _ = dp_pieces(old_w2[0], (between, far_up), ())
-    rold = send(rold, grads, far_up, far_down)
-    rnew = send(rnew, rold)
+    far = [dp_far(after(shard, between)) for shard in shards_dp[:2]]
+    far.append(dp_far(after(shards_dp[2], between, far)))
+    far.append(dp_far(after(shards_dp[3], between, far)))
+    near = [{away: core_swap(piece) for away, piece in f.items()} for f in far[:3]]
+    rold = send(rold, grads, far[:2])
+    own = [core_swap(after(shard, grads)) for shard in shards_dp]
+    rnew = send(rnew, rold, near, own)
 
     lane = lax.broadcasted_iota(jnp.int32, (8, 128), 1)
     line = lax.broadcasted_iota(jnp.int32, (8, 128), 0)
@@ -677,20 +785,24 @@
     def chosen(expert):
         return jnp.where(line == 0, (lane == expert).astype(F32), F32(experts))
 
+    pieces = [dp_pieces(shards_dp[i], own[i], far[i], near[i]) for i in range(2)]
     old_gated, old_in, old_router = expert_call(
-        owners, chosen(2 * me), rold, grads, router_pad, old_ups, old_downs, False
-    )
+        owners, chosen(2 * me), rold, grads, router_pad, *pieces, False
+    )
+    near.append({away: core_swap(after(piece, old_in)) for away, piece in far[3].items()})
+    pieces = [dp_pieces(shards_dp[i], own[i], far[i], near[i]) for i in range(2, 4)]
     rnew, old_in = lax.optimization_barrier((rnew, old_in))
     old_in = send(old_in, rnew)
-    new_gated, new_in, new_router, up_keep, up_send, down_keep, down_send = expert_call(
-        owners, chosen(2 * me + 1), rnew, grads, router_pad, new_ups, new_downs, True
+    new_gated, new_in, new_router, hidden, grad_pre, scaled = expert_call(
+        owners, chosen(2 * me + 1), rnew, grads, router_pad, *pieces, True
+    )
+    up_keep, up_send, down_keep, down_send = weight_grads_call(
+        owners, rnew, scaled, hidden, grad_pre
     )
     new_in = send(new_in, old_in)
+    ups = [up_keep, core_swap(after(up_send, old_in))]
+    downs = [down_keep, core_swap(after(down_send, old_in))]
     old_gated = send(old_gated, new_in)
-    new_gated = send(new_gated, old_gated)
-    up_send, down_send = after((up_send, down_send), old_in)
-    new_w1_grad = scatter_dp(up_keep, up_send)[None]
-    new_w2_grad = scatter_dp(down_keep, down_send)[None]
     router_part = (old_router + new_router)[:experts]
 
     gmid, gctx, out_grad, sums_two = plain_call(
@@ -703,7 +815,7 @@
         ],
         [],
         "branch_backward",
-        0,
+        8,
         old_in,
         new_in,
         by_member,
@@ -713,46 +825,52 @@
         *out_parts,
         vectors,
     )
+    accumulators = [pltpu.VMEM((length, 2 * HEAD_DIM), F32)] * 2
+    (gfirst,) = plain_call(
+        attention_first_kernel,
+        [((length, 3 * width // 2), BF)],
+        accumulators,
+        "attention_backward_first",
+        40,
+        proj,
+        gctx,
+    )
+    new_gated = send(new_gated, old_gated, gfirst)
+    ups_first, downs_first = [scatter_dp_first(after(sums, gctx)) for sums in (ups, downs)]
+    ups_x = scatter_dp(ups, ups_first)
+    downs_x = scatter_dp(downs, downs_first)
+    gfirst = after(gfirst, ups_x)
     half = lax.axis_size("dp") // 2
     gproj, *split = plain_call(
         attention_back_kernel,
         [((length, 3 * width), BF)] + [((half, 3 * width // (2 * half), third), BF)] * 6,
-        [pltpu.VMEM((length, 2 * HEAD_DIM), F32)] * 2,
+        accumulators,
         "attention_backward",
-        0,
+        40,
         owners,
         proj,
         gctx,
         normed,
+        gfirst,
     )
     input_grad, sums_one = plain_call(
         input_kernel,
         [((length, width), F32), ((8, width), F32)],
         [],
-        "input_backward", 0,
+        "input_backward", 20,
         gproj,
         *in_parts,
         block_input,
         vectors,
         gmid,
     )
-    (mixed,) = plain_call(
-        mixed_kernel,
-        [((length, width), BF)],
-        [],
-        "mixed_output", 0,
-        old_gated,
-        new_gated,
-        by_member,
-        middle,
-    )
     lead = canonical()
     core = [("dp", powers(lax.axis_size("dp"))[0])]
     states = []
+    left = [step for step in lead if step != core[0]]
     for keep, away in zip(split[:3], split[3:]):
-        total = keep.astype(F32) + swap(away, *core[0]).astype(F32)
-        left = [step for step in lead if step != core[0]]
-        states.append((total.reshape([2] * len(left) + [in_share, third]), left))
+        addends = [keep, swap(away, *core[0])]
+        states.append([a.reshape([2] * len(left) + [in_share, third]) for a in addends])
     small_grads = jnp.concatenate([sums_one[:2], sums_two[:2], router_part], axis=0)
     small_grads = small_grads.reshape(lines, devices, share).transpose(1, 0, 2)
     small_grads = small_grads.reshape(devices, 1, lines * share).astype(BF)
@@ -763,11 +881,38 @@
         axis=1,
     )
     rest = rest.reshape([2] * len(lead) + list(rest.shape[1:]))
-    states.append(scatter_steps((rest, lead), core))
-    held = after([values for values, _ in states], old_gated, new_gated)
-    sums = [
-        scatter_steps((held[p], states[p][1]), scatter_ways[p])[0] for p in range(len(states))
-    ]
+    got = scatter_step([rest], lead, core[0])
+    states.append(scatter_rest([rest], lead, core[0], got)[0])
+    states = after(states, old_gated, new_gated, downs_x)
+    lefts = [left] * len(states)
+    for at in range(len(left)):
+        arrived = [
+            scatter_step(state, left, way[at])
+            for state, left, way in zip(states, lefts, scatter_ways)
+        ]
+        if at == 0:
+            (mixed,) = plain_call(
+                mixed_kernel,
+                [((length, width), BF)],
+                [],
+                "mixed_output", 5,
+                *after((old_gated, new_gated), arrived),
+                by_member,
+                middle,
+            )
+        if at == 1:
+            (ups, downs, ups_x, downs_x), _ = lax.optimization_barrier(
+                ((ups, downs, ups_x, downs_x), arrived)
+            )
+            new_w1_grad = scatter_dp_total(ups, ups_x)[None]
+            new_w2_grad = scatter_dp_total(downs, downs_x)[None]
+        pairs = [
+            scatter_rest(state, left, way[at], got)
+            for state, left, way, got in zip(states, lefts, scatter_ways, arrived)
+        ]
+        states = [pair[0] for pair in pairs]
+        lefts = [pair[1] for pair in pairs]
+    sums = [total(state) for state in states]
     attn_in_grad = jnp.concatenate(sums[:3], axis=1).T
     attn_out_grad = sums[3][:share].T
     small_grads = sums[3][share:].reshape(-1)[: lines * share].reshape(lines, share)

time: 464 us -> 418 us (0.901)
  waiting for transfers between devices: 155 us -> 104 us
  local copies, waits for them, and re-layouts: 35.2 us -> 24.8 us
  Pallas kernels: 153 us -> 162 us
  other arithmetic: 33.1 us -> 40.6 us
    all_to_all x7, waiting for transfers between devices: 84.6 us -> 26.7 us  [move(): lax.all_to_all(block, 'expert', split_axis=0, concat_axis=0, tiled=True)]
    pallas_call x0 -> x1, Pallas kernels: none -> 16.5 us  [weight_grads_call(): pl.pallas_call(functools.partial(weight_grads_kernel, pieces), grid=(f //...]
    convert_element_type x0 -> x19, other arithmetic: none -> 16.4 us  [the longest x18 16.4 us: away_part(): return send.astype(BF)]
    add x22 -> x5, other arithmetic: 15.1 us -> 3.59 us  [total(): found = found + addend.astype(F32)]
    pallas_call x2, Pallas kernels: 68 us -> 57 us  [expert_call(): pl.pallas_call(functools.partial(expert_kernel, train, steps, pieces), gr...]
    unnamed x64 -> x68, local copies, waits for them, and re-layouts: 13.2 us -> 5.81 us
    ppermute x51, waiting for transfers between devices: 70.8 us -> 77.4 us  [swap(): return lax.ppermute(values, axis, [(i, i ^ bit) for i in range(count)])]
    pallas_call x6 -> x7, Pallas kernels: 84.8 us -> 88.3 us  [plain_call(): pl.pallas_call(body, out_shape=[whole(o) for o in outs], in_specs=[space]...]
  transfers between devices with their start and end apart: 58 -> 58, of which waited for: 26 -> 25; matrix products, arithmetic and copies ran while one was open for 12% -> 13% of each run, Pallas kernels for 32% -> 39%
where the time goes in v3:
time: 418 us; the launch traced here: 412 us
  Pallas kernels  162 us (39%)
  waiting for transfers between devices  104 us (25%)
  starting transfers between devices  78.8 us (19%)
  other arithmetic  40.6 us (10%)
  local copies, waits for them, and re-layouts  24.8 us (6%)
    pallas_call x7, Pallas kernels, plain_call(): pl.pallas_call(body, out_shape=[whole(o) for o in outs], in_specs=[space]...  88.3 us
    ppermute x51, waiting for transfers between devices, swap(): return lax.ppermute(values, axis, [(i, i ^ bit) for i in range(count)])  77.4 us
    pallas_call x2, Pallas kernels, expert_call(): pl.pallas_call(functools.partial(expert_kernel, train, steps, pieces), gr...  57 us
    ppermute x51, starting transfers between devices, swap(): return lax.ppermute(values, axis, [(i, i ^ bit) for i in range(count)])  46.7 us
    all_to_all x7, starting transfers between devices, move(): lax.all_to_all(block, 'expert', split_axis=0, concat_axis=0, tiled=True)  32 us
    all_to_all x7, waiting for transfers between devices, move(): lax.all_to_all(block, 'expert', split_axis=0, concat_axis=0, tiled=True)  26.7 us
    pallas_call x1, Pallas kernels, weight_grads_call(): pl.pallas_call(functools.partial(weight_grads_kernel, pieces), grid=(f //...  16.5 us
    convert_element_type x18, other arithmetic, away_part(): return send.astype(BF)  16.4 us
  transfers between devices with their start and end apart: 58, of which 25 were waited for; matrix products, arithmetic and copies ran while one was open for 13% of the time, Pallas kernels for 39%

profile of v3, /device:TPU:0, one launch (start us, length us, event | category | flops | bytes accessed | tf_op | source)
XLA Modules:
  0.0 412.0 jit_solution(8732094962518284717)
XLA Ops:
  24.9 4.3 %place_grads.1 = bf16[1792,768]{1,0:T(8,128)(2,1)} custom-call(s32[8,512]{1,0:T(8,128)} %pad.29.clone.target_ref, bf16[512,768]{1,0:T(8,128)(2,1)} %cot_ref.1), custom_call_target="tpu_custom_call" | custom-call | flops 1000000000 | tf_op jit(solution)/shard_map/place_grads/pallas_call | solution.py:185
  34.9 4.2 %collective-permute-done.8 = bf16[2,2,2,96,256]{4,3,2,1,0:T(8,128)(2,1)S(1)} collective-permute-done((bf16[2,2,2,96,256]{4,3,2,1,0:T(8,128)(2,1)S(1)}, bf16[2,2,2,96,256]{4,3,2,1,0:T(8,128)(2,1)S(1)}, u32[]{:S(2)}, u32[]{:S(2)}) %collective-permute-start.8) | collective-permute-done | bytes 393248 | tf_op jit(solution)/shard_map/ppermute | solution.py:31
  45.3 4.7 %all-to-all-start = ((bf16[8,2,112,768]{3,2,1,0:T(8,128)(2,1)}), bf16[8,2,112,768]{3,2,1,0:T(8,128)(2,1)}, u32[]{:S(2)}, u32[]{:S(2)}) async-start(bf16[8,2,112,768]{3,2,1,0:T(8,128)(2,1)} %bitcast.333), calls=%async_computation | async-start | bytes 5505024 | tf_op jit(solution)/shard_map/all_to_all | solution.py:744
  64.0 26.8 %attention_forward.1 = (bf16[512,768]{1,0:T(8,128)(2,1)}, bf16[512,2304]{1,0:T(8,128)(2,1)}, bf16[512,768]{1,0:T(8,128)(2,1)}, f32[512,768]{1,0:T(8,128)}, bf16[...) custom-call(bf16[512,768]{1,0:T(8,128)(2,1)} %x_ref.3, bf16[2304,256]{1,0:T(8,128)(2,1)} %bitcast.346, ...), custom_call_target="tpu_custom_call" | custom-call | flops 6750000128 | tf_op jit(solution)/shard_map/attention_forward/pallas_call | solution.py:185
  90.8 14.5 %collective-permute-done.16.rest_6_ = bf16[768,768]{1,0:T(8,128)(2,1)} collective-permute-done((bf16[768,768]{1,0:T(8,128)(2,1)}, bf16[768,768]{1,0:T(8,128)(2,1)}, u32[]{:S(2)}, u32[]{:S(2)}) %collective-permute-start.16) | collective-permute-done | bytes 1179680 | tf_op jit(solution)/shard_map/ppermute | solution.py:31
  105.3 4.9 %all-to-all-done.grads4_ref = bf16[8,2,112,768]{3,2,1,0:T(8,128)(2,1)} async-done(((bf16[8,2,112,768]{3,2,1,0:T(8,128)(2,1)}), bf16[8,2,112,768]{3,2,1,0:T(8,128)(2,1)}, u32[]{:S(2)}, u32[]{:S(2)}) %all-to-all-start) | async-done | bytes 2752544 | tf_op jit(solution)/shard_map/all_to_all | solution.py:744
  110.2 3.6 all-to-all-start.1
  115.6 26.1 %collective-permute-done.21.rest_2_ = bf16[192,3072]{1,0:T(8,128)(2,1)S(1)} collective-permute-done((bf16[192,3072]{1,0:T(8,128)(2,1)}, bf16[192,3072]{1,0:T(8,128)(2,1)S(1)}, u32[]{:S(2)}, u32[]{:S(2)}) %collective-permute-start.21) | collective-permute-done | bytes 1179680 | tf_op jit(solution)/shard_map/ppermute | solution.py:31
  144.6 5.1 %collective-permute-done.17.rest_1_ = bf16[192,3072]{1,0:T(8,128)(2,1)S(1)} collective-permute-done((bf16[192,3072]{1,0:T(8,128)(2,1)S(1)}, bf16[192,3072]{1,0:T(8,128)(2,1)S(1)}, u32[]{:S(2)}, u32[]{:S(2)}) %collective-permute-start.17) | collective-permute-done | bytes 1179680 | tf_op jit(solution)/shard_map/ppermute | solution.py:31
  152.6 6.3 %all-to-all-start.2 = ((bf16[8,112,768]{2,1,0:T(8,128)(2,1)}), bf16[8,112,768]{2,1,0:T(8,128)(2,1)S(1)}, u32[]{:S(2)}, u32[]{:S(2)}) async-start(bf16[8,112,768]{2,1,0:T(8,128)(2,1)} %bitcast.63), calls=%async_computation.2 | async-start | bytes 2752512 | tf_op jit(solution)/shard_map/all_to_all | solution.py:744
  162.1 27.3 %expert_old.1 = (bf16[896,768]{1,0:T(8,128)(2,1)}, bf16[896,768]{1,0:T(8,128)(2,1)}, f32[128,768]{1,0:T(8,128)}) custom-call(s32[4]{0:T(128)} %iota_xor_fusion.place_ref, f32[8,128]{1,0:T(8,128)} %get-tuple-element.204.mine_ref, bf16[896,768]{1,0:T(8,128)(2,1)} %bitcast.336, bf16[8,2,112,768]{3,2,1,0:T(8,128)(2,1)} %all-to-all-done.grads4_ref, ...), custom_call_target="tpu_custom_call" | custom-call | flops 7249999872 | tf_op jit(solution)/shard_map/expert_old/pallas_call | solution.py:591
  191.9 3.8 all-to-all-start.3
  199.9 29.7 %expert_new.1 = (bf16[896,768]{1,0:T(8,128)(2,1)}, bf16[896,768]{1,0:T(8,128)(2,1)}, f32[128,768]{1,0:T(8,128)}, bf16[896,3072]{1,0:T(8,128)(2,1)}, bf16[896,3072]{1,0:T(8,128)(2,1)}, /*index=5*/bf16[896,768]{1,0:T(8,128)(2,1)}) custom-call(s32[4]{0:T(128)} %iota_xor_fusion.place_ref, f32[8,128]{1,0:T(8,128)} %get-tuple-element.203.mine_ref, ...), custom_call_target="tpu_custom_call" | custom-call | flops 7249999872 | tf_op jit(solution)/shard_map/expert_new/pallas_call | solution.py:591
  229.6 6.0 %all-to-all-start.4 = ((bf16[8,112,768]{2,1,0:T(8,128)(2,1)}), bf16[8,112,768]{2,1,0:T(8,128)(2,1)S(1)}, u32[]{:S(2)}, u32[]{:S(2)}) async-start(bf16[8,112,768]{2,1,0:T(8,128)(2,1)} %bitcast.341), calls=%async_computation.4 | async-start | bytes 2752512 | tf_op jit(solution)/shard_map/all_to_all | solution.py:744
  235.6 16.5 %weight_grads.1 = (bf16[2,192,3072]{2,1,0:T(8,128)(2,1)}, bf16[2,192,3072]{2,1,0:T(8,128)(2,1)}, bf16[2,768,768]{2,1,0:T(8,128)(2,1)}, bf16[2,768,768]{2,1,0:T(8,128)(2,1)}) custom-call(s32[4]{0:T(128)} %iota_xor_fusion.place_ref, bf16[896,768]{1,0:T(8,128)(2,1)} %bitcast.327, bf16[896,768]{1,0:T(8,128)(2,1)} %get-tuple-element.115.scaled_ref, ...), custom_call_target="tpu_custom_call" | custom-call | flops 3500000000 | tf_op jit(solution)/shard_map/weight_grads/pallas_call | solution.py:668
  252.7 16.1 %all-to-all-done.4 = bf16[8,112,768]{2,1,0:T(8,128)(2,1)S(1)} async-done(((bf16[8,112,768]{2,1,0:T(8,128)(2,1)}), bf16[8,112,768]{2,1,0:T(8,128)(2,1)S(1)}, u32[]{:S(2)}, u32[]{:S(2)}) %all-to-all-start.4) | async-done | bytes 1376288 | tf_op jit(solution)/shard_map/all_to_all | solution.py:744
  269.8 3.9 all-to-all-start.5
  273.7 8.8 %branch_backward.1 = (f32[512,768]{1,0:T(8,128)}, bf16[512,768]{1,0:T(8,128)(2,1)}, bf16[768,768]{1,0:T(8,128)(2,1)}, f32[8,768]{1,0:T(8,128)}) custom-call(bf16[896,768]{1,0:T(8,128)(2,1)} %bitcast.337, bf16[896,768]{1,0:T(8,128)(2,1)} %bitcast.339, s32[512,2]{1,0:T(8,128)} %copy-done.6, bf16[512,768]{1,0:T(8,128)(2,1)} %cot_ref.1, ...), custom_call_target="tpu_custom_call" | custom-call | flops 2000000000 | tf_op jit(solution)/shard_map/branch_backward/pallas_call | solution.py:185
  287.1 16.2 %attention_backward_first.1.before_ref = bf16[512,1152]{1,0:T(8,128)(2,1)} custom-call(bf16[512,2304]{1,0:T(8,128)(2,1)} %get-tuple-element.109.proj_ref, bf16[512,768]{1,0:T(8,128)(2,1)} %get-tuple-element.112.gctx_ref), custom_call_target="tpu_custom_call" | custom-call | flops 10000000000 | tf_op jit(solution)/shard_map/attention_backward_first/pallas_call | solution.py:185
  306.6 3.6 all-to-all-start.6
  315.0 19.9 %attention_backward.1 = (bf16[512,2304]{1,0:T(8,128)(2,1)}, bf16[2,576,256]{2,1,0:T(8,128)(2,1)}, bf16[2,576,256]{2,1,0:T(8,128)(2,1)}, bf16[2,576,256]{2,1,0:T(...) custom-call(s32[4]{0:T(128)} %iota_xor_fusion.place_ref, ...), custom_call_target="tpu_custom_call" | custom-call | flops 10000000000 | tf_op jit(solution)/shard_map/attention_backward/pallas_call | solution.py:185
  334.9 7.1 %input_backward.1 = (f32[512,768]{1,0:T(8,128)}, f32[8,768]{1,0:T(8,128)}) custom-call(bf16[512,2304]{1,0:T(8,128)(2,1)} %get-tuple-element.131.gproj_ref, bf16[2304,256]{1,0:T(8,128)(2,1)} %bitcast.347, bf16[2304,256]{1,0:T(8,128)(2,1)} %bitcast.345, bf16[2304,256]{1,0:T(8,128)(2,1)} %bitcast.343, bf16[512,768]{1,0:T(8,128)(2,1)} %x_ref.3, ...), custom_call_target="tpu_custom_call" | custom-call | flops 5000000000 | tf_op jit(solution)/shard_map/input_backward/pallas_call | solution.py:185
  375.1 5.2 %mixed_output.1 = bf16[512,768]{1,0:T(8,128)(2,1)} custom-call(bf16[896,768]{1,0:T(8,128)(2,1)} %bitcast.324, bf16[896,768]{1,0:T(8,128)(2,1)} %bitcast.325, s32[512,2]{1,0:T(8,128)} %copy-done.6, f32[512,768]{1,0:T(8,128)} %get-tuple-element.110.middle_ref), custom_call_target="tpu_custom_call" | custom-call | flops 1250000000 | tf_op jit(solution)/shard_map/mixed_output/pallas_call | solution.py:185
  393.3 3.6 fusion.1
  (283 shorter events, 141.7 us)
Async XLA Ops:
  45.3 65.0 %all-to-all-start = ((bf16[8,2,112,768]{3,2,1,0:T(8,128)(2,1)}), bf16[8,2,112,768]{3,2,1,0:T(8,128)(2,1)}, u32[]{:S(2)}, u32[]{:S(2)}) async-start(bf16[8,2,112,768]{3,2,1,0:T(8,128)(2,1)} %bitcast.333), calls=%async_computation | async-start | bytes 5505024 | tf_op jit(solution)/shard_map/all_to_all | solution.py:744
  51.4 39.4 %collective-permute-start.15 = (bf16[192,3072]{1,0:T(8,128)(2,1)}, bf16[192,3072]{1,0:T(8,128)(2,1)}, u32[]{:S(2)}, u32[]{:S(2)}) collective-permute-start(bf16[192,3072]{1,0:T(8,128)(2,1)} %bitcast.384), channel_id=1, source_target_pairs={{0,16},{8,24},{16,0},{24,8},{1,17},{9,25},{17,1},{25,9},{2,18},{10... | collective-permute-start | bytes 3538952 | tf_op jit(solution)/shard_map/ppermute | solution.py:31
  52.9 52.4 %collective-permute-start.16 = (bf16[768,768]{1,0:T(8,128)(2,1)}, bf16[768,768]{1,0:T(8,128)(2,1)}, u32[]{:S(2)}, u32[]{:S(2)}) collective-permute-start(bf16[768,768]{1,0:T(8,128)(2,1)} %bitcast.387), channel_id=1, source_target_pairs={{0,16},{8,24},{16,0},{24,8},{1,17},{9,25},{17,1},{25,9},{2,18},{10... | collective-permute-start | bytes 3538952 | tf_op jit(solution)/shard_map/ppermute | solution.py:31
  110.2 42.3 %all-to-all-start.1 = ((bf16[8,112,768]{2,1,0:T(8,128)(2,1)}), bf16[8,112,768]{2,1,0:T(8,128)(2,1)S(1)}, u32[]{:S(2)}, u32[]{:S(2)}) async-start(bf16[8,112,768]{2,1,0:T(8,128)(2,1)} %bitcast.338), calls=%async_computation.1 | async-start | bytes 2752512 | tf_op jit(solution)/shard_map/all_to_all | solution.py:744
  113.9 27.8 %collective-permute-start.21 = (bf16[192,3072]{1,0:T(8,128)(2,1)}, bf16[192,3072]{1,0:T(8,128)(2,1)S(1)}, u32[]{:S(2)}, u32[]{:S(2)}) collective-permute-start(bf16[192,3072]{1,0:T(8,128)(2,1)} %bitcast.390), channel_id=1, source_target_pairs={{0,16},{8,24},{16,0},{24,8},{1,17},{9,25},{17,1},{25,9},{2,18},{10... | collective-permute-start | bytes 3538952 | tf_op jit(solution)/shard_map/ppermute | solution.py:31
  115.1 27.2 %collective-permute-start.18 = (bf16[192,3072]{1,0:T(8,128)(2,1)}, bf16[192,3072]{1,0:T(8,128)(2,1)}, u32[]{:S(2)}, u32[]{:S(2)}) collective-permute-start(bf16[192,3072]{1,0:T(8,128)(2,1)} %collective-permute-done.15.rest_2_), channel_id=1, source_target_pairs={{0,8},{8,0},{16,24},{24,16},{1,9},{9,1},{17,25},{25,17},{2,10},{10... | collective-permute-start | bytes 3538952 | tf_op jit(solution)/shard_map/ppermute | solution.py:31
  115.1 27.7 %collective-permute-start.20 = (bf16[768,768]{1,0:T(8,128)(2,1)}, bf16[768,768]{1,0:T(8,128)(2,1)S(1)}, u32[]{:S(2)}, u32[]{:S(2)}) collective-permute-start(bf16[768,768]{1,0:T(8,128)(2,1)} %collective-permute-done.16.rest_6_), channel_id=1, source_target_pairs={{0,8},{8,0},{16,24},{24,16},{1,9},{9,1},{17,25},{25,17},{2,10},{10... | collective-permute-start | bytes 3538952 | tf_op jit(solution)/shard_map/ppermute | solution.py:31
  152.6 39.3 %all-to-all-start.2 = ((bf16[8,112,768]{2,1,0:T(8,128)(2,1)}), bf16[8,112,768]{2,1,0:T(8,128)(2,1)S(1)}, u32[]{:S(2)}, u32[]{:S(2)}) async-start(bf16[8,112,768]{2,1,0:T(8,128)(2,1)} %bitcast.63), calls=%async_computation.2 | async-start | bytes 2752512 | tf_op jit(solution)/shard_map/all_to_all | solution.py:744
  161.1 34.7 %collective-permute-start.25 = (bf16[768,768]{1,0:T(8,128)(2,1)}, bf16[768,768]{1,0:T(8,128)(2,1)}, u32[]{:S(2)}, u32[]{:S(2)}) collective-permute-start(bf16[768,768]{1,0:T(8,128)(2,1)} %bitcast.394), channel_id=1, source_target_pairs={{0,16},{8,24},{16,0},{24,8},{1,17},{9,25},{17,1},{25,9},{2,18},{10... | collective-permute-start | bytes 3538952 | tf_op jit(solution)/shard_map/ppermute | solution.py:31
  191.9 37.7 %all-to-all-start.3 = ((bf16[8,112,768]{2,1,0:T(8,128)(2,1)}), bf16[8,112,768]{2,1,0:T(8,128)(2,1)S(1)}, u32[]{:S(2)}, u32[]{:S(2)}) async-start(bf16[8,112,768]{2,1,0:T(8,128)(2,1)} %bitcast.340), calls=%async_computation.3 | async-start | bytes 2752512 | tf_op jit(solution)/shard_map/all_to_all | solution.py:744
  229.6 39.1 %all-to-all-start.4 = ((bf16[8,112,768]{2,1,0:T(8,128)(2,1)}), bf16[8,112,768]{2,1,0:T(8,128)(2,1)S(1)}, u32[]{:S(2)}, u32[]{:S(2)}) async-start(bf16[8,112,768]{2,1,0:T(8,128)(2,1)} %bitcast.341), calls=%async_computation.4 | async-start | bytes 2752512 | tf_op jit(solution)/shard_map/all_to_all | solution.py:744
  252.1 30.4 %collective-permute-start.27 = (bf16[2,192,3072]{2,1,0:T(8,128)(2,1)}, bf16[2,192,3072]{2,1,0:T(8,128)(2,1)}, u32[]{:S(2)}, u32[]{:S(2)}) collective-permute-start(bf16[2,192,3072]{2,1,0:T(8,128)(2,1)} %get-tuple-element.120), channel_id=1, source_target_pairs={{0,8},{8,0},{16,24},{24,16},{1,9},{9,1},{17,25},{25,17},{2,10},{10... | collective-permute-start | bytes 7077896 | tf_op jit(solution)/shard_map/ppermute | solution.py:31
  252.2 34.9 %collective-permute-start.33 = (bf16[2,768,768]{2,1,0:T(8,128)(2,1)}, bf16[2,768,768]{2,1,0:T(8,128)(2,1)}, u32[]{:S(2)}, u32[]{:S(2)}) collective-permute-start(bf16[2,768,768]{2,1,0:T(8,128)(2,1)} %get-tuple-element.139), channel_id=1, source_target_pairs={{0,8},{8,0},{16,24},{24,16},{1,9},{9,1},{17,25},{25,17},{2,10},{10... | collective-permute-start | bytes 7077896 | tf_op jit(solution)/shard_map/ppermute | solution.py:31
  269.8 36.8 %all-to-all-start.5 = ((bf16[8,112,768]{2,1,0:T(8,128)(2,1)}), bf16[8,112,768]{2,1,0:T(8,128)(2,1)S(1)}, u32[]{:S(2)}, u32[]{:S(2)}) async-start(bf16[8,112,768]{2,1,0:T(8,128)(2,1)} %bitcast.69), calls=%async_computation.5 | async-start | bytes 2752512 | tf_op jit(solution)/shard_map/all_to_all | solution.py:744
  285.2 29.8 %collective-permute-start.28 = (bf16[192,3072]{1,0:T(8,128)(2,1)}, bf16[192,3072]{1,0:T(8,128)(2,1)}, u32[]{:S(2)}, u32[]{:S(2)}) collective-permute-start(bf16[192,3072]{1,0:T(8,128)(2,1)} %fusion.2), channel_id=1, source_target_pairs={{0,16},{8,24},{16,0},{24,8},{1,17},{9,25},{17,1},{25,9},{2,18},{10... | collective-permute-start | bytes 3538952 | tf_op jit(solution)/shard_map/ppermute | solution.py:31
  306.6 44.5 %all-to-all-start.6 = ((bf16[8,112,768]{2,1,0:T(8,128)(2,1)}), bf16[8,112,768]{2,1,0:T(8,128)(2,1)S(1)}, u32[]{:S(2)}, u32[]{:S(2)}) async-start(bf16[8,112,768]{2,1,0:T(8,128)(2,1)} %bitcast.335), calls=%async_computation.6 | async-start | bytes 2752512 | tf_op jit(solution)/shard_map/all_to_all | solution.py:744
  313.2 34.1 %collective-permute-start.34 = (bf16[768,768]{1,0:T(8,128)(2,1)}, bf16[768,768]{1,0:T(8,128)(2,1)}, u32[]{:S(2)}, u32[]{:S(2)}) collective-permute-start(bf16[768,768]{1,0:T(8,128)(2,1)} %fusion.3), channel_id=1, source_target_pairs={{0,16},{8,24},{16,0},{24,8},{1,17},{9,25},{17,1},{25,9},{2,18},{10... | collective-permute-start | bytes 3538952 | tf_op jit(solution)/shard_map/ppermute | solution.py:31
  353.3 21.0 %collective-permute-start.38 = (bf16[2,2,2,25,768]{4,3,2,1,0:T(8,128)(2,1)S(1)}, bf16[2,2,2,25,768]{4,3,2,1,0:T(8,128)(2,1)S(1)}, u32[]{:S(2)}, u32[]{:S(2)}) collective-permute-start(bf16[2,2,2,25,768]{4,3,2,1,0:T(8,128)(2,1)S(1)} %copy.182), channel_id=1, source_target_pairs={{0,2},{1,3},{2,0},{3,1},{4,6},{5,7},{6,4},{7,5},{8,10},{9,11},{10,... | collective-permute-start | bytes 921608 | tf_op jit(solution)/shard_map/ppermute | solution.py:31
  369.6 14.2 %collective-permute-start.42 = (bf16[2,2,72,256]{3,2,1,0:T(8,128)(2,1)S(1)}, bf16[2,2,72,256]{3,2,1,0:T(8,128)(2,1)S(1)}, u32[]{:S(2)}, u32[]{:S(2)}) collective-permute-start(bf16[2,2,72,256]{3,2,1,0:T(8,128)(2,1)S(1)} %fusion.12), channel_id=1, source_target_pairs={{0,2},{1,3},{2,0},{3,1},{4,6},{5,7},{6,4},{7,5},{8,10},{9,11},{10,... | collective-permute-start | bytes 442376 | tf_op jit(solution)/shard_map/ppermute | solution.py:31
  371.4 15.9 %collective-permute-start.45 = (bf16[2,2,72,256]{3,2,1,0:T(8,128)(2,1)S(1)}, bf16[2,2,72,256]{3,2,1,0:T(8,128)(2,1)S(1)}, u32[]{:S(2)}, u32[]{:S(2)}) collective-permute-start(bf16[2,2,72,256]{3,2,1,0:T(8,128)(2,1)S(1)} %fusion.11), channel_id=1, source_target_pairs={{0,4},{1,5},{2,6},{3,7},{4,0},{5,1},{6,2},{7,3},{8,12},{9,13},{10,... | collective-permute-start | bytes 442376 | tf_op jit(solution)/shard_map/ppermute | solution.py:31
  375.1 16.4 %collective-permute-start.48 = (bf16[2,2,25,768]{3,2,0,1:T(8,128)(2,1)S(1)}, bf16[2,2,25,768]{3,2,0,1:T(8,128)(2,1)S(1)}, u32[]{:S(2)}, u32[]{:S(2)}) collective-permute-start(bf16[2,2,25,768]{3,2,0,1:T(8,128)(2,1)S(1)} %fusion.7), channel_id=1, source_target_pairs={{0,4},{1,5},{2,6},{3,7},{4,0},{5,1},{6,2},{7,3},{8,12},{9,13},{10,... | collective-permute-start | bytes 460808 | tf_op jit(solution)/shard_map/ppermute | solution.py:31
  381.4 18.9 %collective-permute-start.40 = (bf16[2,72,256]{2,1,0:T(8,128)(2,1)S(1)}, bf16[2,72,256]{2,1,0:T(8,128)(2,1)S(1)}, u32[]{:S(2)}, u32[]{:S(2)}) collective-permute-start(bf16[2,72,256]{2,1,0:T(8,128)(2,1)S(1)} %fusion.24), channel_id=1, source_target_pairs={{0,2},{1,3},{2,0},{3,1},{4,6},{5,7},{6,4},{7,5},{8,10},{9,11},{10,... | collective-permute-start | bytes 221192 | tf_op jit(solution)/shard_map/ppermute | solution.py:31
  384.8 16.4 %collective-permute-start.43 = (bf16[2,72,256]{2,1,0:T(8,128)(2,1)S(1)}, bf16[2,72,256]{2,1,0:T(8,128)(2,1)S(1)}, u32[]{:S(2)}, u32[]{:S(2)}) collective-permute-start(bf16[2,72,256]{2,1,0:T(8,128)(2,1)S(1)} %fusion.23), channel_id=1, source_target_pairs={{0,4},{1,5},{2,6},{3,7},{4,0},{5,1},{6,2},{7,3},{8,12},{9,13},{10,... | collective-permute-start | bytes 221192 | tf_op jit(solution)/shard_map/ppermute | solution.py:31
  388.3 14.9 %collective-permute-start.46 = (bf16[2,72,256]{2,1,0:T(8,128)(2,1)S(1)}, bf16[2,72,256]{2,1,0:T(8,128)(2,1)S(1)}, u32[]{:S(2)}, u32[]{:S(2)}) collective-permute-start(bf16[2,72,256]{2,1,0:T(8,128)(2,1)S(1)} %fusion.22), channel_id=1, source_target_pairs={{0,16},{8,24},{16,0},{24,8},{1,17},{9,25},{17,1},{25,9},{2,18},{10... | collective-permute-start | bytes 221192 | tf_op jit(solution)/shard_map/ppermute | solution.py:31
  (66 other events, 554.4 us)

commit v4 on v3

--- a/solution.py
+++ b/solution.py
@@ -153,7 +153,7 @@
 
 
 LIMIT = 56 * 1024 * 1024
-QUERY_BLOCK = 128
+QUERY_BLOCK = 512
 SCALE = HEAD_DIM ** (-0.5)
 
 
@@ -371,14 +371,13 @@
     outgrad_ref[...] = dot(branch, context_ref[...], 0, 0).astype(BF)
 
 
-def pairs_back(proj_ref, gctx_ref, gproj_ref, gk_acc, gv_acc, first, last, shift, spread):
+def pairs_back(proj_ref, gctx_ref, gproj_ref, gk_acc, gv_acc):
     length, width = gctx_ref.shape
     size = min(QUERY_BLOCK, length)
     seen = causal(size)
 
     def one_pair(pair, carry):
         q_at, k_at, v_at = (pair_columns(pair, part, width) for part in range(3))
-        q_to, k_to, v_to = (pair_columns(pair - shift, part, spread) for part in range(3))
         gk_acc[...] = jnp.zeros_like(gk_acc)
         gv_acc[...] = jnp.zeros_like(gv_acc)
         for block in range(length // size):
@@ -407,25 +406,18 @@
                     gv_acc[s, :] += dot(p.astype(BF), gmine, 0, 0)
                 grads.append(gquery * SCALE)
             lane = lax.broadcasted_iota(jnp.int32, grads[0].shape, 1)
-            gproj_ref[rows, q_to] = jnp.where(lane < HEAD_DIM, grads[0], grads[1]).astype(BF)
-        gproj_ref[:, k_to] = gk_acc[...].astype(BF)
-        gproj_ref[:, v_to] = gv_acc[...].astype(BF)
+            gproj_ref[rows, q_at] = jnp.where(lane < HEAD_DIM, grads[0], grads[1]).astype(BF)
+        gproj_ref[:, k_at] = gk_acc[...].astype(BF)
+        gproj_ref[:, v_at] = gv_acc[...].astype(BF)
         return carry
 
-    lax.fori_loop(first, last, one_pair, 0)
-
-def attention_first_kernel(proj_ref, gctx_ref, gproj_ref, gk_acc, gv_acc):
-    spread = gproj_ref.shape[1] // 3
-    last = spread // (2 * HEAD_DIM)
-    pairs_back(proj_ref, gctx_ref, gproj_ref, gk_acc, gv_acc, 0, last, 0, spread)
-
+    lax.fori_loop(0, HEADS // 2, one_pair, 0)
 
 def attention_back_kernel(
     place_ref,
     proj_ref,
     gctx_ref,
     normed_ref,
-    before_ref,
     gproj_ref,
     keep0_ref,
     keep1_ref,
@@ -437,20 +429,7 @@
     gv_acc,
 ):
     width = gctx_ref.shape[1]
-    done = before_ref.shape[1] // 3
-    for part in range(3):
-        gproj_ref[:, part * width : part * width + done] = before_ref[
-            :, part * done : (part + 1) * done
-        ]
-    first = done // (2 * HEAD_DIM)
-    pairs_back(proj_ref, gctx_ref, gproj_ref, gk_acc, gv_acc, first, HEADS // 2, 0, width)
-    length, width = gctx_ref.shape
-    size = min(QUERY_BLOCK, length)
-    seen = causal(size)
-
-    def one_pair(pair, carry):
-        q_at, k_at, v_at = (pair_columns(pair, part, width) for part in range(3))
-        gk
+    pairs_back(proj_ref, gctx_ref, gproj_ref, gk_acc, gv_acc)
     third = width // 3
     core = place_ref[0] % 2
     halves, rows, _ = keep0_ref.shape
@@ -477,8 +456,8 @@
     sums_ref[...] = jnp.concatenate([gain_sum, bias_sum, jnp.zeros((6, width), F32)], axis=0)
 
 
-def mixed_kernel(old_ref, new_ref, target_ref, middle_ref, mixed_ref):
-    total = take_rows(target_ref, (old_ref, new_ref), middle_ref.shape[0])
+def mixed_kernel(slots_ref, target_ref, middle_ref, mixed_ref):
+    total = take_rows(target_ref, (slots_ref,), middle_ref.shape[0])
     mixed_ref[...] = (middle_ref[...] + total).astype(BF)
 
 
@@ -493,8 +472,8 @@
 def expert_kernel(train, steps, pieces, place_ref, mine_ref, rows_ref, grads4_ref, router_ref, *rest):
     ups, downs, rest = rest[:pieces], rest[pieces : 2 * pieces], rest[2 * pieces :]
     if train:
-        gated_ref, gin_ref, rgrad_ref, hid_ref, gpre_ref, scaled_ref = rest[:6]
-        rest = rest[6:]
+        _, gated_ref, gin_ref, rgrad_ref, hid_ref, gpre_ref, scaled_ref = rest[:7]
+        rest = rest[7:]
     else:
         gated_ref, gin_ref, rgrad_ref = rest[:3]
         rest = rest[3:]
@@ -558,14 +537,15 @@
     def _():
         produced = out_acc[...].astype(BF).astype(F32)
         gate = gate_s[:, 0:1]
-        gated_ref[...] = (produced * gate).astype(BF)
+        gated_ref[...] = (produced * gate).astype(BF).reshape(gated_ref.shape)
         grad_gate = jnp.sum(produced * grads(), axis=1, keepdims=True)
         gl = (grad_gate * gate * (mine - probs_s[...])).astype(BF)
         gin_ref[...] = (gin_acc[...] + dot(gl, router_ref[...], 1, 0)).astype(BF)
         rgrad_ref[...] = dot(gl, rows_ref[...], 0, 0)
 
 
-def expert_call(owners, mine, rows, grads, router_pad, ups, downs, train):
+def expert_call(owners, mine, rows, grads, router_pad, ups, downs, gated=None):
+    train = gated is not None
     n, d = rows.shape
     pieces = len(ups)
     f = ups[0].shape[1]
@@ -582,12 +562,12 @@
         (peers, 1, capacity, d), lambda j: (0, member, 0, 0), pipeline_mode=one
     )
     anywhere = pl.BlockSpec(memory_space=pl.ANY)
-    outs = [((n, d), BF), ((n, d), BF), ((128, d), F32)]
-    out_specs = [all_of((n, d)), all_of((n, d)), all_of((128, d))]
+    outs = [(grads.shape, BF), ((n, d), BF), ((128, d), F32)]
+    out_specs = [slot_spec, all_of((n, d)), all_of((128, d))]
     if train:
         outs += [((n, f), BF)] * 2 + [((n, d), BF)]
         out_specs += [pl.BlockSpec((n, tile), lambda j: (0, j))] * 2 + [all_of((n, d))]
-    args = [owners, mine, rows, grads, router_pad, *ups, *downs]
+    args = [owners, mine, rows, grads, router_pad, *ups, *downs] + ([gated] if train else [])
     return pl.pallas_call(
         functools.partial(expert_kernel, train, steps, pieces),
         grid=(steps,),
@@ -598,7 +578,7 @@
             slot_spec,
             all_of((128, d)),
         ]
-        + [anywhere] * (2 * pieces),
+        + [anywhere] * (2 * pieces + train),
         out_specs=out_specs,
         out_shape=[whole(o) for o in outs],
         scratch_shapes=[
@@ -611,6 +591,7 @@
             pltpu.VMEM((n, 128), F32),
             pltpu.SemaphoreType.DMA((2, pieces)),
         ],
+        input_output_aliases={len(args) - 1: 0} if train else {},
         compiler_params=pltpu.CompilerParams(vmem_limit_bytes=LIMIT),
         cost_estimate=cost(29),
         name="expert_new" if train else "expert_old",
@@ -775,9 +756,9 @@
     far.append(dp_far(after(shards_dp[2], between, far)))
     far.append(dp_far(after(shards_dp[3], between, far)))
     near = [{away: core_swap(piece) for away, piece in f.items()} for f in far[:3]]
-    rold = send(rold, grads, far[:2])
-    own = [core_swap(after(shard, grads)) for shard in shards_dp]
-    rnew = send(rnew, rold, near, own)
+    own = [core_swap(after(shard, normed)) for shard in shards_dp]
+    rold = send(rold, grads, far[:2], own)
+    rnew = send(rnew, rold, near)
 
     lane = lax.broadcasted_iota(jnp.int32, (8, 128), 1)
     line = lax.broadcasted_iota(jnp.int32, (8, 128), 0)
@@ -786,15 +767,15 @@
         return jnp.where(line == 0, (lane == expert).astype(F32), F32(experts))
 
     pieces = [dp_pieces(shards_dp[i], own[i], far[i], near[i]) for i in range(2)]
-    old_gated, old_in, old_router = expert_call(
-        owners, chosen(2 * me), rold, grads, router_pad, *pieces, False
+    gated, old_in, old_router = expert_call(
+        owners, chosen(2 * me), rold, grads, router_pad, *pieces
     )
     near.append({away: core_swap(after(piece, old_in)) for away, piece in far[3].items()})
     pieces = [dp_pieces(shards_dp[i], own[i], far[i], near[i]) for i in range(2, 4)]
     rnew, old_in = lax.optimization_barrier((rnew, old_in))
     old_in = send(old_in, rnew)
-    new_gated, new_in, new_router, hidden, grad_pre, scaled = expert_call(
-        owners, chosen(2 * me + 1), rnew, grads, router_pad, *pieces, True
+    gated, new_in, new_router, hidden, grad_pre, scaled = expert_call(
+        owners, chosen(2 * me + 1), rnew, grads, router_pad, *pieces, gated
     )
     up_keep, up_send, down_keep, down_send = weight_grads_call(
         owners, rnew, scaled, hidden, grad_pre
@@ -802,7 +783,7 @@
     new_in = send(new_in, old_in)
     ups = [up_keep, core_swap(after(up_send, old_in))]
     downs = [down_keep, core_swap(after(down_send, old_in))]
-    old_gated = send(old_gated, new_in)
+    gated = move(after(gated, new_in, ups, downs)).reshape(2 * count, width)
     router_part = (old_router + new_router)[:experts]
 
     gmid, gctx, out_grad, sums_two = plain_call(
@@ -815,7 +796,7 @@
         ],
         [],
         "branch_backward",
-        8,
+        0,
         old_in,
         new_in,
         by_member,
@@ -826,38 +807,26 @@
         vectors,
     )
     accumulators = [pltpu.VMEM((length, 2 * HEAD_DIM), F32)] * 2
-    (gfirst,) = plain_call(
-        attention_first_kernel,
-        [((length, 3 * width // 2), BF)],
-        accumulators,
-        "attention_backward_first",
-        40,
-        proj,
-        gctx,
-    )
-    new_gated = send(new_gated, old_gated, gfirst)
     ups_first, downs_first = [scatter_dp_first(after(sums, gctx)) for sums in (ups, downs)]
     ups_x = scatter_dp(ups, ups_first)
     downs_x = scatter_dp(downs, downs_first)
-    gfirst = after(gfirst, ups_x)
     half = lax.axis_size("dp") // 2
     gproj, *split = plain_call(
         attention_back_kernel,
         [((length, 3 * width), BF)] + [((half, 3 * width // (2 * half), third), BF)] * 6,
         accumulators,
         "attention_backward",
-        40,
+        0,
         owners,
         proj,
-        gctx,
+        after(gctx, ups_first, downs_first),
         normed,
-        gfirst,
     )
     input_grad, sums_one = plain_call(
         input_kernel,
         [((length, width), F32), ((8, width), F32)],
         [],
-        "input_backward", 20,
+        "input_backward", 0,
         gproj,
         *in_parts,
         block_input,
@@ -875,6 +844,7 @@
     small_grads = small_grads.reshape(lines, devices, share).transpose(1, 0, 2)
     small_grads = small_grads.reshape(devices, 1, lines * share).astype(BF)
     small_rows = -(-lines * share // width)
+    small_rows += -(share + small_rows) % 8
     small_grads = jnp.pad(small_grads, ((0, 0), (0, 0), (0, small_rows * width - lines * share)))
     rest = jnp.concatenate(
         [out_grad.reshape(devices, share, width), small_grads.reshape(devices, small_rows, width)],
@@ -883,7 +853,7 @@
     rest = rest.reshape([2] * len(lead) + list(rest.shape[1:]))
     got = scatter_step([rest], lead, core[0])
     states.append(scatter_rest([rest], lead, core[0], got)[0])
-    states = after(states, old_gated, new_gated, downs_x)
+    states = after(states, gated, ups_x, downs_x)
     lefts = [left] * len(states)
     for at in range(len(left)):
         arrived = [
@@ -896,8 +866,8 @@
                 [((length, width), BF)],
                 [],
                 "mixed_output", 5,
-                *after((old_gated, new_gated), arrived),
-                by_member,
+                after(gated, arrived),
+                target,
                 middle,
             )
         if at == 1:

time: 418 us -> 399 us (0.955)
  Pallas kernels: 162 us -> 135 us
  waiting for transfers between devices: 104 us -> 111 us
  local copies, waits for them, and re-layouts: 24.8 us -> 29.6 us
    pallas_call x7 -> x6, Pallas kernels: 88.3 us -> 61.4 us  [plain_call(): pl.pallas_call(body, out_shape=[whole(o) for o in outs], in_specs=[space]...]
    ppermute x51, waiting for transfers between devices: 77.4 us -> 97.4 us  [swap(): return lax.ppermute(values, axis, [(i, i ^ bit) for i in range(count)])]
    all_to_all x7 -> x6, waiting for transfers between devices: 26.7 us -> 13.5 us  [move(): lax.all_to_all(block, 'expert', split_axis=0, concat_axis=0, tiled=True)]
    unnamed x68 -> x70, local copies, waits for them, and re-layouts: 5.81 us -> 11.7 us
    all_to_all x7 -> x6, starting transfers between devices: 32 us -> 27.8 us  [move(): lax.all_to_all(block, 'expert', split_axis=0, concat_axis=0, tiled=True)]
  transfers between devices with their start and end apart: 58 -> 57, of which waited for: 25 -> 23; matrix products, arithmetic and copies ran while one was open for 13% -> 13% of each run, Pallas kernels for 39% -> 34%
where the time goes in v4:
time: 399 us; the launch traced here: 393 us
  Pallas kernels  135 us (34%)
  waiting for transfers between devices  111 us (28%)
  starting transfers between devices  75.1 us (19%)
  other arithmetic  41.3 us (10%)
  local copies, waits for them, and re-layouts  29.6 us (7%)
    ppermute x51, waiting for transfers between devices, swap(): return lax.ppermute(values, axis, [(i, i ^ bit) for i in range(count)])  97.4 us
    pallas_call x6, Pallas kernels, plain_call(): pl.pallas_call(body, out_shape=[whole(o) for o in outs], in_specs=[space]...  61.4 us
    pallas_call x2, Pallas kernels, expert_call(): pl.pallas_call(functools.partial(expert_kernel, train, steps, pieces), gr...  57 us
    ppermute x51, starting transfers between devices, swap(): return lax.ppermute(values, axis, [(i, i ^ bit) for i in range(count)])  47.3 us
    all_to_all x6, starting transfers between devices, move(): lax.all_to_all(block, 'expert', split_axis=0, concat_axis=0, tiled=True)  27.8 us
    convert_element_type x18, other arithmetic, away_part(): return send.astype(BF)  19.7 us
    pallas_call x1, Pallas kernels, weight_grads_call(): pl.pallas_call(functools.partial(weight_grads_kernel, pieces), grid=(f //...  16.3 us
    all_to_all x6, waiting for transfers between devices, move(): lax.all_to_all(block, 'expert', split_axis=0, concat_axis=0, tiled=True)  13.5 us
  transfers between devices with their start and end apart: 57, of which 23 were waited for; matrix products, arithmetic and copies ran while one was open for 13% of the time, Pallas kernels for 34%

profile of v4, /device:TPU:0, one launch (start us, length us, event | category | flops | bytes accessed | tf_op | source)
XLA Modules:
  0.0 393.4 jit_solution(16409999633863630236)
XLA Ops:
  23.9 4.3 %place_grads.1 = bf16[1792,768]{1,0:T(8,128)(2,1)} custom-call(s32[8,512]{1,0:T(8,128)} %pad.29.clone.target_ref, bf16[512,768]{1,0:T(8,128)(2,1)} %cot_ref.1), custom_call_target="tpu_custom_call" | custom-call | flops 1000000000 | tf_op jit(solution)/shard_map/place_grads/pallas_call | solution.py:185
  33.9 4.2 %collective-permute-done.8 = bf16[2,2,2,96,256]{4,3,2,1,0:T(8,128)(2,1)S(1)} collective-permute-done((bf16[2,2,2,96,256]{4,3,2,1,0:T(8,128)(2,1)S(1)}, bf16[2,2,2,96,256]{4,3,2,1,0:T(8,128)(2,1)S(1)}, u32[]{:S(2)}, u32[]{:S(2)}) %collective-permute-start.8) | collective-permute-done | bytes 393248 | tf_op jit(solution)/shard_map/ppermute | solution.py:31
  44.3 4.8 %all-to-all-start = ((bf16[8,2,112,768]{3,2,1,0:T(8,128)(2,1)}), bf16[8,2,112,768]{3,2,1,0:T(8,128)(2,1)}, u32[]{:S(2)}, u32[]{:S(2)}) async-start(bf16[8,2,112,768]{3,2,1,0:T(8,128)(2,1)} %bitcast.328), calls=%async_computation | async-start | bytes 5505024 | tf_op jit(solution)/shard_map/all_to_all | solution.py:725
  63.8 16.5 %attention_forward.1 = (bf16[512,768]{1,0:T(8,128)(2,1)}, bf16[512,2304]{1,0:T(8,128)(2,1)}, bf16[512,768]{1,0:T(8,128)(2,1)}, f32[512,768]{1,0:T(8,128)}, bf16[...) custom-call(bf16[512,768]{1,0:T(8,128)(2,1)} %x_ref.3, bf16[2304,256]{1,0:T(8,128)(2,1)} %bitcast.321, ...), custom_call_target="tpu_custom_call" | custom-call | flops 6750000128 | tf_op jit(solution)/shard_map/attention_forward/pallas_call | solution.py:185
  81.4 24.1 %collective-permute-done.16.rest_6_ = bf16[768,768]{1,0:T(8,128)(2,1)} collective-permute-done((bf16[768,768]{1,0:T(8,128)(2,1)}, bf16[768,768]{1,0:T(8,128)(2,1)}, u32[]{:S(2)}, u32[]{:S(2)}) %collective-permute-start.16) | collective-permute-done | bytes 1179680 | tf_op jit(solution)/shard_map/ppermute | solution.py:31
  109.3 4.6 %all-to-all-start.1 = ((bf16[8,112,768]{2,1,0:T(8,128)(2,1)}), bf16[8,112,768]{2,1,0:T(8,128)(2,1)S(1)}, u32[]{:S(2)}, u32[]{:S(2)}) async-start(bf16[8,112,768]{2,1,0:T(8,128)(2,1)} %bitcast.340), calls=%async_computation.1 | async-start | bytes 2752512 | tf_op jit(solution)/shard_map/all_to_all | solution.py:725
  115.9 25.2 %collective-permute-done.23.rest_2_ = bf16[192,3072]{1,0:T(8,128)(2,1)S(1)} collective-permute-done((bf16[192,3072]{1,0:T(8,128)(2,1)S(1)}, bf16[192,3072]{1,0:T(8,128)(2,1)S(1)}, u32[]{:S(2)}, u32[]{:S(2)}) %collective-permute-start.23) | collective-permute-done | bytes 1179680 | tf_op jit(solution)/shard_map/ppermute | solution.py:31
  146.5 3.9 all-to-all-start.2
  154.1 27.4 %expert_old.1 = (bf16[8,2,112,768]{3,2,1,0:T(8,128)(2,1)}, bf16[896,768]{1,0:T(8,128)(2,1)}, f32[128,768]{1,0:T(8,128)}) custom-call(s32[4]{0:T(128)} %iota_xor_fusion.place_ref, f32[8,128]{1,0:T(8,128)} %get-tuple-element.199.mine_ref, bf16[896,768]{1,0:T(8,128)(2,1)} %bitcast.339, bf16[8,2,112,768]{3,2,1,0:T(8,128)(2,1)} %all-to-all-done.grads4_ref, ...), custom_call_target="tpu_custom_call" | custom-call | flops 7249999872 | tf_op jit(solution)/shard_map/expert_old/pallas_call | solution.py:571
  183.3 4.7 %all-to-all-start.3 = ((bf16[8,112,768]{2,1,0:T(8,128)(2,1)}), bf16[8,112,768]{2,1,0:T(8,128)(2,1)S(1)}, u32[]{:S(2)}, u32[]{:S(2)}) async-start(bf16[8,112,768]{2,1,0:T(8,128)(2,1)} %bitcast.341), calls=%async_computation.3 | async-start | bytes 2752512 | tf_op jit(solution)/shard_map/all_to_all | solution.py:725
  192.2 29.6 %expert_new.1 = (bf16[8,2,112,768]{3,2,1,0:T(8,128)(2,1)}, bf16[896,768]{1,0:T(8,128)(2,1)}, f32[128,768]{1,0:T(8,128)}, bf16[896,3072]{1,0:T(8,128)(2,1)}, bf16...) custom-call(s32[4]{0:T(128)} %iota_xor_fusion.place_ref, ...), custom_call_target="tpu_custom_call", output_to_operand_aliasing={{0}: (13, {})} | custom-call | flops 7249999872 | tf_op jit(solution)/shard_map/expert_new/pallas_call | solution.py:571
  221.8 6.0 %all-to-all-start.4 = ((bf16[8,112,768]{2,1,0:T(8,128)(2,1)}), bf16[8,112,768]{2,1,0:T(8,128)(2,1)S(1)}, u32[]{:S(2)}, u32[]{:S(2)}) async-start(bf16[8,112,768]{2,1,0:T(8,128)(2,1)} %bitcast.342), calls=%async_computation.4 | async-start | bytes 2752512 | tf_op jit(solution)/shard_map/all_to_all | solution.py:725
  227.8 16.3 %weight_grads.1 = (bf16[2,192,3072]{2,1,0:T(8,128)(2,1)}, bf16[2,192,3072]{2,1,0:T(8,128)(2,1)}, bf16[2,768,768]{2,1,0:T(8,128)(2,1)}, bf16[2,768,768]{2,1,0:T(8,128)(2,1)}) custom-call(s32[4]{0:T(128)} %iota_xor_fusion.place_ref, bf16[896,768]{1,0:T(8,128)(2,1)} %bitcast.316, bf16[896,768]{1,0:T(8,128)(2,1)} %get-tuple-element.107.scaled_ref, ...), custom_call_target="tpu_custom_call" | custom-call | flops 3500000000 | tf_op jit(solution)/shard_map/weight_grads/pallas_call | solution.py:649
  244.8 6.8 %collective-permute-done.28 = bf16[2,768,768]{2,1,0:T(8,128)(2,1)S(1)} collective-permute-done((bf16[2,768,768]{2,1,0:T(8,128)(2,1)}, bf16[2,768,768]{2,1,0:T(8,128)(2,1)S(1)}, u32[]{:S(2)}, u32[]{:S(2)}) %collective-permute-start.28) | collective-permute-done | bytes 2359328 | tf_op jit(solution)/shard_map/ppermute | solution.py:31
  253.0 7.9 %all-to-all-done.4 = bf16[8,112,768]{2,1,0:T(8,128)(2,1)S(1)} async-done(((bf16[8,112,768]{2,1,0:T(8,128)(2,1)}), bf16[8,112,768]{2,1,0:T(8,128)(2,1)S(1)}, u32[]{:S(2)}, u32[]{:S(2)}) %all-to-all-start.4) | async-done | bytes 1376288 | tf_op jit(solution)/shard_map/all_to_all | solution.py:725
  262.0 3.8 all-to-all-start.5
  265.9 8.7 %branch_backward.1 = (f32[512,768]{1,0:T(8,128)}, bf16[512,768]{1,0:T(8,128)(2,1)}, bf16[768,768]{1,0:T(8,128)(2,1)}, f32[8,768]{1,0:T(8,128)}) custom-call(bf16[896,768]{1,0:T(8,128)(2,1)} %bitcast.313, bf16[896,768]{1,0:T(8,128)(2,1)} %bitcast.314, s32[512,2]{1,0:T(8,128)} %copy-done.5, bf16[512,768]{1,0:T(8,128)(2,1)} %cot_ref.1, ...), custom_call_target="tpu_custom_call" | custom-call | tf_op jit(solution)/shard_map/branch_backward/pallas_call | solution.py:185
  280.7 19.6 %attention_backward.1 = (bf16[512,2304]{1,0:T(8,128)(2,1)}, bf16[2,576,256]{2,1,0:T(8,128)(2,1)}, bf16[2,576,256]{2,1,0:T(8,128)(2,1)}, bf16[2,576,256]{2,1,0:T(...) custom-call(s32[4]{0:T(128)} %iota_xor_fusion.place_ref, ...), custom_call_target="tpu_custom_call" | custom-call | tf_op jit(solution)/shard_map/attention_backward/pallas_call | solution.py:185
  301.1 7.1 %input_backward.1 = (f32[512,768]{1,0:T(8,128)}, f32[8,768]{1,0:T(8,128)}) custom-call(bf16[512,2304]{1,0:T(8,128)(2,1)} %get-tuple-element.133.gproj_ref, bf16[2304,256]{1,0:T(8,128)(2,1)} %bitcast.322, bf16[2304,256]{1,0:T(8,128)(2,1)} %bitcast.320, bf16[2304,256]{1,0:T(8,128)(2,1)} %bitcast.318, bf16[512,768]{1,0:T(8,128)(2,1)} %x_ref.3, ...), custom_call_target="tpu_custom_call" | custom-call | tf_op jit(solution)/shard_map/input_backward/pallas_call | solution.py:185
  317.0 12.1 %collective-permute-done.33 = bf16[192,3072]{1,0:T(8,128)(2,1)} collective-permute-done((bf16[192,3072]{1,0:T(8,128)(2,1)}, bf16[192,3072]{1,0:T(8,128)(2,1)}, u32[]{:S(2)}, u32[]{:S(2)}) %collective-permute-start.33) | collective-permute-done | bytes 1179680 | tf_op jit(solution)/shard_map/ppermute | solution.py:31
  341.0 3.4 collective-permute-done.36
  346.1 4.5 %collective-permute-done.37 = bf16[2,2,2,72,256]{4,3,2,1,0:T(8,128)(2,1)S(1)} collective-permute-done((bf16[2,2,2,72,256]{4,3,2,1,0:T(8,128)(2,1)S(1)}, bf16[2,2,2,72,256]{4,3,2,1,0:T(8,128)(2,1)S(1)}, u32[]{:S(2)}, u32[]{:S(2)}) %collective-permute-start.37) | collective-permute-done | bytes 294944 | tf_op jit(solution)/shard_map/ppermute | solution.py:31
  355.6 5.1 %mixed_output.1 = bf16[512,768]{1,0:T(8,128)(2,1)} custom-call(bf16[1792,768]{1,0:T(8,128)(2,1)} %bitcast.305, s32[512,2]{1,0:T(8,128)} %copy-done.13, f32[512,768]{1,0:T(8,128)} %get-tuple-element.118.middle_ref), custom_call_target="tpu_custom_call" | custom-call | flops 1250000000 | tf_op jit(solution)/shard_map/mixed_output/pallas_call | solution.py:185
  381.7 3.6 fusion.1
  (281 shorter events, 137.2 us)
Async XLA Ops:
  44.3 65.0 %all-to-all-start = ((bf16[8,2,112,768]{3,2,1,0:T(8,128)(2,1)}), bf16[8,2,112,768]{3,2,1,0:T(8,128)(2,1)}, u32[]{:S(2)}, u32[]{:S(2)}) async-start(bf16[8,2,112,768]{3,2,1,0:T(8,128)(2,1)} %bitcast.328), calls=%async_computation | async-start | bytes 5505024 | tf_op jit(solution)/shard_map/all_to_all | solution.py:725
  51.5 29.4 %collective-permute-start.15 = (bf16[192,3072]{1,0:T(8,128)(2,1)}, bf16[192,3072]{1,0:T(8,128)(2,1)}, u32[]{:S(2)}, u32[]{:S(2)}) collective-permute-start(bf16[192,3072]{1,0:T(8,128)(2,1)} %bitcast.367), channel_id=1, source_target_pairs={{0,16},{8,24},{16,0},{24,8},{1,17},{9,25},{17,1},{25,9},{2,18},{10... | collective-permute-start | bytes 3538952 | tf_op jit(solution)/shard_map/ppermute | solution.py:31
  53.0 52.4 %collective-permute-start.16 = (bf16[768,768]{1,0:T(8,128)(2,1)}, bf16[768,768]{1,0:T(8,128)(2,1)}, u32[]{:S(2)}, u32[]{:S(2)}) collective-permute-start(bf16[768,768]{1,0:T(8,128)(2,1)} %bitcast.370), channel_id=1, source_target_pairs={{0,16},{8,24},{16,0},{24,8},{1,17},{9,25},{17,1},{25,9},{2,18},{10... | collective-permute-start | bytes 3538952 | tf_op jit(solution)/shard_map/ppermute | solution.py:31
  80.3 25.1 %collective-permute-start.17 = (bf16[192,3072]{1,0:T(8,128)(2,1)S(1)}, bf16[192,3072]{1,0:T(8,128)(2,1)S(1)}, u32[]{:S(2)}, u32[]{:S(2)}) collective-permute-start(bf16[192,3072]{1,0:T(8,128)(2,1)S(1)} %bitcast.369), channel_id=1, source_target_pairs={{0,8},{8,0},{16,24},{24,16},{1,9},{9,1},{17,25},{25,17},{2,10},{10... | collective-permute-start | bytes 3538952 | tf_op jit(solution)/shard_map/ppermute | solution.py:31
  80.3 25.1 %collective-permute-start.18 = (bf16[768,768]{1,0:T(8,128)(2,1)S(1)}, bf16[768,768]{1,0:T(8,128)(2,1)S(1)}, u32[]{:S(2)}, u32[]{:S(2)}) collective-permute-start(bf16[768,768]{1,0:T(8,128)(2,1)S(1)} %bitcast.372), channel_id=1, source_target_pairs={{0,8},{8,0},{16,24},{24,16},{1,9},{9,1},{17,25},{25,17},{2,10},{10... | collective-permute-start | bytes 3538952 | tf_op jit(solution)/shard_map/ppermute | solution.py:31
  80.8 24.6 %collective-permute-start.19 = (bf16[192,3072]{1,0:T(8,128)(2,1)S(1)}, bf16[192,3072]{1,0:T(8,128)(2,1)S(1)}, u32[]{:S(2)}, u32[]{:S(2)}) collective-permute-start(bf16[192,3072]{1,0:T(8,128)(2,1)S(1)} %bitcast.374), channel_id=1, source_target_pairs={{0,8},{8,0},{16,24},{24,16},{1,9},{9,1},{17,25},{25,17},{2,10},{10... | collective-permute-start | bytes 3538952 | tf_op jit(solution)/shard_map/ppermute | solution.py:31
  80.9 27.0 %collective-permute-start.20 = (bf16[768,768]{1,0:T(8,128)(2,1)S(1)}, bf16[768,768]{1,0:T(8,128)(2,1)}, u32[]{:S(2)}, u32[]{:S(2)}) collective-permute-start(bf16[768,768]{1,0:T(8,128)(2,1)S(1)} %bitcast.378), channel_id=1, source_target_pairs={{0,8},{8,0},{16,24},{24,16},{1,9},{9,1},{17,25},{25,17},{2,10},{10... | collective-permute-start | bytes 3538952 | tf_op jit(solution)/shard_map/ppermute | solution.py:31
  109.3 37.2 %all-to-all-start.1 = ((bf16[8,112,768]{2,1,0:T(8,128)(2,1)}), bf16[8,112,768]{2,1,0:T(8,128)(2,1)S(1)}, u32[]{:S(2)}, u32[]{:S(2)}) async-start(bf16[8,112,768]{2,1,0:T(8,128)(2,1)} %bitcast.340), calls=%async_computation.1 | async-start | bytes 2752512 | tf_op jit(solution)/shard_map/all_to_all | solution.py:725
  113.9 27.3 %collective-permute-start.23 = (bf16[192,3072]{1,0:T(8,128)(2,1)S(1)}, bf16[192,3072]{1,0:T(8,128)(2,1)S(1)}, u32[]{:S(2)}, u32[]{:S(2)}) collective-permute-start(bf16[192,3072]{1,0:T(8,128)(2,1)S(1)} %bitcast.375), channel_id=1, source_target_pairs={{0,16},{8,24},{16,0},{24,8},{1,17},{9,25},{17,1},{25,9},{2,18},{10... | collective-permute-start | bytes 3538952 | tf_op jit(solution)/shard_map/ppermute | solution.py:31
  115.4 25.7 %collective-permute-start.21 = (bf16[192,3072]{1,0:T(8,128)(2,1)}, bf16[192,3072]{1,0:T(8,128)(2,1)S(1)}, u32[]{:S(2)}, u32[]{:S(2)}) collective-permute-start(bf16[192,3072]{1,0:T(8,128)(2,1)} %collective-permute-done.15.rest_2_), channel_id=1, source_target_pairs={{0,8},{8,0},{16,24},{24,16},{1,9},{9,1},{17,25},{25,17},{2,10},{10... | collective-permute-start | bytes 3538952 | tf_op jit(solution)/shard_map/ppermute | solution.py:31
  115.4 25.7 %collective-permute-start.22 = (bf16[768,768]{1,0:T(8,128)(2,1)}, bf16[768,768]{1,0:T(8,128)(2,1)S(1)}, u32[]{:S(2)}, u32[]{:S(2)}) collective-permute-start(bf16[768,768]{1,0:T(8,128)(2,1)} %collective-permute-done.16.rest_6_), channel_id=1, source_target_pairs={{0,8},{8,0},{16,24},{24,16},{1,9},{9,1},{17,25},{25,17},{2,10},{10... | collective-permute-start | bytes 3538952 | tf_op jit(solution)/shard_map/ppermute | solution.py:31
  146.5 36.8 %all-to-all-start.2 = ((bf16[8,112,768]{2,1,0:T(8,128)(2,1)}), bf16[8,112,768]{2,1,0:T(8,128)(2,1)S(1)}, u32[]{:S(2)}, u32[]{:S(2)}) async-start(bf16[8,112,768]{2,1,0:T(8,128)(2,1)} %bitcast.63), calls=%async_computation.2 | async-start | bytes 2752512 | tf_op jit(solution)/shard_map/all_to_all | solution.py:725
  152.6 35.5 %collective-permute-start.25 = (bf16[768,768]{1,0:T(8,128)(2,1)}, bf16[768,768]{1,0:T(8,128)(2,1)}, u32[]{:S(2)}, u32[]{:S(2)}) collective-permute-start(bf16[768,768]{1,0:T(8,128)(2,1)} %bitcast.376), channel_id=1, source_target_pairs={{0,16},{8,24},{16,0},{24,8},{1,17},{9,25},{17,1},{25,9},{2,18},{10... | collective-permute-start | bytes 3538952 | tf_op jit(solution)/shard_map/ppermute | solution.py:31
  183.3 38.5 %all-to-all-start.3 = ((bf16[8,112,768]{2,1,0:T(8,128)(2,1)}), bf16[8,112,768]{2,1,0:T(8,128)(2,1)S(1)}, u32[]{:S(2)}, u32[]{:S(2)}) async-start(bf16[8,112,768]{2,1,0:T(8,128)(2,1)} %bitcast.341), calls=%async_computation.3 | async-start | bytes 2752512 | tf_op jit(solution)/shard_map/all_to_all | solution.py:725
  221.8 39.1 %all-to-all-start.4 = ((bf16[8,112,768]{2,1,0:T(8,128)(2,1)}), bf16[8,112,768]{2,1,0:T(8,128)(2,1)S(1)}, u32[]{:S(2)}, u32[]{:S(2)}) async-start(bf16[8,112,768]{2,1,0:T(8,128)(2,1)} %bitcast.342), calls=%async_computation.4 | async-start | bytes 2752512 | tf_op jit(solution)/shard_map/all_to_all | solution.py:725
  262.0 67.2 %all-to-all-start.5 = ((bf16[8,2,112,768]{3,2,1,0:T(8,128)(2,1)}), bf16[8,2,112,768]{3,2,1,0:T(8,128)(2,1)S(1)}, u32[]{:S(2)}, u32[]{:S(2)}) async-start(bf16[8,2,112,768]{3,2,1,0:T(8,128)(2,1)} %get-tuple-element.116), calls=%async_computation.5 | async-start | bytes 5505024 | tf_op jit(solution)/shard_map/all_to_all | solution.py:725
  276.0 41.1 %collective-permute-start.34 = (bf16[768,768]{1,0:T(8,128)(2,1)}, bf16[768,768]{1,0:T(8,128)(2,1)}, u32[]{:S(2)}, u32[]{:S(2)}) collective-permute-start(bf16[768,768]{1,0:T(8,128)(2,1)} %fusion.3), channel_id=1, source_target_pairs={{0,16},{8,24},{16,0},{24,8},{1,17},{9,25},{17,1},{25,9},{2,18},{10... | collective-permute-start | bytes 3538952 | tf_op jit(solution)/shard_map/ppermute | solution.py:31
  279.7 49.5 %collective-permute-start.33 = (bf16[192,3072]{1,0:T(8,128)(2,1)}, bf16[192,3072]{1,0:T(8,128)(2,1)}, u32[]{:S(2)}, u32[]{:S(2)}) collective-permute-start(bf16[192,3072]{1,0:T(8,128)(2,1)} %fusion.2), channel_id=1, source_target_pairs={{0,16},{8,24},{16,0},{24,8},{1,17},{9,25},{17,1},{25,9},{2,18},{10... | collective-permute-start | bytes 3538952 | tf_op jit(solution)/shard_map/ppermute | solution.py:31
  300.3 12.8 %collective-permute-start.29 = (bf16[2,576,256]{2,1,0:T(8,128)(2,1)}, bf16[2,576,256]{2,1,0:T(8,128)(2,1)}, u32[]{:S(2)}, u32[]{:S(2)}) collective-permute-start(bf16[2,576,256]{2,1,0:T(8,128)(2,1)} %get-tuple-element.127), channel_id=1, source_target_pairs={{0,8},{8,0},{16,24},{24,16},{1,9},{9,1},{17,25},{25,17},{2,10},{10... | collective-permute-start | bytes 1769480 | tf_op jit(solution)/shard_map/ppermute | solution.py:31
  333.0 21.5 %collective-permute-start.38 = (bf16[2,2,2,32,768]{4,3,2,1,0:T(8,128)(2,1)S(1)}, bf16[2,2,2,32,768]{4,3,2,1,0:T(8,128)(2,1)S(1)}, u32[]{:S(2)}, u32[]{:S(2)}) collective-permute-start(bf16[2,2,2,32,768]{4,3,2,1,0:T(8,128)(2,1)S(1)} %copy.128), channel_id=1, source_target_pairs={{0,2},{1,3},{2,0},{3,1},{4,6},{5,7},{6,4},{7,5},{8,10},{9,11},{10,... | collective-permute-start | bytes 1179656 | tf_op jit(solution)/shard_map/ppermute | solution.py:31
  340.1 20.7 %collective-permute-start.39 = (bf16[2,2,72,256]{3,2,1,0:T(8,128)(2,1)S(1)}, bf16[2,2,72,256]{3,2,1,0:T(8,128)(2,1)S(1)}, u32[]{:S(2)}, u32[]{:S(2)}) collective-permute-start(bf16[2,2,72,256]{3,2,1,0:T(8,128)(2,1)S(1)} %fusion.13), channel_id=1, source_target_pairs={{0,1},{1,0},{2,3},{3,2},{4,5},{5,4},{6,7},{7,6},{8,9},{9,8},{10,11... | collective-permute-start | bytes 442376 | tf_op jit(solution)/shard_map/ppermute | solution.py:31
  345.4 17.8 %collective-permute-start.42 = (bf16[2,2,72,256]{3,2,1,0:T(8,128)(2,1)S(1)}, bf16[2,2,72,256]{3,2,1,0:T(8,128)(2,1)S(1)}, u32[]{:S(2)}, u32[]{:S(2)}) collective-permute-start(bf16[2,2,72,256]{3,2,1,0:T(8,128)(2,1)S(1)} %fusion.12), channel_id=1, source_target_pairs={{0,2},{1,3},{2,0},{3,1},{4,6},{5,7},{6,4},{7,5},{8,10},{9,11},{10,... | collective-permute-start | bytes 442376 | tf_op jit(solution)/shard_map/ppermute | solution.py:31
  351.6 15.0 %collective-permute-start.45 = (bf16[2,2,72,256]{3,2,1,0:T(8,128)(2,1)S(1)}, bf16[2,2,72,256]{3,2,1,0:T(8,128)(2,1)S(1)}, u32[]{:S(2)}, u32[]{:S(2)}) collective-permute-start(bf16[2,2,72,256]{3,2,1,0:T(8,128)(2,1)S(1)} %fusion.11), channel_id=1, source_target_pairs={{0,4},{1,5},{2,6},{3,7},{4,0},{5,1},{6,2},{7,3},{8,12},{9,13},{10,... | collective-permute-start | bytes 442376 | tf_op jit(solution)/shard_map/ppermute | solution.py:31
  355.5 23.7 %collective-permute-start.48 = (bf16[2,2,32,768]{3,2,1,0:T(8,128)(2,1)S(1)}, bf16[2,2,32,768]{3,2,1,0:T(8,128)(2,1)S(1)}, u32[]{:S(2)}, u32[]{:S(2)}) collective-permute-start(bf16[2,2,32,768]{3,2,1,0:T(8,128)(2,1)S(1)} %copy.141), channel_id=1, source_target_pairs={{0,4},{1,5},{2,6},{3,7},{4,0},{5,1},{6,2},{7,3},{8,12},{9,13},{10,... | collective-permute-start | bytes 589832 | tf_op jit(solution)/shard_map/ppermute | solution.py:31
  (65 other events, 483.4 us)

commit v5 on v4

--- a/solution.py
+++ b/solution.py
@@ -50,7 +50,7 @@
     zs = [("expert", b) for b in reversed(expert_bits[1:])]
     gathering = (zs + ys + xs + core, xs + zs + ys + core, ys + xs + zs + core)
     near = zs[::-1]
-    summing = (xs + ys + near, ys + near + xs, near + xs + ys, near + ys + xs)
+    summing = (xs + ys + near, ys + near + xs, near + xs + ys, xs + ys + near)
     return gathering, summing
 
 
@@ -126,28 +126,15 @@
     return [("dp", b) for b in powers(lax.axis_size("dp"))[1:]]
 
 
-def scatter_dp_first(addends):
-    order = x_steps()
-    addends = [a.reshape([2] * len(order) + list(a.shape[1:])) for a in addends]
-    return away_part(addends, order[::-1], order[0])
-
-
-def scatter_dp(addends, first):
+def scatter_dp(own, first):
     order = x_steps()
     lead = order[::-1]
-    addends = [a.reshape([2] * len(order) + list(a.shape[1:])) for a in addends]
-    arrived = [swap(first, *order[0])]
-    for at, step in enumerate(order[1:]):
-        addends, lead = scatter_rest(addends, lead, order[at], arrived[-1])
-        arrived.append(scatter_step(addends, lead, step))
-    return arrived
-
-
-def scatter_dp_total(addends, arrived):
-    order = x_steps()
-    lead = order[::-1]
-    addends = [a.reshape([2] * len(order) + list(a.shape[1:])) for a in addends]
-    for step, got in zip(order, arrived):
+    addends = [own.reshape([2] * (len(order) - 1) + list(own.shape[1:]))]
+    first = first.reshape(addends[0].shape)
+    addends.append(swap(first, *order[0]))
+    lead.remove(order[0])
+    for step in order[1:]:
+        got = scatter_step(addends, lead, step)
         addends, lead = scatter_rest(addends, lead, step, got)
     return total(addends)
 
@@ -654,9 +641,39 @@
         + [pl.BlockSpec(down_shape, lambda j: (0, 0, 0), pipeline_mode=one)] * 2,
         out_shape=[whole((up_shape, BF))] * 2 + [whole((down_shape, BF))] * 2,
         compiler_params=pltpu.CompilerParams(vmem_limit_bytes=LIMIT),
-        cost_estimate=cost(14),
+        cost_estimate=cost(1),
         name="weight_grads",
     )(owners, rows, scaled, hidden, grad_pre)
+
+
+def x_parts_kernel(place_ref, keep_ref, got_ref, own_ref, away_ref):
+    mine = (place_ref[0] // 2) % 2
+    for at in range(own_ref.shape[0]):
+        first = keep_ref[2 * at].astype(F32) + got_ref[2 * at].astype(F32)
+        second = keep_ref[2 * at + 1].astype(F32) + got_ref[2 * at + 1].astype(F32)
+        own_ref[at] = jnp.where(mine == 0, first, second)
+        away_ref[at] = jnp.where(mine == 0, second, first).astype(BF)
+
+
+def x_parts_call(owners, keep, got):
+    half, rows, width = keep.shape
+    tile = min(width, 768)
+    grid = width // tile
+
+    def block(count):
+        return pl.BlockSpec((count, rows, tile), lambda j: (0, 0, j))
+
+    own = (half // 2, rows, width)
+    return pl.pallas_call(
+        x_parts_kernel,
+        grid=(grid,),
+        in_specs=[pl.BlockSpec(memory_space=pltpu.SMEM), block(half), block(half)],
+        out_specs=[block(half // 2)] * 2,
+        out_shape=[whole((own, F32)), whole((own, BF))],
+        compiler_params=pltpu.CompilerParams(vmem_limit_bytes=LIMIT),
+        cost_estimate=cost(0),
+        name="x_parts",
+    )(owners, keep, got)
 
 
 def shards(
@@ -781,9 +798,11 @@
         owners, rnew, scaled, hidden, grad_pre
     )
     new_in = send(new_in, old_in)
-    ups = [up_keep, core_swap(after(up_send, old_in))]
-    downs = [down_keep, core_swap(after(down_send, old_in))]
-    gated = move(after(gated, new_in, ups, downs)).reshape(2 * count, width)
+    up_own, up_away = x_parts_call(owners, up_keep, core_swap(after(up_send, old_in)))
+    down_own, down_away = x_parts_call(owners, down_keep, core_swap(after(down_send, old_in)))
+    gated = move(after(gated, new_in, up_away, down_away)).reshape(2 * count, width)
+    new_w1_grad = scatter_dp(up_own, up_away)[None]
+    new_w2_grad = scatter_dp(down_own, down_away)[None]
     router_part = (old_router + new_router)[:experts]
 
     gmid, gctx, out_grad, sums_two = plain_call(
@@ -807,9 +826,6 @@
         vectors,
     )
     accumulators = [pltpu.VMEM((length, 2 * HEAD_DIM), F32)] * 2
-    ups_first, downs_first = [scatter_dp_first(after(sums, gctx)) for sums in (ups, downs)]
-    ups_x = scatter_dp(ups, ups_first)
-    downs_x = scatter_dp(downs, downs_first)
     half = lax.axis_size("dp") // 2
     gproj, *split = plain_call(
         attention_back_kernel,
@@ -819,7 +835,7 @@
         0,
         owners,
         proj,
-        after(gctx, ups_first, downs_first),
+        gctx,
         normed,
     )
     input_grad, sums_one = plain_call(
@@ -853,13 +869,22 @@
     rest = rest.reshape([2] * len(lead) + list(rest.shape[1:]))
     got = scatter_step([rest], lead, core[0])
     states.append(scatter_rest([rest], lead, core[0], got)[0])
-    states = after(states, gated, ups_x, downs_x)
     lefts = [left] * len(states)
+
+    def advance(chains, step_of):
+        found = {
+            p: scatter_step(states[p], lefts[p], scatter_ways[p][step_of(p)]) for p in chains
+        }
+        for p in chains:
+            step = scatter_ways[p][step_of(p)]
+            states[p], lefts[p] = scatter_rest(states[p], lefts[p], step, found[p])
+        return list(found.values())
+
+    ahead = ()
+    states = after(states, gated, new_w1_grad, new_w2_grad)
     for at in range(len(left)):
-        arrived = [
-            scatter_step(state, left, way[at])
-            for state, left, way in zip(states, lefts, scatter_ways)
-        ]
+        chains = [p for p in range(4) if at + (p in ahead) < len(left)]
+        arrived = advance(chains, lambda p: at + (p in ahead))
         if at == 0:
             (mixed,) = plain_call(
                 mixed_kernel,
@@ -870,18 +895,6 @@
                 target,
                 middle,
             )
-        if at == 1:
-            (ups, downs, ups_x, downs_x), _ = lax.optimization_barrier(
-                ((ups, downs, ups_x, downs_x), arrived)
-            )
-            new_w1_grad = scatter_dp_total(ups, ups_x)[None]
-            new_w2_grad = scatter_dp_total(downs, downs_x)[None]
-        pairs = [
-            scatter_rest(state, left, way[at], got)
-            for state, left, way, got in zip(states, lefts, scatter_ways, arrived)
-        ]
-        states = [pair[0] for pair in pairs]
-        lefts = [pair[1] for pair in pairs]
     sums = [total(state) for state in states]
     attn_in_grad = jnp.concatenate(sums[:3], axis=1).T
     attn_out_grad = sums[3][:share].T

time: 399 us -> 387 us (0.970)
  other arithmetic: 41.3 us -> 24.8 us
  waiting for transfers between devices: 111 us -> 101 us
  Pallas kernels: 135 us -> 144 us
    convert_element_type x18 -> x16, other arithmetic: 19.7 us -> 6.1 us  [away_part(): return send.astype(BF)]
    pallas_call x0 -> x2, Pallas kernels: none -> 9.5 us  [x_parts_call(): pl.pallas_call(x_parts_kernel, grid=(grid,), in_specs=[pl.BlockSpec(memor...]
    ppermute x51, waiting for transfers between devices: 97.4 us -> 91.6 us  [swap(): return lax.ppermute(values, axis, [(i, i ^ bit) for i in range(count)])]
    unnamed x70 -> x88, local copies, waits for them, and re-layouts: 11.7 us -> 16.3 us
  transfers between devices with their start and end apart: 57 -> 57, of which waited for: 23 -> 26; matrix products, arithmetic and copies ran while one was open for 13% -> 9% of each run, Pallas kernels for 34% -> 38%
where the time goes in v5:
time: 387 us; the launch traced here: 382 us
  Pallas kernels  144 us (37%)
  waiting for transfers between devices  101 us (26%)
  starting transfers between devices  77.3 us (20%)
  local copies, waits for them, and re-layouts  32.4 us (8%)
  other arithmetic  24.8 us (6%)
    ppermute x51, waiting for transfers between devices, swap(): return lax.ppermute(values, axis, [(i, i ^ bit) for i in range(count)])  91.6 us
    pallas_call x6, Pallas kernels, plain_call(): pl.pallas_call(body, out_shape=[whole(o) for o in outs], in_specs=[space]...  61.2 us
    pallas_call x2, Pallas kernels, expert_call(): pl.pallas_call(functools.partial(expert_kernel, train, steps, pieces), gr...  57.2 us
    ppermute x51, starting transfers between devices, swap(): return lax.ppermute(values, axis, [(i, i ^ bit) for i in range(count)])  47.1 us
    all_to_all x6, starting transfers between devices, move(): lax.all_to_all(block, 'expert', split_axis=0, concat_axis=0, tiled=True)  30.2 us
    pallas_call x1, Pallas kernels, weight_grads_call(): pl.pallas_call(functools.partial(weight_grads_kernel, pieces), grid=(f //...  16.4 us
    unnamed x88, local copies, waits for them, and re-layouts  16.3 us
    all_to_all x6, waiting for transfers between devices, move(): lax.all_to_all(block, 'expert', split_axis=0, concat_axis=0, tiled=True)  9.83 us
  transfers between devices with their start and end apart: 57, of which 26 were waited for; matrix products, arithmetic and copies ran while one was open for 9% of the time, Pallas kernels for 38%

profile of v5, /device:TPU:0, one launch (start us, length us, event | category | flops | bytes accessed | tf_op | source)
XLA Modules:
  0.0 382.1 jit_solution(15988158457201267389)
XLA Ops:
  23.9 4.3 %place_grads.1 = bf16[1792,768]{1,0:T(8,128)(2,1)} custom-call(s32[8,512]{1,0:T(8,128)} %pad.29.clone.target_ref, bf16[512,768]{1,0:T(8,128)(2,1)} %cot_ref.1), custom_call_target="tpu_custom_call" | custom-call | flops 1000000000 | tf_op jit(solution)/shard_map/place_grads/pallas_call | solution.py:172
  33.9 4.2 %collective-permute-done.8 = bf16[2,2,2,96,256]{4,3,2,1,0:T(8,128)(2,1)S(1)} collective-permute-done((bf16[2,2,2,96,256]{4,3,2,1,0:T(8,128)(2,1)S(1)}, bf16[2,2,2,96,256]{4,3,2,1,0:T(8,128)(2,1)S(1)}, u32[]{:S(2)}, u32[]{:S(2)}) %collective-permute-start.8) | collective-permute-done | bytes 393248 | tf_op jit(solution)/shard_map/ppermute | solution.py:31
  44.3 4.8 %all-to-all-start = ((bf16[8,2,112,768]{3,2,1,0:T(8,128)(2,1)}), bf16[8,2,112,768]{3,2,1,0:T(8,128)(2,1)}, u32[]{:S(2)}, u32[]{:S(2)}) async-start(bf16[8,2,112,768]{3,2,1,0:T(8,128)(2,1)} %bitcast.326), calls=%async_computation | async-start | bytes 5505024 | tf_op jit(solution)/shard_map/all_to_all | solution.py:742
  63.8 16.5 %attention_forward.1 = (bf16[512,768]{1,0:T(8,128)(2,1)}, bf16[512,2304]{1,0:T(8,128)(2,1)}, bf16[512,768]{1,0:T(8,128)(2,1)}, f32[512,768]{1,0:T(8,128)}, bf16[...) custom-call(bf16[512,768]{1,0:T(8,128)(2,1)} %x_ref.3, bf16[2304,256]{1,0:T(8,128)(2,1)} %bitcast.319, ...), custom_call_target="tpu_custom_call" | custom-call | flops 6750000128 | tf_op jit(solution)/shard_map/attention_forward/pallas_call | solution.py:172
  81.3 24.1 %collective-permute-done.16.rest_6_ = bf16[768,768]{1,0:T(8,128)(2,1)} collective-permute-done((bf16[768,768]{1,0:T(8,128)(2,1)}, bf16[768,768]{1,0:T(8,128)(2,1)}, u32[]{:S(2)}, u32[]{:S(2)}) %collective-permute-start.16) | collective-permute-done | bytes 1179680 | tf_op jit(solution)/shard_map/ppermute | solution.py:31
  109.3 4.6 %all-to-all-start.1 = ((bf16[8,112,768]{2,1,0:T(8,128)(2,1)}), bf16[8,112,768]{2,1,0:T(8,128)(2,1)S(1)}, u32[]{:S(2)}, u32[]{:S(2)}) async-start(bf16[8,112,768]{2,1,0:T(8,128)(2,1)} %bitcast.338), calls=%async_computation.1 | async-start | bytes 2752512 | tf_op jit(solution)/shard_map/all_to_all | solution.py:742
  115.9 25.2 %collective-permute-done.23.rest_2_ = bf16[192,3072]{1,0:T(8,128)(2,1)S(1)} collective-permute-done((bf16[192,3072]{1,0:T(8,128)(2,1)S(1)}, bf16[192,3072]{1,0:T(8,128)(2,1)S(1)}, u32[]{:S(2)}, u32[]{:S(2)}) %collective-permute-start.23) | collective-permute-done | bytes 1179680 | tf_op jit(solution)/shard_map/ppermute | solution.py:31
  146.5 3.9 %all-to-all-start.2 = ((bf16[8,112,768]{2,1,0:T(8,128)(2,1)}), bf16[8,112,768]{2,1,0:T(8,128)(2,1)S(1)}, u32[]{:S(2)}, u32[]{:S(2)}) async-start(bf16[8,112,768]{2,1,0:T(8,128)(2,1)} %bitcast.63), calls=%async_computation.2 | async-start | bytes 2752512 | tf_op jit(solution)/shard_map/all_to_all | solution.py:742
  154.1 27.4 %expert_old.1 = (bf16[8,2,112,768]{3,2,1,0:T(8,128)(2,1)}, bf16[896,768]{1,0:T(8,128)(2,1)}, f32[128,768]{1,0:T(8,128)}) custom-call(s32[4]{0:T(128)} %iota_xor_fusion.place_ref, f32[8,128]{1,0:T(8,128)} %get-tuple-element.185.mine_ref, bf16[896,768]{1,0:T(8,128)(2,1)} %bitcast.337, bf16[8,2,112,768]{3,2,1,0:T(8,128)(2,1)} %all-to-all-done.grads4_ref, ...), custom_call_target="tpu_custom_call" | custom-call | flops 7249999872 | tf_op jit(solution)/shard_map/expert_old/pallas_call | solution.py:558
  183.3 4.7 %all-to-all-start.3 = ((bf16[8,112,768]{2,1,0:T(8,128)(2,1)}), bf16[8,112,768]{2,1,0:T(8,128)(2,1)S(1)}, u32[]{:S(2)}, u32[]{:S(2)}) async-start(bf16[8,112,768]{2,1,0:T(8,128)(2,1)} %bitcast.340), calls=%async_computation.3 | async-start | bytes 2752512 | tf_op jit(solution)/shard_map/all_to_all | solution.py:742
  192.2 29.8 %expert_new.1 = (bf16[8,2,112,768]{3,2,1,0:T(8,128)(2,1)}, bf16[896,768]{1,0:T(8,128)(2,1)}, f32[128,768]{1,0:T(8,128)}, bf16[896,3072]{1,0:T(8,128)(2,1)}, bf16...) custom-call(s32[4]{0:T(128)} %iota_xor_fusion.place_ref, ...), custom_call_target="tpu_custom_call", output_to_operand_aliasing={{0}: (13, {})} | custom-call | flops 7249999872 | tf_op jit(solution)/shard_map/expert_new/pallas_call | solution.py:558
  222.0 6.0 %all-to-all-start.4 = ((bf16[8,112,768]{2,1,0:T(8,128)(2,1)}), bf16[8,112,768]{2,1,0:T(8,128)(2,1)S(1)}, u32[]{:S(2)}, u32[]{:S(2)}) async-start(bf16[8,112,768]{2,1,0:T(8,128)(2,1)} %bitcast.339), calls=%async_computation.4 | async-start | bytes 2752512 | tf_op jit(solution)/shard_map/all_to_all | solution.py:742
  228.0 16.4 %weight_grads.1 = (bf16[2,192,3072]{2,1,0:T(8,128)(2,1)}, bf16[2,192,3072]{2,1,0:T(8,128)(2,1)}, bf16[2,768,768]{2,1,0:T(8,128)(2,1)}, bf16[2,768,768]{2,1,0:T(8,128)(2,1)}) custom-call(s32[4]{0:T(128)} %iota_xor_fusion.place_ref, bf16[896,768]{1,0:T(8,128)(2,1)} %bitcast.314, bf16[896,768]{1,0:T(8,128)(2,1)} %get-tuple-element.100.scaled_ref, ...), custom_call_target="tpu_custom_call" | custom-call | flops 250000000 | tf_op jit(solution)/shard_map/weight_grads/pallas_call | solution.py:636
  245.0 4.2 %collective-permute-done.28.got_ref = bf16[2,768,768]{2,1,0:T(8,128)(2,1)S(1)} collective-permute-done((bf16[2,768,768]{2,1,0:T(8,128)(2,1)}, bf16[2,768,768]{2,1,0:T(8,128)(2,1)S(1)}, u32[]{:S(2)}, u32[]{:S(2)}) %collective-permute-start.28) | collective-permute-done | bytes 2359328 | tf_op jit(solution)/shard_map/ppermute | solution.py:31
  250.7 4.7 %x_parts.3 = (f32[1,768,768]{2,1,0:T(8,128)}, bf16[1,768,768]{2,1,0:T(8,128)(2,1)}) custom-call(s32[4]{0:T(128)} %iota_xor_fusion.place_ref, bf16[2,768,768]{2,1,0:T(8,128)(2,1)} %get-tuple-element.107.keep_ref, bf16[2,768,768]{2,1,0:T(8,128)(2,1)} %copy-done.6), custom_call_target="tpu_custom_call" | custom-call | tf_op jit(solution)/shard_map/x_parts/pallas_call | solution.py:667
  256.8 4.8 %x_parts.2 = (f32[1,192,3072]{2,1,0:T(8,128)}, bf16[1,192,3072]{2,1,0:T(8,128)(2,1)}) custom-call(s32[4]{0:T(128)} %iota_xor_fusion.place_ref, bf16[2,192,3072]{2,1,0:T(8,128)(2,1)} %get-tuple-element.103.keep_ref, bf16[2,192,3072]{2,1,0:T(8,128)(2,1)} %copy-done.5), custom_call_target="tpu_custom_call" | custom-call | tf_op jit(solution)/shard_map/x_parts/pallas_call | solution.py:667
  262.7 6.2 %all-to-all-start.5 = ((bf16[8,2,112,768]{3,2,1,0:T(8,128)(2,1)}), bf16[8,2,112,768]{3,2,1,0:T(8,128)(2,1)S(1)}, u32[]{:S(2)}, u32[]{:S(2)}) async-start(bf16[8,2,112,768]{3,2,1,0:T(8,128)(2,1)} %get-tuple-element.111), calls=%async_computation.5 | async-start | bytes 5505024 | tf_op jit(solution)/shard_map/all_to_all | solution.py:742
  271.9 8.5 %branch_backward.1 = (f32[512,768]{1,0:T(8,128)}, bf16[512,768]{1,0:T(8,128)(2,1)}, bf16[768,768]{1,0:T(8,128)(2,1)}, f32[8,768]{1,0:T(8,128)}) custom-call(bf16[896,768]{1,0:T(8,128)(2,1)} %bitcast.311, bf16[896,768]{1,0:T(8,128)(2,1)} %bitcast.312, s32[512,2]{1,0:T(8,128)} %copy-done.4, bf16[512,768]{1,0:T(8,128)(2,1)} %cot_ref.1, ...), custom_call_target="tpu_custom_call" | custom-call | tf_op jit(solution)/shard_map/branch_backward/pallas_call | solution.py:172
  280.4 19.6 %attention_backward.1 = (bf16[512,2304]{1,0:T(8,128)(2,1)}, bf16[2,576,256]{2,1,0:T(8,128)(2,1)}, bf16[2,576,256]{2,1,0:T(8,128)(2,1)}, bf16[2,576,256]{2,1,0:T(...) custom-call(s32[4]{0:T(128)} %iota_xor_fusion.place_ref, ...), custom_call_target="tpu_custom_call" | custom-call | tf_op jit(solution)/shard_map/attention_backward/pallas_call | solution.py:172
  300.1 7.1 %input_backward.1 = (f32[512,768]{1,0:T(8,128)}, f32[8,768]{1,0:T(8,128)}) custom-call(bf16[512,2304]{1,0:T(8,128)(2,1)} %get-tuple-element.123.gproj_ref, bf16[2304,256]{1,0:T(8,128)(2,1)} %bitcast.320, bf16[2304,256]{1,0:T(8,128)(2,1)} %bitcast.318, bf16[2304,256]{1,0:T(8,128)(2,1)} %bitcast.316, bf16[512,768]{1,0:T(8,128)(2,1)} %x_ref.3, ...), custom_call_target="tpu_custom_call" | custom-call | tf_op jit(solution)/shard_map/input_backward/pallas_call | solution.py:172
  315.8 6.5 %collective-permute-done.34 = bf16[768,768]{1,0:T(8,128)(2,1)} collective-permute-done((bf16[768,768]{1,0:T(8,128)(2,1)}, bf16[768,768]{1,0:T(8,128)(2,1)}, u32[]{:S(2)}, u32[]{:S(2)}) %collective-permute-start.34) | collective-permute-done | bytes 1179680 | tf_op jit(solution)/shard_map/ppermute | solution.py:31
  327.2 4.2 %all-to-all-done.5 = bf16[8,2,112,768]{3,2,1,0:T(8,128)(2,1)S(1)} async-done(((bf16[8,2,112,768]{3,2,1,0:T(8,128)(2,1)}), bf16[8,2,112,768]{3,2,1,0:T(8,128)(2,1)S(1)}, u32[]{:S(2)}, u32[]{:S(2)}) %all-to-all-start.5) | async-done | bytes 2752544 | tf_op jit(solution)/shard_map/all_to_all | solution.py:742
  338.3 4.9 %collective-permute-done.35 = bf16[2,2,2,72,256]{4,3,2,1,0:T(8,128)(2,1)S(1)} collective-permute-done((bf16[2,2,2,72,256]{4,3,2,1,0:T(8,128)(2,1)S(1)}, bf16[2,2,2,72,256]{4,3,2,1,0:T(8,128)(2,1)S(1)}, u32[]{:S(2)}, u32[]{:S(2)}) %collective-permute-start.35) | collective-permute-done | bytes 294944 | tf_op jit(solution)/shard_map/ppermute | solution.py:31
  352.3 5.1 %mixed_output.1 = bf16[512,768]{1,0:T(8,128)(2,1)} custom-call(bf16[1792,768]{1,0:T(8,128)(2,1)} %bitcast.303, s32[512,2]{1,0:T(8,128)} %copy-done.9, f32[512,768]{1,0:T(8,128)} %get-tuple-element.113.middle_ref), custom_call_target="tpu_custom_call" | custom-call | flops 1250000000 | tf_op jit(solution)/shard_map/mixed_output/pallas_call | solution.py:172
  (299 shorter events, 132.3 us)
Async XLA Ops:
  44.3 65.0 %all-to-all-start = ((bf16[8,2,112,768]{3,2,1,0:T(8,128)(2,1)}), bf16[8,2,112,768]{3,2,1,0:T(8,128)(2,1)}, u32[]{:S(2)}, u32[]{:S(2)}) async-start(bf16[8,2,112,768]{3,2,1,0:T(8,128)(2,1)} %bitcast.326), calls=%async_computation | async-start | bytes 5505024 | tf_op jit(solution)/shard_map/all_to_all | solution.py:742
  51.5 29.4 %collective-permute-start.15 = (bf16[192,3072]{1,0:T(8,128)(2,1)}, bf16[192,3072]{1,0:T(8,128)(2,1)}, u32[]{:S(2)}, u32[]{:S(2)}) collective-permute-start(bf16[192,3072]{1,0:T(8,128)(2,1)} %bitcast.381), channel_id=1, source_target_pairs={{0,16},{8,24},{16,0},{24,8},{1,17},{9,25},{17,1},{25,9},{2,18},{10... | collective-permute-start | bytes 3538952 | tf_op jit(solution)/shard_map/ppermute | solution.py:31
  53.0 52.4 %collective-permute-start.16 = (bf16[768,768]{1,0:T(8,128)(2,1)}, bf16[768,768]{1,0:T(8,128)(2,1)}, u32[]{:S(2)}, u32[]{:S(2)}) collective-permute-start(bf16[768,768]{1,0:T(8,128)(2,1)} %bitcast.384), channel_id=1, source_target_pairs={{0,16},{8,24},{16,0},{24,8},{1,17},{9,25},{17,1},{25,9},{2,18},{10... | collective-permute-start | bytes 3538952 | tf_op jit(solution)/shard_map/ppermute | solution.py:31
  80.3 25.1 %collective-permute-start.17 = (bf16[192,3072]{1,0:T(8,128)(2,1)S(1)}, bf16[192,3072]{1,0:T(8,128)(2,1)S(1)}, u32[]{:S(2)}, u32[]{:S(2)}) collective-permute-start(bf16[192,3072]{1,0:T(8,128)(2,1)S(1)} %bitcast.383), channel_id=1, source_target_pairs={{0,8},{8,0},{16,24},{24,16},{1,9},{9,1},{17,25},{25,17},{2,10},{10... | collective-permute-start | bytes 3538952 | tf_op jit(solution)/shard_map/ppermute | solution.py:31
  80.3 25.1 %collective-permute-start.18 = (bf16[768,768]{1,0:T(8,128)(2,1)S(1)}, bf16[768,768]{1,0:T(8,128)(2,1)S(1)}, u32[]{:S(2)}, u32[]{:S(2)}) collective-permute-start(bf16[768,768]{1,0:T(8,128)(2,1)S(1)} %bitcast.386), channel_id=1, source_target_pairs={{0,8},{8,0},{16,24},{24,16},{1,9},{9,1},{17,25},{25,17},{2,10},{10... | collective-permute-start | bytes 3538952 | tf_op jit(solution)/shard_map/ppermute | solution.py:31
  80.8 24.6 %collective-permute-start.19 = (bf16[192,3072]{1,0:T(8,128)(2,1)S(1)}, bf16[192,3072]{1,0:T(8,128)(2,1)S(1)}, u32[]{:S(2)}, u32[]{:S(2)}) collective-permute-start(bf16[192,3072]{1,0:T(8,128)(2,1)S(1)} %bitcast.388), channel_id=1, source_target_pairs={{0,8},{8,0},{16,24},{24,16},{1,9},{9,1},{17,25},{25,17},{2,10},{10... | collective-permute-start | bytes 3538952 | tf_op jit(solution)/shard_map/ppermute | solution.py:31
  80.9 27.0 %collective-permute-start.20 = (bf16[768,768]{1,0:T(8,128)(2,1)S(1)}, bf16[768,768]{1,0:T(8,128)(2,1)}, u32[]{:S(2)}, u32[]{:S(2)}) collective-permute-start(bf16[768,768]{1,0:T(8,128)(2,1)S(1)} %bitcast.392), channel_id=1, source_target_pairs={{0,8},{8,0},{16,24},{24,16},{1,9},{9,1},{17,25},{25,17},{2,10},{10... | collective-permute-start | bytes 3538952 | tf_op jit(solution)/shard_map/ppermute | solution.py:31
  109.3 37.2 %all-to-all-start.1 = ((bf16[8,112,768]{2,1,0:T(8,128)(2,1)}), bf16[8,112,768]{2,1,0:T(8,128)(2,1)S(1)}, u32[]{:S(2)}, u32[]{:S(2)}) async-start(bf16[8,112,768]{2,1,0:T(8,128)(2,1)} %bitcast.338), calls=%async_computation.1 | async-start | bytes 2752512 | tf_op jit(solution)/shard_map/all_to_all | solution.py:742
  113.9 27.3 %collective-permute-start.23 = (bf16[192,3072]{1,0:T(8,128)(2,1)S(1)}, bf16[192,3072]{1,0:T(8,128)(2,1)S(1)}, u32[]{:S(2)}, u32[]{:S(2)}) collective-permute-start(bf16[192,3072]{1,0:T(8,128)(2,1)S(1)} %bitcast.389), channel_id=1, source_target_pairs={{0,16},{8,24},{16,0},{24,8},{1,17},{9,25},{17,1},{25,9},{2,18},{10... | collective-permute-start | bytes 3538952 | tf_op jit(solution)/shard_map/ppermute | solution.py:31
  115.4 25.7 %collective-permute-start.21 = (bf16[192,3072]{1,0:T(8,128)(2,1)}, bf16[192,3072]{1,0:T(8,128)(2,1)S(1)}, u32[]{:S(2)}, u32[]{:S(2)}) collective-permute-start(bf16[192,3072]{1,0:T(8,128)(2,1)} %collective-permute-done.15.rest_2_), channel_id=1, source_target_pairs={{0,8},{8,0},{16,24},{24,16},{1,9},{9,1},{17,25},{25,17},{2,10},{10... | collective-permute-start | bytes 3538952 | tf_op jit(solution)/shard_map/ppermute | solution.py:31
  115.4 25.7 %collective-permute-start.22 = (bf16[768,768]{1,0:T(8,128)(2,1)}, bf16[768,768]{1,0:T(8,128)(2,1)S(1)}, u32[]{:S(2)}, u32[]{:S(2)}) collective-permute-start(bf16[768,768]{1,0:T(8,128)(2,1)} %collective-permute-done.16.rest_6_), channel_id=1, source_target_pairs={{0,8},{8,0},{16,24},{24,16},{1,9},{9,1},{17,25},{25,17},{2,10},{10... | collective-permute-start | bytes 3538952 | tf_op jit(solution)/shard_map/ppermute | solution.py:31
  146.5 36.8 %all-to-all-start.2 = ((bf16[8,112,768]{2,1,0:T(8,128)(2,1)}), bf16[8,112,768]{2,1,0:T(8,128)(2,1)S(1)}, u32[]{:S(2)}, u32[]{:S(2)}) async-start(bf16[8,112,768]{2,1,0:T(8,128)(2,1)} %bitcast.63), calls=%async_computation.2 | async-start | bytes 2752512 | tf_op jit(solution)/shard_map/all_to_all | solution.py:742
  152.6 35.5 %collective-permute-start.25 = (bf16[768,768]{1,0:T(8,128)(2,1)}, bf16[768,768]{1,0:T(8,128)(2,1)}, u32[]{:S(2)}, u32[]{:S(2)}) collective-permute-start(bf16[768,768]{1,0:T(8,128)(2,1)} %bitcast.390), channel_id=1, source_target_pairs={{0,16},{8,24},{16,0},{24,8},{1,17},{9,25},{17,1},{25,9},{2,18},{10... | collective-permute-start | bytes 3538952 | tf_op jit(solution)/shard_map/ppermute | solution.py:31
  183.3 38.7 %all-to-all-start.3 = ((bf16[8,112,768]{2,1,0:T(8,128)(2,1)}), bf16[8,112,768]{2,1,0:T(8,128)(2,1)S(1)}, u32[]{:S(2)}, u32[]{:S(2)}) async-start(bf16[8,112,768]{2,1,0:T(8,128)(2,1)} %bitcast.340), calls=%async_computation.3 | async-start | bytes 2752512 | tf_op jit(solution)/shard_map/all_to_all | solution.py:742
  222.0 39.6 %all-to-all-start.4 = ((bf16[8,112,768]{2,1,0:T(8,128)(2,1)}), bf16[8,112,768]{2,1,0:T(8,128)(2,1)S(1)}, u32[]{:S(2)}, u32[]{:S(2)}) async-start(bf16[8,112,768]{2,1,0:T(8,128)(2,1)} %bitcast.339), calls=%async_computation.4 | async-start | bytes 2752512 | tf_op jit(solution)/shard_map/all_to_all | solution.py:742
  262.7 68.7 %all-to-all-start.5 = ((bf16[8,2,112,768]{3,2,1,0:T(8,128)(2,1)}), bf16[8,2,112,768]{3,2,1,0:T(8,128)(2,1)S(1)}, u32[]{:S(2)}, u32[]{:S(2)}) async-start(bf16[8,2,112,768]{3,2,1,0:T(8,128)(2,1)} %get-tuple-element.111), calls=%async_computation.5 | async-start | bytes 5505024 | tf_op jit(solution)/shard_map/all_to_all | solution.py:742
  269.0 43.0 %collective-permute-start.33 = (bf16[192,3072]{1,0:T(8,128)(2,1)}, bf16[192,3072]{1,0:T(8,128)(2,1)}, u32[]{:S(2)}, u32[]{:S(2)}) collective-permute-start(bf16[192,3072]{1,0:T(8,128)(2,1)} %bitcast.394), channel_id=1, source_target_pairs={{0,16},{8,24},{16,0},{24,8},{1,17},{9,25},{17,1},{25,9},{2,18},{10... | collective-permute-start | bytes 3538952 | tf_op jit(solution)/shard_map/ppermute | solution.py:31
  270.0 52.4 %collective-permute-start.34 = (bf16[768,768]{1,0:T(8,128)(2,1)}, bf16[768,768]{1,0:T(8,128)(2,1)}, u32[]{:S(2)}, u32[]{:S(2)}) collective-permute-start(bf16[768,768]{1,0:T(8,128)(2,1)} %bitcast.393), channel_id=1, source_target_pairs={{0,16},{8,24},{16,0},{24,8},{1,17},{9,25},{17,1},{25,9},{2,18},{10... | collective-permute-start | bytes 3538952 | tf_op jit(solution)/shard_map/ppermute | solution.py:31
  310.7 16.6 %collective-permute-start.32 = (bf16[2,2,2,2,32,768]{5,4,1,3,2,0:T(8,128)(2,1)S(1)}, bf16[2,2,2,2,32,768]{5,4,1,3,2,0:T(8,128)(2,1)}, u32[]{:S(2)}, u32[]{:S(2)}) collective-permute-start(bf16[2,2,2,2,32,768]{5,4,1,3,2,0:T(8,128)(2,1)S(1)} %bitcast.342), channel_id=1, source_target_pairs={{0,8},{8,0},{16,24},{24,16},{1,9},{9,1},{17,25},{25,17},{2,10},{10... | collective-permute-start | bytes 2359304 | tf_op jit(solution)/shard_map/ppermute | solution.py:31
  311.5 13.9 %collective-permute-start.29 = (bf16[2,576,256]{2,1,0:T(8,128)(2,1)S(1)}, bf16[2,576,256]{2,1,0:T(8,128)(2,1)S(1)}, u32[]{:S(2)}, u32[]{:S(2)}) collective-permute-start(bf16[2,576,256]{2,1,0:T(8,128)(2,1)S(1)} %copy-done.40), channel_id=1, source_target_pairs={{0,8},{8,0},{16,24},{24,16},{1,9},{9,1},{17,25},{25,17},{2,10},{10... | collective-permute-start | bytes 1769480 | tf_op jit(solution)/shard_map/ppermute | solution.py:31
  335.3 14.3 %collective-permute-start.38 = (bf16[2,2,2,32,768]{4,3,2,1,0:T(8,128)(2,1)S(1)}, bf16[2,2,2,32,768]{4,3,2,1,0:T(8,128)(2,1)S(1)}, u32[]{:S(2)}, u32[]{:S(2)}) collective-permute-start(bf16[2,2,2,32,768]{4,3,2,1,0:T(8,128)(2,1)S(1)} %copy.128), channel_id=1, source_target_pairs={{0,16},{8,24},{16,0},{24,8},{1,17},{9,25},{17,1},{25,9},{2,18},{10... | collective-permute-start | bytes 1179656 | tf_op jit(solution)/shard_map/ppermute | solution.py:31
  343.3 14.2 %collective-permute-start.39 = (bf16[2,2,72,256]{3,2,1,0:T(8,128)(2,1)S(1)}, bf16[2,2,72,256]{3,2,1,0:T(8,128)(2,1)S(1)}, u32[]{:S(2)}, u32[]{:S(2)}) collective-permute-start(bf16[2,2,72,256]{3,2,1,0:T(8,128)(2,1)S(1)} %fusion.11), channel_id=1, source_target_pairs={{0,1},{1,0},{2,3},{3,2},{4,5},{5,4},{6,7},{7,6},{8,9},{9,8},{10,11... | collective-permute-start | bytes 442376 | tf_op jit(solution)/shard_map/ppermute | solution.py:31
  346.6 14.0 %collective-permute-start.45 = (bf16[2,2,72,256]{3,2,1,0:T(8,128)(2,1)S(1)}, bf16[2,2,72,256]{3,2,1,0:T(8,128)(2,1)S(1)}, u32[]{:S(2)}, u32[]{:S(2)}) collective-permute-start(bf16[2,2,72,256]{3,2,1,0:T(8,128)(2,1)S(1)} %fusion.9), channel_id=1, source_target_pairs={{0,4},{1,5},{2,6},{3,7},{4,0},{5,1},{6,2},{7,3},{8,12},{9,13},{10,... | collective-permute-start | bytes 442376 | tf_op jit(solution)/shard_map/ppermute | solution.py:31
  350.7 16.8 %collective-permute-start.48 = (bf16[2,2,32,768]{3,2,1,0:T(8,128)(2,1)S(1)}, bf16[2,2,32,768]{3,2,1,0:T(8,128)(2,1)S(1)}, u32[]{:S(2)}, u32[]{:S(2)}) collective-permute-start(bf16[2,2,32,768]{3,2,1,0:T(8,128)(2,1)S(1)} %copy.141), channel_id=1, source_target_pairs={{0,1},{1,0},{2,3},{3,2},{4,5},{5,4},{6,7},{7,6},{8,9},{9,8},{10,11... | collective-permute-start | bytes 589832 | tf_op jit(solution)/shard_map/ppermute | solution.py:31
  (74 other events, 473.2 us)

commit v6 on v5

--- a/solution.py
+++ b/solution.py
@@ -716,10 +716,10 @@
         cols = slice(p * third, (p + 1) * third)
         rows = [in_t[:, cols], out_t[:, cols]] + ([small] if p == 0 else [])
         states.append((jnp.concatenate(rows, axis=0), []))
-    states = [gather_steps(states[p], ways[p][:2]) for p in range(3)]
+    states = [gather_steps(states[p], ways[p][:3]) for p in range(3)]
     shards_dp = [old_w1[0], old_w2[0], new_w1[0], new_w2[0]]
     early = [state[0] for state in states]
-    states = [gather_steps(states[p], ways[p][2:-1]) for p in range(3)]
+    states = [gather_steps(states[p], ways[p][3:-1]) for p in range(3)]
     between = [state[0] for state in states]
     parts = [gather_finish(gather_steps(states[p], ways[p][-1:])) for p in range(3)]
     parts = [part.reshape(devices, -1, third) for part in parts]

time: 387 us -> 387 us (level)
  transfers between devices with their start and end apart: 57 -> 57, of which waited for: 26 -> 25; matrix products, arithmetic and copies ran while one was open for 9% -> 9% of each run, Pallas kernels for 38% -> 38%
where the time goes in v6:
time: 387 us; the launch traced here: 382 us
  Pallas kernels  144 us (37%)
  waiting for transfers between devices  102 us (26%)
  starting transfers between devices  76.6 us (20%)
  local copies, waits for them, and re-layouts  32.4 us (8%)
  other arithmetic  24.8 us (6%)
    ppermute x51, waiting for transfers between devices, swap(): return lax.ppermute(values, axis, [(i, i ^ bit) for i in range(count)])  92.3 us
    pallas_call x6, Pallas kernels, plain_call(): pl.pallas_call(body, out_shape=[whole(o) for o in outs], in_specs=[space]...  61.2 us
    pallas_call x2, Pallas kernels, expert_call(): pl.pallas_call(functools.partial(expert_kernel, train, steps, pieces), gr...  57.2 us
    ppermute x51, starting transfers between devices, swap(): return lax.ppermute(values, axis, [(i, i ^ bit) for i in range(count)])  46.4 us
    all_to_all x6, starting transfers between devices, move(): lax.all_to_all(block, 'expert', split_axis=0, concat_axis=0, tiled=True)  30.2 us
    pallas_call x1, Pallas kernels, weight_grads_call(): pl.pallas_call(functools.partial(weight_grads_kernel, pieces), grid=(f //...  16.4 us
    unnamed x88, local copies, waits for them, and re-layouts  16.3 us
    all_to_all x6, waiting for transfers between devices, move(): lax.all_to_all(block, 'expert', split_axis=0, concat_axis=0, tiled=True)  9.82 us
  transfers between devices with their start and end apart: 57, of which 25 were waited for; matrix products, arithmetic and copies ran while one was open for 9% of the time, Pallas kernels for 38%

profile of v6, /device:TPU:0, one launch (start us, length us, event | category | flops | bytes accessed | tf_op | source)
XLA Modules:
  0.0 382.1 jit_solution(7261570904996605760)
XLA Ops:
  23.9 4.9 %collective-permute-done.7 = bf16[2,2,96,256]{3,2,1,0:T(8,128)(2,1)S(1)} collective-permute-done((bf16[2,2,96,256]{3,2,1,0:T(8,128)(2,1)S(1)}, bf16[2,2,96,256]{3,2,1,0:T(8,128)(2,1)S(1)}, u32[]{:S(2)}, u32[]{:S(2)}) %collective-permute-start.7) | collective-permute-done | bytes 196640 | tf_op jit(solution)/shard_map/ppermute | solution.py:31
  33.9 4.3 %place_grads.1 = bf16[1792,768]{1,0:T(8,128)(2,1)} custom-call(s32[8,512]{1,0:T(8,128)} %pad.29.clone.target_ref, bf16[512,768]{1,0:T(8,128)(2,1)} %cot_ref.1), custom_call_target="tpu_custom_call" | custom-call | flops 1000000000 | tf_op jit(solution)/shard_map/place_grads/pallas_call | solution.py:172
  44.3 4.8 %all-to-all-start = ((bf16[8,2,112,768]{3,2,1,0:T(8,128)(2,1)}), bf16[8,2,112,768]{3,2,1,0:T(8,128)(2,1)}, u32[]{:S(2)}, u32[]{:S(2)}) async-start(bf16[8,2,112,768]{3,2,1,0:T(8,128)(2,1)} %bitcast.326), calls=%async_computation | async-start | bytes 5505024 | tf_op jit(solution)/shard_map/all_to_all | solution.py:742
  63.8 16.5 %attention_forward.1 = (bf16[512,768]{1,0:T(8,128)(2,1)}, bf16[512,2304]{1,0:T(8,128)(2,1)}, bf16[512,768]{1,0:T(8,128)(2,1)}, f32[512,768]{1,0:T(8,128)}, bf16[...) custom-call(bf16[512,768]{1,0:T(8,128)(2,1)} %x_ref.3, bf16[2304,256]{1,0:T(8,128)(2,1)} %bitcast.319, ...), custom_call_target="tpu_custom_call" | custom-call | flops 6750000128 | tf_op jit(solution)/shard_map/attention_forward/pallas_call | solution.py:172
  81.3 24.1 %collective-permute-done.16.rest_6_ = bf16[768,768]{1,0:T(8,128)(2,1)} collective-permute-done((bf16[768,768]{1,0:T(8,128)(2,1)}, bf16[768,768]{1,0:T(8,128)(2,1)}, u32[]{:S(2)}, u32[]{:S(2)}) %collective-permute-start.16) | collective-permute-done | bytes 1179680 | tf_op jit(solution)/shard_map/ppermute | solution.py:31
  109.3 4.6 %all-to-all-start.1 = ((bf16[8,112,768]{2,1,0:T(8,128)(2,1)}), bf16[8,112,768]{2,1,0:T(8,128)(2,1)S(1)}, u32[]{:S(2)}, u32[]{:S(2)}) async-start(bf16[8,112,768]{2,1,0:T(8,128)(2,1)} %bitcast.338), calls=%async_computation.1 | async-start | bytes 2752512 | tf_op jit(solution)/shard_map/all_to_all | solution.py:742
  115.9 25.2 %collective-permute-done.23.rest_2_ = bf16[192,3072]{1,0:T(8,128)(2,1)S(1)} collective-permute-done((bf16[192,3072]{1,0:T(8,128)(2,1)S(1)}, bf16[192,3072]{1,0:T(8,128)(2,1)S(1)}, u32[]{:S(2)}, u32[]{:S(2)}) %collective-permute-start.23) | collective-permute-done | bytes 1179680 | tf_op jit(solution)/shard_map/ppermute | solution.py:31
  146.5 3.9 %all-to-all-start.2 = ((bf16[8,112,768]{2,1,0:T(8,128)(2,1)}), bf16[8,112,768]{2,1,0:T(8,128)(2,1)S(1)}, u32[]{:S(2)}, u32[]{:S(2)}) async-start(bf16[8,112,768]{2,1,0:T(8,128)(2,1)} %bitcast.63), calls=%async_computation.2 | async-start | bytes 2752512 | tf_op jit(solution)/shard_map/all_to_all | solution.py:742
  154.1 27.4 %expert_old.1 = (bf16[8,2,112,768]{3,2,1,0:T(8,128)(2,1)}, bf16[896,768]{1,0:T(8,128)(2,1)}, f32[128,768]{1,0:T(8,128)}) custom-call(s32[4]{0:T(128)} %iota_xor_fusion.place_ref, f32[8,128]{1,0:T(8,128)} %get-tuple-element.185.mine_ref, bf16[896,768]{1,0:T(8,128)(2,1)} %bitcast.337, bf16[8,2,112,768]{3,2,1,0:T(8,128)(2,1)} %all-to-all-done.grads4_ref, ...), custom_call_target="tpu_custom_call" | custom-call | flops 7249999872 | tf_op jit(solution)/shard_map/expert_old/pallas_call | solution.py:558
  183.3 4.7 %all-to-all-start.3 = ((bf16[8,112,768]{2,1,0:T(8,128)(2,1)}), bf16[8,112,768]{2,1,0:T(8,128)(2,1)S(1)}, u32[]{:S(2)}, u32[]{:S(2)}) async-start(bf16[8,112,768]{2,1,0:T(8,128)(2,1)} %bitcast.340), calls=%async_computation.3 | async-start | bytes 2752512 | tf_op jit(solution)/shard_map/all_to_all | solution.py:742
  192.2 29.8 %expert_new.1 = (bf16[8,2,112,768]{3,2,1,0:T(8,128)(2,1)}, bf16[896,768]{1,0:T(8,128)(2,1)}, f32[128,768]{1,0:T(8,128)}, bf16[896,3072]{1,0:T(8,128)(2,1)}, bf16...) custom-call(s32[4]{0:T(128)} %iota_xor_fusion.place_ref, ...), custom_call_target="tpu_custom_call", output_to_operand_aliasing={{0}: (13, {})} | custom-call | flops 7249999872 | tf_op jit(solution)/shard_map/expert_new/pallas_call | solution.py:558
  222.0 6.0 %all-to-all-start.4 = ((bf16[8,112,768]{2,1,0:T(8,128)(2,1)}), bf16[8,112,768]{2,1,0:T(8,128)(2,1)S(1)}, u32[]{:S(2)}, u32[]{:S(2)}) async-start(bf16[8,112,768]{2,1,0:T(8,128)(2,1)} %bitcast.339), calls=%async_computation.4 | async-start | bytes 2752512 | tf_op jit(solution)/shard_map/all_to_all | solution.py:742
  228.1 16.4 %weight_grads.1 = (bf16[2,192,3072]{2,1,0:T(8,128)(2,1)}, bf16[2,192,3072]{2,1,0:T(8,128)(2,1)}, bf16[2,768,768]{2,1,0:T(8,128)(2,1)}, bf16[2,768,768]{2,1,0:T(8,128)(2,1)}) custom-call(s32[4]{0:T(128)} %iota_xor_fusion.place_ref, bf16[896,768]{1,0:T(8,128)(2,1)} %bitcast.314, bf16[896,768]{1,0:T(8,128)(2,1)} %get-tuple-element.100.scaled_ref, ...), custom_call_target="tpu_custom_call" | custom-call | flops 250000000 | tf_op jit(solution)/shard_map/weight_grads/pallas_call | solution.py:636
  245.0 4.2 %collective-permute-done.28.got_ref = bf16[2,768,768]{2,1,0:T(8,128)(2,1)S(1)} collective-permute-done((bf16[2,768,768]{2,1,0:T(8,128)(2,1)}, bf16[2,768,768]{2,1,0:T(8,128)(2,1)S(1)}, u32[]{:S(2)}, u32[]{:S(2)}) %collective-permute-start.28) | collective-permute-done | bytes 2359328 | tf_op jit(solution)/shard_map/ppermute | solution.py:31
  250.7 4.7 %x_parts.3 = (f32[1,768,768]{2,1,0:T(8,128)}, bf16[1,768,768]{2,1,0:T(8,128)(2,1)}) custom-call(s32[4]{0:T(128)} %iota_xor_fusion.place_ref, bf16[2,768,768]{2,1,0:T(8,128)(2,1)} %get-tuple-element.107.keep_ref, bf16[2,768,768]{2,1,0:T(8,128)(2,1)} %copy-done.6), custom_call_target="tpu_custom_call" | custom-call | tf_op jit(solution)/shard_map/x_parts/pallas_call | solution.py:667
  256.8 4.8 %x_parts.2 = (f32[1,192,3072]{2,1,0:T(8,128)}, bf16[1,192,3072]{2,1,0:T(8,128)(2,1)}) custom-call(s32[4]{0:T(128)} %iota_xor_fusion.place_ref, bf16[2,192,3072]{2,1,0:T(8,128)(2,1)} %get-tuple-element.103.keep_ref, bf16[2,192,3072]{2,1,0:T(8,128)(2,1)} %copy-done.5), custom_call_target="tpu_custom_call" | custom-call | tf_op jit(solution)/shard_map/x_parts/pallas_call | solution.py:667
  262.8 6.2 %all-to-all-start.5 = ((bf16[8,2,112,768]{3,2,1,0:T(8,128)(2,1)}), bf16[8,2,112,768]{3,2,1,0:T(8,128)(2,1)S(1)}, u32[]{:S(2)}, u32[]{:S(2)}) async-start(bf16[8,2,112,768]{3,2,1,0:T(8,128)(2,1)} %get-tuple-element.111), calls=%async_computation.5 | async-start | bytes 5505024 | tf_op jit(solution)/shard_map/all_to_all | solution.py:742
  271.9 8.5 %branch_backward.1 = (f32[512,768]{1,0:T(8,128)}, bf16[512,768]{1,0:T(8,128)(2,1)}, bf16[768,768]{1,0:T(8,128)(2,1)}, f32[8,768]{1,0:T(8,128)}) custom-call(bf16[896,768]{1,0:T(8,128)(2,1)} %bitcast.311, bf16[896,768]{1,0:T(8,128)(2,1)} %bitcast.312, s32[512,2]{1,0:T(8,128)} %copy-done.4, bf16[512,768]{1,0:T(8,128)(2,1)} %cot_ref.1, ...), custom_call_target="tpu_custom_call" | custom-call | tf_op jit(solution)/shard_map/branch_backward/pallas_call | solution.py:172
  280.4 19.6 %attention_backward.1 = (bf16[512,2304]{1,0:T(8,128)(2,1)}, bf16[2,576,256]{2,1,0:T(8,128)(2,1)}, bf16[2,576,256]{2,1,0:T(8,128)(2,1)}, bf16[2,576,256]{2,1,0:T(...) custom-call(s32[4]{0:T(128)} %iota_xor_fusion.place_ref, ...), custom_call_target="tpu_custom_call" | custom-call | tf_op jit(solution)/shard_map/attention_backward/pallas_call | solution.py:172
  300.1 7.1 %input_backward.1 = (f32[512,768]{1,0:T(8,128)}, f32[8,768]{1,0:T(8,128)}) custom-call(bf16[512,2304]{1,0:T(8,128)(2,1)} %get-tuple-element.123.gproj_ref, bf16[2304,256]{1,0:T(8,128)(2,1)} %bitcast.320, bf16[2304,256]{1,0:T(8,128)(2,1)} %bitcast.318, bf16[2304,256]{1,0:T(8,128)(2,1)} %bitcast.316, bf16[512,768]{1,0:T(8,128)(2,1)} %x_ref.3, ...), custom_call_target="tpu_custom_call" | custom-call | tf_op jit(solution)/shard_map/input_backward/pallas_call | solution.py:172
  315.8 6.5 %collective-permute-done.34 = bf16[768,768]{1,0:T(8,128)(2,1)} collective-permute-done((bf16[768,768]{1,0:T(8,128)(2,1)}, bf16[768,768]{1,0:T(8,128)(2,1)}, u32[]{:S(2)}, u32[]{:S(2)}) %collective-permute-start.34) | collective-permute-done | bytes 1179680 | tf_op jit(solution)/shard_map/ppermute | solution.py:31
  327.2 4.2 %all-to-all-done.5 = bf16[8,2,112,768]{3,2,1,0:T(8,128)(2,1)S(1)} async-done(((bf16[8,2,112,768]{3,2,1,0:T(8,128)(2,1)}), bf16[8,2,112,768]{3,2,1,0:T(8,128)(2,1)S(1)}, u32[]{:S(2)}, u32[]{:S(2)}) %all-to-all-start.5) | async-done | bytes 2752544 | tf_op jit(solution)/shard_map/all_to_all | solution.py:742
  338.3 4.9 %collective-permute-done.35 = bf16[2,2,2,72,256]{4,3,2,1,0:T(8,128)(2,1)S(1)} collective-permute-done((bf16[2,2,2,72,256]{4,3,2,1,0:T(8,128)(2,1)S(1)}, bf16[2,2,2,72,256]{4,3,2,1,0:T(8,128)(2,1)S(1)}, u32[]{:S(2)}, u32[]{:S(2)}) %collective-permute-start.35) | collective-permute-done | bytes 294944 | tf_op jit(solution)/shard_map/ppermute | solution.py:31
  352.3 5.1 %mixed_output.1 = bf16[512,768]{1,0:T(8,128)(2,1)} custom-call(bf16[1792,768]{1,0:T(8,128)(2,1)} %bitcast.303, s32[512,2]{1,0:T(8,128)} %copy-done.9, f32[512,768]{1,0:T(8,128)} %get-tuple-element.113.middle_ref), custom_call_target="tpu_custom_call" | custom-call | flops 1250000000 | tf_op jit(solution)/shard_map/mixed_output/pallas_call | solution.py:172
  (299 shorter events, 131.6 us)
Async XLA Ops:
  44.3 65.0 %all-to-all-start = ((bf16[8,2,112,768]{3,2,1,0:T(8,128)(2,1)}), bf16[8,2,112,768]{3,2,1,0:T(8,128)(2,1)}, u32[]{:S(2)}, u32[]{:S(2)}) async-start(bf16[8,2,112,768]{3,2,1,0:T(8,128)(2,1)} %bitcast.326), calls=%async_computation | async-start | bytes 5505024 | tf_op jit(solution)/shard_map/all_to_all | solution.py:742
  51.5 29.4 %collective-permute-start.15 = (bf16[192,3072]{1,0:T(8,128)(2,1)}, bf16[192,3072]{1,0:T(8,128)(2,1)}, u32[]{:S(2)}, u32[]{:S(2)}) collective-permute-start(bf16[192,3072]{1,0:T(8,128)(2,1)} %bitcast.381), channel_id=1, source_target_pairs={{0,16},{8,24},{16,0},{24,8},{1,17},{9,25},{17,1},{25,9},{2,18},{10... | collective-permute-start | bytes 3538952 | tf_op jit(solution)/shard_map/ppermute | solution.py:31
  53.0 52.4 %collective-permute-start.16 = (bf16[768,768]{1,0:T(8,128)(2,1)}, bf16[768,768]{1,0:T(8,128)(2,1)}, u32[]{:S(2)}, u32[]{:S(2)}) collective-permute-start(bf16[768,768]{1,0:T(8,128)(2,1)} %bitcast.384), channel_id=1, source_target_pairs={{0,16},{8,24},{16,0},{24,8},{1,17},{9,25},{17,1},{25,9},{2,18},{10... | collective-permute-start | bytes 3538952 | tf_op jit(solution)/shard_map/ppermute | solution.py:31
  80.3 25.1 %collective-permute-start.17 = (bf16[192,3072]{1,0:T(8,128)(2,1)S(1)}, bf16[192,3072]{1,0:T(8,128)(2,1)S(1)}, u32[]{:S(2)}, u32[]{:S(2)}) collective-permute-start(bf16[192,3072]{1,0:T(8,128)(2,1)S(1)} %bitcast.383), channel_id=1, source_target_pairs={{0,8},{8,0},{16,24},{24,16},{1,9},{9,1},{17,25},{25,17},{2,10},{10... | collective-permute-start | bytes 3538952 | tf_op jit(solution)/shard_map/ppermute | solution.py:31
  80.3 25.1 %collective-permute-start.18 = (bf16[768,768]{1,0:T(8,128)(2,1)S(1)}, bf16[768,768]{1,0:T(8,128)(2,1)S(1)}, u32[]{:S(2)}, u32[]{:S(2)}) collective-permute-start(bf16[768,768]{1,0:T(8,128)(2,1)S(1)} %bitcast.386), channel_id=1, source_target_pairs={{0,8},{8,0},{16,24},{24,16},{1,9},{9,1},{17,25},{25,17},{2,10},{10... | collective-permute-start | bytes 3538952 | tf_op jit(solution)/shard_map/ppermute | solution.py:31
  80.8 24.6 %collective-permute-start.19 = (bf16[192,3072]{1,0:T(8,128)(2,1)S(1)}, bf16[192,3072]{1,0:T(8,128)(2,1)S(1)}, u32[]{:S(2)}, u32[]{:S(2)}) collective-permute-start(bf16[192,3072]{1,0:T(8,128)(2,1)S(1)} %bitcast.388), channel_id=1, source_target_pairs={{0,8},{8,0},{16,24},{24,16},{1,9},{9,1},{17,25},{25,17},{2,10},{10... | collective-permute-start | bytes 3538952 | tf_op jit(solution)/shard_map/ppermute | solution.py:31
  80.9 27.0 %collective-permute-start.20 = (bf16[768,768]{1,0:T(8,128)(2,1)S(1)}, bf16[768,768]{1,0:T(8,128)(2,1)}, u32[]{:S(2)}, u32[]{:S(2)}) collective-permute-start(bf16[768,768]{1,0:T(8,128)(2,1)S(1)} %bitcast.392), channel_id=1, source_target_pairs={{0,8},{8,0},{16,24},{24,16},{1,9},{9,1},{17,25},{25,17},{2,10},{10... | collective-permute-start | bytes 3538952 | tf_op jit(solution)/shard_map/ppermute | solution.py:31
  109.3 37.2 %all-to-all-start.1 = ((bf16[8,112,768]{2,1,0:T(8,128)(2,1)}), bf16[8,112,768]{2,1,0:T(8,128)(2,1)S(1)}, u32[]{:S(2)}, u32[]{:S(2)}) async-start(bf16[8,112,768]{2,1,0:T(8,128)(2,1)} %bitcast.338), calls=%async_computation.1 | async-start | bytes 2752512 | tf_op jit(solution)/shard_map/all_to_all | solution.py:742
  113.9 27.3 %collective-permute-start.23 = (bf16[192,3072]{1,0:T(8,128)(2,1)S(1)}, bf16[192,3072]{1,0:T(8,128)(2,1)S(1)}, u32[]{:S(2)}, u32[]{:S(2)}) collective-permute-start(bf16[192,3072]{1,0:T(8,128)(2,1)S(1)} %bitcast.389), channel_id=1, source_target_pairs={{0,16},{8,24},{16,0},{24,8},{1,17},{9,25},{17,1},{25,9},{2,18},{10... | collective-permute-start | bytes 3538952 | tf_op jit(solution)/shard_map/ppermute | solution.py:31
  115.4 25.7 %collective-permute-start.21 = (bf16[192,3072]{1,0:T(8,128)(2,1)}, bf16[192,3072]{1,0:T(8,128)(2,1)S(1)}, u32[]{:S(2)}, u32[]{:S(2)}) collective-permute-start(bf16[192,3072]{1,0:T(8,128)(2,1)} %collective-permute-done.15.rest_2_), channel_id=1, source_target_pairs={{0,8},{8,0},{16,24},{24,16},{1,9},{9,1},{17,25},{25,17},{2,10},{10... | collective-permute-start | bytes 3538952 | tf_op jit(solution)/shard_map/ppermute | solution.py:31
  115.4 25.7 %collective-permute-start.22 = (bf16[768,768]{1,0:T(8,128)(2,1)}, bf16[768,768]{1,0:T(8,128)(2,1)S(1)}, u32[]{:S(2)}, u32[]{:S(2)}) collective-permute-start(bf16[768,768]{1,0:T(8,128)(2,1)} %collective-permute-done.16.rest_6_), channel_id=1, source_target_pairs={{0,8},{8,0},{16,24},{24,16},{1,9},{9,1},{17,25},{25,17},{2,10},{10... | collective-permute-start | bytes 3538952 | tf_op jit(solution)/shard_map/ppermute | solution.py:31
  146.5 36.8 %all-to-all-start.2 = ((bf16[8,112,768]{2,1,0:T(8,128)(2,1)}), bf16[8,112,768]{2,1,0:T(8,128)(2,1)S(1)}, u32[]{:S(2)}, u32[]{:S(2)}) async-start(bf16[8,112,768]{2,1,0:T(8,128)(2,1)} %bitcast.63), calls=%async_computation.2 | async-start | bytes 2752512 | tf_op jit(solution)/shard_map/all_to_all | solution.py:742
  152.6 35.5 %collective-permute-start.25 = (bf16[768,768]{1,0:T(8,128)(2,1)}, bf16[768,768]{1,0:T(8,128)(2,1)}, u32[]{:S(2)}, u32[]{:S(2)}) collective-permute-start(bf16[768,768]{1,0:T(8,128)(2,1)} %bitcast.390), channel_id=1, source_target_pairs={{0,16},{8,24},{16,0},{24,8},{1,17},{9,25},{17,1},{25,9},{2,18},{10... | collective-permute-start | bytes 3538952 | tf_op jit(solution)/shard_map/ppermute | solution.py:31
  183.3 38.7 %all-to-all-start.3 = ((bf16[8,112,768]{2,1,0:T(8,128)(2,1)}), bf16[8,112,768]{2,1,0:T(8,128)(2,1)S(1)}, u32[]{:S(2)}, u32[]{:S(2)}) async-start(bf16[8,112,768]{2,1,0:T(8,128)(2,1)} %bitcast.340), calls=%async_computation.3 | async-start | bytes 2752512 | tf_op jit(solution)/shard_map/all_to_all | solution.py:742
  222.0 39.6 %all-to-all-start.4 = ((bf16[8,112,768]{2,1,0:T(8,128)(2,1)}), bf16[8,112,768]{2,1,0:T(8,128)(2,1)S(1)}, u32[]{:S(2)}, u32[]{:S(2)}) async-start(bf16[8,112,768]{2,1,0:T(8,128)(2,1)} %bitcast.339), calls=%async_computation.4 | async-start | bytes 2752512 | tf_op jit(solution)/shard_map/all_to_all | solution.py:742
  262.8 68.7 %all-to-all-start.5 = ((bf16[8,2,112,768]{3,2,1,0:T(8,128)(2,1)}), bf16[8,2,112,768]{3,2,1,0:T(8,128)(2,1)S(1)}, u32[]{:S(2)}, u32[]{:S(2)}) async-start(bf16[8,2,112,768]{3,2,1,0:T(8,128)(2,1)} %get-tuple-element.111), calls=%async_computation.5 | async-start | bytes 5505024 | tf_op jit(solution)/shard_map/all_to_all | solution.py:742
  269.0 43.0 %collective-permute-start.33 = (bf16[192,3072]{1,0:T(8,128)(2,1)}, bf16[192,3072]{1,0:T(8,128)(2,1)}, u32[]{:S(2)}, u32[]{:S(2)}) collective-permute-start(bf16[192,3072]{1,0:T(8,128)(2,1)} %bitcast.394), channel_id=1, source_target_pairs={{0,16},{8,24},{16,0},{24,8},{1,17},{9,25},{17,1},{25,9},{2,18},{10... | collective-permute-start | bytes 3538952 | tf_op jit(solution)/shard_map/ppermute | solution.py:31
  270.0 52.4 %collective-permute-start.34 = (bf16[768,768]{1,0:T(8,128)(2,1)}, bf16[768,768]{1,0:T(8,128)(2,1)}, u32[]{:S(2)}, u32[]{:S(2)}) collective-permute-start(bf16[768,768]{1,0:T(8,128)(2,1)} %bitcast.393), channel_id=1, source_target_pairs={{0,16},{8,24},{16,0},{24,8},{1,17},{9,25},{17,1},{25,9},{2,18},{10... | collective-permute-start | bytes 3538952 | tf_op jit(solution)/shard_map/ppermute | solution.py:31
  310.7 16.6 %collective-permute-start.32 = (bf16[2,2,2,2,32,768]{5,4,1,3,2,0:T(8,128)(2,1)S(1)}, bf16[2,2,2,2,32,768]{5,4,1,3,2,0:T(8,128)(2,1)}, u32[]{:S(2)}, u32[]{:S(2)}) collective-permute-start(bf16[2,2,2,2,32,768]{5,4,1,3,2,0:T(8,128)(2,1)S(1)} %bitcast.342), channel_id=1, source_target_pairs={{0,8},{8,0},{16,24},{24,16},{1,9},{9,1},{17,25},{25,17},{2,10},{10... | collective-permute-start | bytes 2359304 | tf_op jit(solution)/shard_map/ppermute | solution.py:31
  311.5 13.9 %collective-permute-start.29 = (bf16[2,576,256]{2,1,0:T(8,128)(2,1)S(1)}, bf16[2,576,256]{2,1,0:T(8,128)(2,1)S(1)}, u32[]{:S(2)}, u32[]{:S(2)}) collective-permute-start(bf16[2,576,256]{2,1,0:T(8,128)(2,1)S(1)} %copy-done.40), channel_id=1, source_target_pairs={{0,8},{8,0},{16,24},{24,16},{1,9},{9,1},{17,25},{25,17},{2,10},{10... | collective-permute-start | bytes 1769480 | tf_op jit(solution)/shard_map/ppermute | solution.py:31
  335.3 14.3 %collective-permute-start.38 = (bf16[2,2,2,32,768]{4,3,2,1,0:T(8,128)(2,1)S(1)}, bf16[2,2,2,32,768]{4,3,2,1,0:T(8,128)(2,1)S(1)}, u32[]{:S(2)}, u32[]{:S(2)}) collective-permute-start(bf16[2,2,2,32,768]{4,3,2,1,0:T(8,128)(2,1)S(1)} %copy.128), channel_id=1, source_target_pairs={{0,16},{8,24},{16,0},{24,8},{1,17},{9,25},{17,1},{25,9},{2,18},{10... | collective-permute-start | bytes 1179656 | tf_op jit(solution)/shard_map/ppermute | solution.py:31
  343.3 14.2 %collective-permute-start.39 = (bf16[2,2,72,256]{3,2,1,0:T(8,128)(2,1)S(1)}, bf16[2,2,72,256]{3,2,1,0:T(8,128)(2,1)S(1)}, u32[]{:S(2)}, u32[]{:S(2)}) collective-permute-start(bf16[2,2,72,256]{3,2,1,0:T(8,128)(2,1)S(1)} %fusion.11), channel_id=1, source_target_pairs={{0,1},{1,0},{2,3},{3,2},{4,5},{5,4},{6,7},{7,6},{8,9},{9,8},{10,11... | collective-permute-start | bytes 442376 | tf_op jit(solution)/shard_map/ppermute | solution.py:31
  346.6 14.0 %collective-permute-start.45 = (bf16[2,2,72,256]{3,2,1,0:T(8,128)(2,1)S(1)}, bf16[2,2,72,256]{3,2,1,0:T(8,128)(2,1)S(1)}, u32[]{:S(2)}, u32[]{:S(2)}) collective-permute-start(bf16[2,2,72,256]{3,2,1,0:T(8,128)(2,1)S(1)} %fusion.9), channel_id=1, source_target_pairs={{0,4},{1,5},{2,6},{3,7},{4,0},{5,1},{6,2},{7,3},{8,12},{9,13},{10,... | collective-permute-start | bytes 442376 | tf_op jit(solution)/shard_map/ppermute | solution.py:31
  350.7 16.8 %collective-permute-start.48 = (bf16[2,2,32,768]{3,2,1,0:T(8,128)(2,1)S(1)}, bf16[2,2,32,768]{3,2,1,0:T(8,128)(2,1)S(1)}, u32[]{:S(2)}, u32[]{:S(2)}) collective-permute-start(bf16[2,2,32,768]{3,2,1,0:T(8,128)(2,1)S(1)} %copy.141), channel_id=1, source_target_pairs={{0,1},{1,0},{2,3},{3,2},{4,5},{5,4},{6,7},{7,6},{8,9},{9,8},{10,11... | collective-permute-start | bytes 589832 | tf_op jit(solution)/shard_map/ppermute | solution.py:31
  (74 other events, 473.3 us)
